TPU v7x, 32 devices: a whole 2x2x4 slice. The times are simulated.
32 devices in a mesh: section: 2 (over core), dp: 16 (over z, y, x).
Axes of the slice: x: 2, y: 2, z: 4, core: 2. Of those that a mesh axis runs over, the one named last changes fastest.
Arguments:
- tokens: bfloat16 [64, 512, 512], P('dp', 'section'), may hold values from -6 to 6
- memory: bfloat16 [64, 64, 512], P('dp', 'section'), may hold values from -6 to 6
- lengths: int32 [32], P('dp'), may hold values from 256 to 1024, as said below
- w_qkv: bfloat16 [2, 512, 1536], P('section', 'dp'), may hold values from -0.25 to 0.25
- w_out: bfloat16 [2, 512, 512], P('section', 'dp'), may hold values from -1 to 1
- w_up: bfloat16 [2, 512, 2048], P('section', 'dp'), may hold values from -0.25 to 0.25
- w_down: bfloat16 [2, 2048, 512], P('section', 'dp'), may hold values from -0.125 to 0.125
- gain_attn: bfloat16 [2, 512], P('section', 'dp'), may hold values from 0.5 to 1.5
- gain_ffn: bfloat16 [2, 512], P('section', 'dp'), may hold values from 0.5 to 1.5
- forget_bias: bfloat16 [2, 512], P('section', 'dp'), may hold values from -4 to 4
- grad_tokens: bfloat16 [64, 512, 512], P('dp', 'section'), may hold values from -6 to 6
- grad_memory: bfloat16 [64, 64, 512], P('dp', 'section'), may hold values from -6 to 6
Outputs:
- out_tokens: bfloat16 [64, 512, 512], P('dp', 'section')
- out_memory: bfloat16 [64, 64, 512], P('dp', 'section')
- grad_in_tokens: bfloat16 [64, 512, 512], P('dp', 'section')
- grad_in_memory: bfloat16 [64, 64, 512], P('dp', 'section')
- grad_w_qkv: float32 [2, 512, 1536], P('section', 'dp')
- grad_w_out: float32 [2, 512, 512], P('section', 'dp')
- grad_w_up: float32 [2, 512, 2048], P('section', 'dp')
- grad_w_down: float32 [2, 2048, 512], P('section', 'dp')
- grad_gain_attn: float32 [2, 512], P('section', 'dp')
- grad_gain_ffn: float32 [2, 512], P('section', 'dp')
- grad_forget_bias: float32 [2, 512], P('section', 'dp')
- rms: float32 [2, 3], replicated
Inputs may be any that keep to these rules, and one draw needn't show every extreme that they name: `lengths`: in every draw some document has exactly 1024 tokens.
All inputs are finite; a program needn't handle non-finite values.
Results may differ from a plain program's by a relative error of at most 0.018.
Values may be sent and summed in bfloat16 or wider, within the bound.
A program may use at most 192 MiB of HBM per device.

v0:
```python
from functools import partial

import jax
import jax.numpy as jnp
from jax import lax
from jax.sharding import PartitionSpec as P

norm_eps = 1e-06
score_scale = 0.125
masked_score = -1000000000.0


def partner(block, axis, bit):
    count = lax.axis_size(axis)
    route = []
    for low in range(count):
        high = low | 1 << bit
        if high != low and high < count:
            route += [(low, high), (high, low)]
    return lax.ppermute(block, axis, route)


def from_behind(shard, axis, by):
    peers = lax.axis_size(axis)
    pairs = [(i, i + by) for i in range(peers) if 0 <= i + by < peers]
    return lax.ppermute(shard, axis, pairs)


def rms_scale(row_vals, gain_vec):
    return (
        row_vals
        * lax.rsqrt(jnp.mean(row_vals * row_vals, axis=-1, keepdims=True) + norm_eps)
        * gain_vec
    )


def inner_rows(left_mat, right_mat):
    return lax.dot_general(
        left_mat, right_mat, (((0,), (0,)), ((), ())), preferred_element_type=jnp.float32
    )


def times_trans(left_mat, right_mat):
    return lax.dot_general(
        left_mat, right_mat, (((1,), (1,)), ((), ())), preferred_element_type=jnp.float32
    )


def token_squares(values, valid_rows, slot_count):
    token_part = values[slot_count:]
    return jnp.sum(
        jnp.sum(token_part * token_part, axis=1) * valid_rows[slot_count:].astype(jnp.float32)
    )


def split_project(project, head_count):
    row_count = project.shape[0]
    model_width = project.shape[1] // 3
    head_size = model_width // head_count
    queries = project[:, :model_width].reshape(row_count, head_count, head_size)
    keys_h = project[:, model_width : 2 * model_width].reshape(row_count, head_count, head_size)
    values_h = project[:, 2 * model_width :].reshape(row_count, head_count, head_size)
    return (queries, keys_h, values_h)


def scores_of(queries, keys_h, forget_bias, valid_rows, slot_count, head_count):
    row_count = queries.shape[0]
    bias_rows = jnp.concatenate(
        [
            forget_bias.astype(jnp.float32).reshape(slot_count, head_count).T,
            jnp.zeros((head_count, row_count - slot_count), jnp.float32),
        ],
        axis=1,
    )
    raw_scores = (
        jnp.einsum("qhd,khd->hqk", queries, keys_h, preferred_element_type=jnp.float32)
        * score_scale
        + bias_rows[:, None, :]
    )
    return jnp.where(valid_rows[None, None, :], raw_scores, masked_score)


def layer_forward(layer_in, valid_rows, weights, slot_count):
    w_qkv, w_out, w_up, w_down, gain_attn, gain_ffn, forget_bias = weights
    row_count, model_width = layer_in.shape
    head_count = forget_bias.shape[0] // slot_count
    resid_in = layer_in.astype(jnp.float32)
    normed = rms_scale(resid_in, gain_attn.astype(jnp.float32)).astype(jnp.bfloat16)
    project = jnp.dot(normed, w_qkv, preferred_element_type=jnp.float32).astype(jnp.bfloat16)
    queries, keys_h, values_h = split_project(project, head_count)
    scores = scores_of(queries, keys_h, forget_bias, valid_rows, slot_count, head_count)
    row_max = jnp.max(scores, axis=-1, keepdims=True)
    log_total = row_max + jnp.log(jnp.sum(jnp.exp(scores - row_max), axis=-1, keepdims=True))
    attn_low = jnp.exp(scores - log_total).astype(jnp.bfloat16)
    attended = (
        jnp.einsum("hqk,khd->qhd", attn_low, values_h, preferred_element_type=jnp.float32)
        .reshape(row_count, model_width)
        .astype(jnp.bfloat16)
    )
    branch = jnp.dot(attended, w_out, preferred_element_type=jnp.float32)
    middle = resid_in + branch
    normed_two = rms_scale(middle, gain_ffn.astype(jnp.float32)).astype(jnp.bfloat16)
    before = jnp.dot(normed_two, w_up, preferred_element_type=jnp.float32)
    active = jax.nn.gelu(before, approximate=True).astype(jnp.bfloat16)
    ffn_out = jnp.dot(active, w_down, preferred_element_type=jnp.float32)
    layer_out = middle + ffn_out
    squares = jnp.stack(
        [
            token_squares(resid_in, valid_rows, slot_count),
            token_squares(branch, valid_rows, slot_count),
            token_squares(ffn_out, valid_rows, slot_count),
        ]
    )
    saved_state = (
        resid_in,
        normed,
        project,
        log_total,
        attended,
        middle,
        normed_two,
        before,
        active,
    )
    return (layer_out, saved_state, squares)


def layer_backward(saved_state, valid_rows, weights, slot_count, grad_out):
    w_qkv, w_out, w_up, w_down, gain_attn, gain_ffn, forget_bias = weights
    resid_in, normed, project, log_total, attended, middle, normed_two, before, active = saved_state
    row_count, model_width = resid_in.shape
    head_count = forget_bias.shape[0] // slot_count
    head_size = model_width // head_count
    grad_ffn = grad_out.astype(jnp.bfloat16)
    grad_down = inner_rows(active, grad_ffn)
    d_active = times_trans(grad_ffn, w_down)
    _, gelu_back = jax.vjp(partial(jax.nn.gelu, approximate=True), before)
    d_before = gelu_back(d_active)[0].astype(jnp.bfloat16)
    grad_up = inner_rows(normed_two, d_before)
    d_normed_two = times_trans(d_before, w_up)
    _, norm_back_two = jax.vjp(rms_scale, middle, gain_ffn.astype(jnp.float32))
    d_middle_norm, grad_gain_ffn = norm_back_two(d_normed_two)
    d_middle = grad_out + d_middle_norm
    d_branch = d_middle.astype(jnp.bfloat16)
    grad_out_w = inner_rows(attended, d_branch)
    d_attended = (
        times_trans(d_branch, w_out).astype(jnp.bfloat16).reshape(row_count, head_count, head_size)
    )
    queries, keys_h, values_h = split_project(project, head_count)
    scores = scores_of(queries, keys_h, forget_bias, valid_rows, slot_count, head_count)
    attn_probs = jnp.exp(scores - log_total)
    attn_low = attn_probs.astype(jnp.bfloat16)
    d_probs = jnp.einsum("qhd,khd->hqk", d_attended, values_h, preferred_element_type=jnp.float32)
    d_values = jnp.einsum("hqk,qhd->khd", attn_low, d_attended, preferred_element_type=jnp.float32)
    d_scores = (
        attn_probs * (d_probs - jnp.sum(d_probs * attn_probs, axis=-1, keepdims=True))
    ).astype(jnp.bfloat16)
    grad_bias = jnp.sum(d_scores[:, :, :slot_count].astype(jnp.float32), axis=1).T.reshape(
        slot_count * head_count
    )
    d_queries = (
        jnp.einsum("hqk,khd->qhd", d_scores, keys_h, preferred_element_type=jnp.float32)
        * score_scale
    )
    d_keys = (
        jnp.einsum("hqk,qhd->khd", d_scores, queries, preferred_element_type=jnp.float32)
        * score_scale
    )
    d_project = jnp.concatenate(
        [
            d_queries.reshape(row_count, model_width),
            d_keys.reshape(row_count, model_width),
            d_values.reshape(row_count, model_width),
        ],
        axis=1,
    ).astype(jnp.bfloat16)
    grad_qkv = inner_rows(normed, d_project)
    d_normed = times_trans(d_project, w_qkv)
    _, norm_back_one = jax.vjp(rms_scale, resid_in, gain_attn.astype(jnp.float32))
    d_resid_norm, grad_gain_attn = norm_back_one(d_normed)
    grad_in = d_middle + d_resid_norm
    return (
        grad_in,
        (grad_qkv, grad_out_w, grad_up, grad_down, grad_gain_attn, grad_gain_ffn, grad_bias),
    )


def body(
    tokens,
    memory,
    lengths,
    w_qkv,
    w_out,
    w_up,
    w_down,
    gain_attn,
    gain_ffn,
    forget_bias,
    grad_tokens,
    grad_memory,
):
    section_idx = lax.axis_index("section")
    is_first = section_idx == 0
    micro_count = tokens.shape[0]
    half_tok = tokens.shape[1]
    half_mem = memory.shape[1]
    seg_len = 2 * half_tok
    slot_count = 2 * half_mem
    model_width = tokens.shape[2]
    per_doc = micro_count // lengths.shape[0]
    sent_tok = jnp.where(is_first, grad_tokens, tokens)
    sent_mem = jnp.where(is_first, grad_memory, memory)
    got_tok, got_mem = partner((sent_tok, sent_mem), "section", 0)
    full_tok = jnp.concatenate(
        [jnp.where(is_first, tokens, got_tok), jnp.where(is_first, got_tok, grad_tokens)], axis=1
    )
    full_mem = jnp.concatenate(
        [jnp.where(is_first, memory, got_mem), jnp.where(is_first, got_mem, grad_memory)], axis=1
    )
    feed_rows = jnp.concatenate([full_mem, full_tok], axis=1)
    gathered = (
        lax.all_gather(w_qkv, "dp", axis=1, tiled=True),
        lax.all_gather(w_out, "dp", axis=1, tiled=True),
        lax.all_gather(w_up, "dp", axis=1, tiled=True),
        lax.all_gather(w_down, "dp", axis=1, tiled=True),
        lax.all_gather(gain_attn, "dp", axis=1, tiled=True),
        lax.all_gather(gain_ffn, "dp", axis=1, tiled=True),
        lax.all_gather(forget_bias, "dp", axis=1, tiled=True),
    )
    weights = tuple((piece[0] for piece in gathered))
    doc_len = jnp.repeat(lengths, per_doc)
    seg_part = jnp.arange(micro_count, dtype=jnp.int32) % per_doc
    positions = seg_part[:, None] * seg_len + jnp.arange(seg_len, dtype=jnp.int32)[None, :]
    token_valid = positions < doc_len[:, None]
    valid_all = jnp.concatenate(
        [jnp.ones((micro_count, slot_count), dtype=bool), token_valid], axis=1
    )
    step_count = micro_count + 1

    def forward_step(incoming, step_idx):
        own_rows = lax.dynamic_index_in_dim(
            feed_rows, jnp.minimum(step_idx, micro_count - 1), 0, keepdims=False
        )
        layer_in = jnp.where(is_first, own_rows, incoming)
        micro_idx = step_idx - section_idx
        is_live = (micro_idx >= 0) & (micro_idx < micro_count)
        safe_idx = jnp.clip(micro_idx, 0, micro_count - 1)
        valid_rows = lax.dynamic_index_in_dim(valid_all, safe_idx, 0, keepdims=False)
        layer_out, saved_state, squares = layer_forward(layer_in, valid_rows, weights, slot_count)
        out_low = layer_out.astype(jnp.bfloat16)
        passed = from_behind(out_low, "section", 1)
        squares = jnp.where(is_live, squares, 0.0)
        stored = (layer_in, out_low, squares)
        return (passed, stored)

    _, stored = lax.scan(
        forward_step, jnp.zeros_like(feed_rows[0]), jnp.arange(step_count, dtype=jnp.int32)
    )

    def own_micro(stacked, offset):
        return lax.dynamic_slice_in_dim(stacked, offset, micro_count, 0)

    kept_in = own_micro(stored[0], section_idx)
    kept_out = own_micro(stored[1], section_idx)
    squares_total = jnp.sum(stored[2], axis=0)
    zero_grads = tuple((jnp.zeros(piece.shape, jnp.float32) for piece in weights))

    def backward_step(carry, step_idx):
        incoming, grad_acc = carry
        micro_idx = step_idx - 1 + section_idx
        is_live = (micro_idx >= 0) & (micro_idx < micro_count)
        safe_idx = jnp.clip(micro_idx, 0, micro_count - 1)
        valid_rows = lax.dynamic_index_in_dim(valid_all, safe_idx, 0, keepdims=False)
        own_cot = lax.dynamic_index_in_dim(feed_rows, safe_idx, 0, keepdims=False).astype(
            jnp.float32
        )
        cotangent = jnp.where(is_first, incoming.astype(jnp.float32), own_cot)
        layer_in = lax.dynamic_index_in_dim(kept_in, safe_idx, 0, keepdims=False)
        _, saved_state, _ = layer_forward(layer_in, valid_rows, weights, slot_count)
        grad_in, grads = layer_backward(saved_state, valid_rows, weights, slot_count, cotangent)
        grads = tuple((jnp.where(is_live, piece, 0.0) for piece in grads))
        grad_low = grad_in.astype(jnp.bfloat16)
        passed = from_behind(grad_low, "section", -1)
        grad_acc = tuple((total + share for total, share in zip(grad_acc, grads)))
        return ((passed, grad_acc), grad_low)

    (_, grad_acc), grad_rows = lax.scan(
        backward_step,
        (jnp.zeros_like(feed_rows[0]), zero_grads),
        jnp.arange(step_count, dtype=jnp.int32),
    )
    grad_parts = (
        lax.psum_scatter(grad_acc[0][None], "dp", scatter_dimension=1, tiled=True),
        lax.psum_scatter(grad_acc[1][None], "dp", scatter_dimension=1, tiled=True),
        lax.psum_scatter(grad_acc[2][None], "dp", scatter_dimension=1, tiled=True),
        lax.psum_scatter(grad_acc[3][None], "dp", scatter_dimension=1, tiled=True),
        lax.psum_scatter(grad_acc[4][None], "dp", scatter_dimension=1, tiled=True),
        lax.psum_scatter(grad_acc[5][None], "dp", scatter_dimension=1, tiled=True),
        lax.psum_scatter(grad_acc[6][None], "dp", scatter_dimension=1, tiled=True),
    )
    token_count = jnp.sum(token_valid.astype(jnp.float32))
    row_stats = jnp.concatenate([squares_total, token_count[None]])
    partial_stats = jnp.where((jnp.arange(2) == section_idx)[:, None], row_stats[None, :], 0.0)
    totals = lax.psum(partial_stats, ("section", "dp"))
    rms = jnp.sqrt(totals[:, :3] / (totals[:, 3:] * model_width))
    result_rows = jnp.where(is_first, own_micro(grad_rows, 1 - section_idx), kept_out)
    result_mem = result_rows[:, :slot_count]
    result_tok = result_rows[:, slot_count:]
    send_tok = lax.dynamic_slice_in_dim(result_tok, (1 - section_idx) * half_tok, half_tok, 1)
    send_mem = lax.dynamic_slice_in_dim(result_mem, (1 - section_idx) * half_mem, half_mem, 1)
    recv_tok, recv_mem = partner((send_tok, send_mem), "section", 0)
    keep_tok = lax.dynamic_slice_in_dim(result_tok, section_idx * half_tok, half_tok, 1)
    keep_mem = lax.dynamic_slice_in_dim(result_mem, section_idx * half_mem, half_mem, 1)
    out_tokens = jnp.where(is_first, recv_tok, keep_tok)
    out_memory = jnp.where(is_first, recv_mem, keep_mem)
    grad_in_tokens = jnp.where(is_first, keep_tok, recv_tok)
    grad_in_memory = jnp.where(is_first, keep_mem, recv_mem)
    return (
        out_tokens,
        out_memory,
        grad_in_tokens,
        grad_in_memory,
        grad_parts[0],
        grad_parts[1],
        grad_parts[2],
        grad_parts[3],
        grad_parts[4],
        grad_parts[5],
        grad_parts[6],
        rms,
    )


def solution(mesh):
    placed = (
        P("dp", "section", None),
        P("dp", "section", None),
        P("dp"),
        P("section", "dp", None),
        P("section", "dp", None),
        P("section", "dp", None),
        P("section", "dp", None),
        P("section", "dp"),
        P("section", "dp"),
        P("section", "dp"),
        P("dp", "section", None),
        P("dp", "section", None),
    )
    return jax.shard_map(
        body,
        mesh=mesh,
        in_specs=placed,
        out_specs=(
            P("dp", "section", None),
            P("dp", "section", None),
            P("dp", "section", None),
            P("dp", "section", None),
            P("section", "dp", None),
            P("section", "dp", None),
            P("section", "dp", None),
            P("section", "dp", None),
            P("section", "dp"),
            P("section", "dp"),
            P("section", "dp"),
            P(),
        ),
        check_vma=False,
    )
```

profile of v0, /device:TPU:0, one launch (start us, length us, event | category | flops | bytes accessed | tf_op | source)
XLA Modules:
  0.0 1539.8 jit_solution(9696597637139531590)
XLA Ops:
  15.2 44.3 %all-reduce.6 = (bf16[512]{0:T(512)(128)(2,1)S(1)}, bf16[512]{0:T(512)(128)(2,1)}, bf16[512]{0:T(512)(128)(2,1)}) all-reduce(bf16[512]{0:T(512)(128)(2,1)S(1)} %dynamic-update-slice, bf16[512]{0:T(512)(128)(2,1)S(1)} %dynamic-update-slice.1, bf16[512]{0:T(512)(128)(2,1)S(1)} %dynamic-update-slice.2), channel_id=1, replica_groups=mesh['section'=2,'dp'=16] {'dp'}, use_global_device_ids=true, to_apply=%add.3 | all-reduce | flops 1536 | bytes 6144 | tf_op jit(solution)/shard_map/squeeze | solution.py:230
  59.5 42.4 %all_gather.25 = bf16[1,512,512]{2,1,0:T(8,128)(2,1)} all-gather(bf16[1,32,512]{2,1,0:T(8,128)(2,1)} %param.20), channel_id=1, replica_groups=mesh['section'=2,'dp'=16] {'dp'}, dimensions={1}, use_global_device_ids=true | all-gather | bytes 557056 | tf_op jit(solution)/shard_map/all_gather | solution.py:223
  105.9 30.3 %all-gather.8.cloned.1.call-done = bf16[1,512,2048]{2,1,0:T(8,128)(2,1)} async-done(((bf16[1,32,2048]{2,1,0:T(8,128)(2,1)}), bf16[1,512,2048]{2,1,0:T(8,128)(2,1)}) %all-gather.8.cloned.1.call-update) | async-done | bytes 2097168 | tf_op jit(solution)/shard_map/all_gather | solution.py:224
  136.3 62.2 %all-gather.4.cloned.1.call-done = bf16[1,2048,512]{2,1,0:T(8,128)(2,1)} async-done(((bf16[1,128,512]{2,1,0:T(8,128)(2,1)}), bf16[1,2048,512]{2,1,0:T(8,128)(2,1)}) %all-gather.4.cloned.1.call-update) | async-done | bytes 2097168 | tf_op jit(solution)/shard_map/all_gather | solution.py:225
  203.5 193.7 %while.45 = (s32[]{:T(128)}, bf16[576,512]{1,0:T(8,128)(2,1)}, bf16[5,576,512]{2,1,0:T(8,128)(2,1)}, bf16[5,576,512]{2,1,0:T(8,128)(2,1)}, f32[5,3]{0,1:T(4,128)...) while((s32[]{:T(128)}, bf16[576,512]{1,0:T(8,128)(2,1)}, ...), condition=%wide.region_11.12_spmd, body=%wide.region_0.11_spmd.sunk | while | flops 4360375808 | bytes 70527096 | solution.py:256
  403.7 493.7 %while.46 = (s32[]{:T(128)}, bf16[576,512]{1,0:T(8,128)(2,1)}, f32[512,1536]{1,0:T(8,128)}, f32[512,512]{1,0:T(8,128)}, f32[512,2048]{1,0:T(8,128)}, /*index=5*/...) while((s32[]{:T(128)}, bf16[576,512]{1,0:T(8,128)(2,1)}, ...), condition=%wide.region_23.24_spmd.clone, body=%wide.region_12.23_spmd.clone.sunk | while | flops 11823028224 | bytes 408286336 | solution.py:287
  462.9 8.4 multiply_reduce_fusion.16
  490.8 7.4 select_add_fusion.10
  553.7 8.4 multiply_reduce_fusion.16
  581.6 8.6 select_add_fusion.10
  649.6 8.4 multiply_reduce_fusion.16
  677.5 8.6 select_add_fusion.10
  745.5 8.4 multiply_reduce_fusion.16
  773.4 8.6 select_add_fusion.10
  841.5 8.4 multiply_reduce_fusion.16
  869.3 8.6 select_add_fusion.10
  915.9 39.2 %psum.7 = f32[2,4]{1,0:T(2,128)S(1)} all-reduce(f32[2,4]{1,0:T(2,128)S(1)} %broadcast_select_fusion.10), channel_id=1, replica_groups=mesh['section'=2,'dp'=16] {'section','dp'}, use_global_device_ids=true, to_apply=%region_33.34 | all-reduce | flops 8 | bytes 64 | tf_op jit(solution)/shard_map/psum | solution.py:304
  957.1 21.5 %reduce-scatter.26.cloned.1.call-done = f32[32,1]{1,0:T(8,128)} async-done(((f32[512,1]{1,0:T(8,128)}), f32[32,1]{1,0:T(8,128)}) %reduce-scatter.26.cloned.1.call-update) | async-done | bytes 144
  979.9 73.9 %reduce-scatter.22.cloned.1.call-done = f32[32,1]{1,0:T(8,128)} async-done(((f32[512,1]{1,0:T(8,128)}), f32[32,1]{1,0:T(8,128)}) %reduce-scatter.22.cloned.1.call-update) | async-done | bytes 144
  1055.1 73.3 %reduce-scatter.24.cloned.1.call-done = f32[32,1]{1,0:T(8,128)} async-done(((f32[512,1]{1,0:T(8,128)}), f32[32,1]{1,0:T(8,128)}) %reduce-scatter.24.cloned.1.call-update) | async-done | bytes 144
  1133.1 72.2 %reduce-scatter.16.cloned.1.call-done = f32[1,32,512]{2,1,0:T(8,128)} async-done(((f32[1,512,512]{2,1,0:T(8,128)}), f32[1,32,512]{2,1,0:T(8,128)}) %reduce-scatter.16.cloned.1.call-update) | async-done | bytes 65552 | tf_op jit(solution)/shard_map/reduce_scatter | solution.py:294
  1205.3 132.7 %reduce-scatter.14.cloned.1.call-done = f32[1,32,1536]{2,1,0:T(8,128)} async-done(((f32[1,512,1536]{2,1,0:T(8,128)}), f32[1,32,1536]{2,1,0:T(8,128)}) %reduce-scatter.14.cloned.1.call-update) | async-done | bytes 196624 | tf_op jit(solution)/shard_map/reduce_scatter | solution.py:293
  1338.0 97.3 %reduce-scatter.18.cloned.1.call-done = f32[1,32,2048]{2,1,0:T(8,128)} async-done(((f32[1,512,2048]{2,1,0:T(8,128)}), f32[1,32,2048]{2,1,0:T(8,128)}) %reduce-scatter.18.cloned.1.call-update) | async-done | bytes 262160 | tf_op jit(solution)/shard_map/reduce_scatter | solution.py:295
  1435.2 97.5 %reduce-scatter.20.cloned.1.call-done = f32[1,128,512]{2,1,0:T(8,128)} async-done(((f32[1,2048,512]{2,1,0:T(8,128)}), f32[1,128,512]{2,1,0:T(8,128)}) %reduce-scatter.20.cloned.1.call-update) | async-done | bytes 262160 | tf_op jit(solution)/shard_map/reduce_scatter | solution.py:296
  (888 shorter events, 621.4 us)
Async XLA Ops:
  7.3 98.7 %all-gather.6.cloned.1.call-start = ((), (), s32[]{:S(2)}) async-start(), calls=%async_computation.8 | async-start | bytes 1671168 | tf_op jit(solution)/shard_map/all_gather | solution.py:222
  8.0 128.3 %all-gather.8.cloned.1.call-start = ((), (), s32[]{:S(2)}) async-start(), calls=%async_computation.9 | async-start | bytes 2228224 | tf_op jit(solution)/shard_map/all_gather | solution.py:224
  8.7 189.7 %all-gather.4.cloned.1.call-start = ((), (), s32[]{:S(2)}) async-start(), calls=%async_computation.7 | async-start | bytes 2228224 | tf_op jit(solution)/shard_map/all_gather | solution.py:225
  9.5 969.1 %reduce-scatter.26.cloned.1.call-start = ((), (), s32[]{:S(2)}) async-start(), calls=%async_computation.16 | async-start | bytes 278528
  10.9 92.0 %collective-permute-start.3 = (bf16[4,256,512]{2,1,0:T(8,128)(2,1)S(1)}, bf16[4,256,512]{2,1,0:T(8,128)(2,1)}, u32[]{:S(2)}, u32[]{:S(2)}) collective-permute-start(bf16[4,256,512]{2,1,0:T(8,128)(2,1)S(1)} %broadcast_select_fusion.4), channel_id=1, source_target_pairs={{0,16},{16,0},{1,17},{17,1},{2,18},{18,2},{3,19},{19,3},{4,20},{20... | collective-permute-start | bytes 3145736 | tf_op jit(solution)/shard_map/ppermute | solution.py:20
  11.4 90.5 %collective-permute-start.2 = (bf16[4,32,512]{2,1,0:T(8,128)(2,1)S(1)}, bf16[4,32,512]{2,1,0:T(8,128)(2,1)}, u32[]{:S(2)}, u32[]{:S(2)}) collective-permute-start(bf16[4,32,512]{2,1,0:T(8,128)(2,1)S(1)} %broadcast_select_fusion.9), channel_id=1, source_target_pairs={{0,16},{16,0},{1,17},{17,1},{2,18},{18,2},{3,19},{19,3},{4,20},{20... | collective-permute-start | bytes 393224 | tf_op jit(solution)/shard_map/ppermute | solution.py:20
  235.1 6.7 collective-permute-start
  273.9 6.6 collective-permute-start
  312.6 6.6 collective-permute-start
  351.3 6.6 collective-permute-start
  390.0 6.6 collective-permute-start
  488.2 23.4 %collective-permute-start.1 = (bf16[576,512]{1,0:T(8,128)(2,1)}, bf16[576,512]{1,0:T(8,128)(2,1)}, u32[]{:S(2)}, u32[]{:S(2)}) collective-permute-start(bf16[576,512]{1,0:T(8,128)(2,1)} %get-tuple-element.913), channel_id=1, source_target_pairs={{16,0},{17,1},{18,2},{19,3},{20,4},{21,5},{22,6},{23,7},{24,8},{25... | collective-permute-start | bytes 1769480 | tf_op jit(solution)/shard_map/while/body/eval_jaxpr/ppermute | solution.py:26
  579.0 28.5 %collective-permute-start.1 = (bf16[576,512]{1,0:T(8,128)(2,1)}, bf16[576,512]{1,0:T(8,128)(2,1)}, u32[]{:S(2)}, u32[]{:S(2)}) collective-permute-start(bf16[576,512]{1,0:T(8,128)(2,1)} %get-tuple-element.913), channel_id=1, source_target_pairs={{16,0},{17,1},{18,2},{19,3},{20,4},{21,5},{22,6},{23,7},{24,8},{25... | collective-permute-start | bytes 1769480 | tf_op jit(solution)/shard_map/while/body/eval_jaxpr/ppermute | solution.py:26
  674.9 28.5 %collective-permute-start.1 = (bf16[576,512]{1,0:T(8,128)(2,1)}, bf16[576,512]{1,0:T(8,128)(2,1)}, u32[]{:S(2)}, u32[]{:S(2)}) collective-permute-start(bf16[576,512]{1,0:T(8,128)(2,1)} %get-tuple-element.913), channel_id=1, source_target_pairs={{16,0},{17,1},{18,2},{19,3},{20,4},{21,5},{22,6},{23,7},{24,8},{25... | collective-permute-start | bytes 1769480 | tf_op jit(solution)/shard_map/while/body/eval_jaxpr/ppermute | solution.py:26
  770.8 28.5 %collective-permute-start.1 = (bf16[576,512]{1,0:T(8,128)(2,1)}, bf16[576,512]{1,0:T(8,128)(2,1)}, u32[]{:S(2)}, u32[]{:S(2)}) collective-permute-start(bf16[576,512]{1,0:T(8,128)(2,1)} %get-tuple-element.913), channel_id=1, source_target_pairs={{16,0},{17,1},{18,2},{19,3},{20,4},{21,5},{22,6},{23,7},{24,8},{25... | collective-permute-start | bytes 1769480 | tf_op jit(solution)/shard_map/while/body/eval_jaxpr/ppermute | solution.py:26
  866.7 28.5 %collective-permute-start.1 = (bf16[576,512]{1,0:T(8,128)(2,1)}, bf16[576,512]{1,0:T(8,128)(2,1)}, u32[]{:S(2)}, u32[]{:S(2)}) collective-permute-start(bf16[576,512]{1,0:T(8,128)(2,1)} %get-tuple-element.913), channel_id=1, source_target_pairs={{16,0},{17,1},{18,2},{19,3},{20,4},{21,5},{22,6},{23,7},{24,8},{25... | collective-permute-start | bytes 1769480 | tf_op jit(solution)/shard_map/while/body/eval_jaxpr/ppermute | solution.py:26
  898.9 154.9 %reduce-scatter.22.cloned.1.call-start = ((), (), s32[]{:S(2)}) async-start(), calls=%async_computation.14 | async-start | bytes 278528
  900.5 227.9 %reduce-scatter.24.cloned.1.call-start = ((), (), s32[]{:S(2)}) async-start(), calls=%async_computation.15 | async-start | bytes 278528
  902.1 303.2 %reduce-scatter.16.cloned.1.call-start = ((), (), s32[]{:S(2)}) async-start(), calls=%async_computation.11 | async-start | bytes 1114112 | tf_op jit(solution)/shard_map/reduce_scatter | solution.py:294
  902.9 435.1 %reduce-scatter.14.cloned.1.call-start = ((), (), s32[]{:S(2)}) async-start(), calls=%async_computation.10 | async-start | bytes 3342336 | tf_op jit(solution)/shard_map/reduce_scatter | solution.py:293
  903.6 531.6 %reduce-scatter.18.cloned.1.call-start = ((), (), s32[]{:S(2)}) async-start(), calls=%async_computation.12 | async-start | bytes 4456448 | tf_op jit(solution)/shard_map/reduce_scatter | solution.py:295
  904.4 628.3 %reduce-scatter.20.cloned.1.call-start = ((), (), s32[]{:S(2)}) async-start(), calls=%async_computation.13 | async-start | bytes 4456448 | tf_op jit(solution)/shard_map/reduce_scatter | solution.py:296
  909.8 221.5 %collective-permute-start.4 = (bf16[4,256,512]{2,1,0:T(8,128)(2,1)}, bf16[4,256,512]{2,1,0:T(8,128)(2,1)S(1)}, u32[]{:S(2)}, u32[]{:S(2)}) collective-permute-start(bf16[4,256,512]{2,1,0:T(8,128)(2,1)} %constant_dynamic-slice_fusion.1), channel_id=1, source_target_pairs={{0,16},{16,0},{1,17},{17,1},{2,18},{18,2},{3,19},{19,3},{4,20},{20... | collective-permute-start | bytes 3145736 | tf_op jit(solution)/shard_map/ppermute | solution.py:20
  956.1 173.6 %collective-permute-start.5 = (bf16[4,32,512]{2,1,0:T(8,128)(2,1)S(1)}, bf16[4,32,512]{2,1,0:T(8,128)(2,1)}, u32[]{:S(2)}, u32[]{:S(2)}) collective-permute-start(bf16[4,32,512]{2,1,0:T(8,128)(2,1)S(1)} %constant_dynamic-slice_fusion), channel_id=1, source_target_pairs={{0,16},{16,0},{1,17},{17,1},{2,18},{18,2},{3,19},{19,3},{4,20},{20... | collective-permute-start | bytes 393224 | tf_op jit(solution)/shard_map/ppermute | solution.py:20
  (211 other events, 1548.0 us)
Sparse Core Ops, SparseCore 0:
  10.9 61.7 all-gather.5
  75.4 60.8 all-gather.7
  139.0 59.3 all-gather.3
  899.0 79.5 reduce-scatter.25
  981.3 72.4 reduce-scatter.21
  1055.9 72.4 reduce-scatter.23
  1131.3 73.9 reduce-scatter.15
  1210.8 127.0 reduce-scatter.13
  1340.8 94.3 reduce-scatter.17
  1437.9 94.7 reduce-scatter.19
where the time goes:
time: 1550 us; the launch traced here: 1540 us
  waiting for transfers between devices  666 us (43%)
  matrix products  403 us (26%)
  other arithmetic  144 us (9%)
  local copies, waits for them, and re-layouts  130 us (8%)
  blocking collectives  126 us (8%)
  loops' own time  32.2 us (2%)
  starting transfers between devices  24 us (2%)
    unnamed x13, waiting for transfers between devices  173 us
    reduce_scatter x1, waiting for transfers between devices, body(): lax.psum_scatter(grad_acc[0][None], 'dp', scatter_dimension=1, tiled=True)  133 us
    dot_general x20, matrix products, inner_rows(): lax.dot_general(left_mat, right_mat, (((0,), (0,)), ((), ())), preferred_...  104 us
    reduce_scatter x1, waiting for transfers between devices, body(): lax.psum_scatter(grad_acc[3][None], 'dp', scatter_dimension=1, tiled=True)  97.5 us
    reduce_scatter x1, waiting for transfers between devices, body(): lax.psum_scatter(grad_acc[2][None], 'dp', scatter_dimension=1, tiled=True)  97.3 us
    reduce_scatter x1, waiting for transfers between devices, body(): lax.psum_scatter(grad_acc[1][None], 'dp', scatter_dimension=1, tiled=True)  72.2 us
    all_gather x1, waiting for transfers between devices, body(): lax.all_gather(w_down, 'dp', axis=1, tiled=True)  62.2 us
    dot_general x20, matrix products, times_trans(): lax.dot_general(left_mat, right_mat, (((1,), (1,)), ((), ())), preferred_...  61.5 us
  transfers between devices with their start and end apart: 24, of which 9 were waited for; matrix products, arithmetic and copies ran while one was open for 11% of the time, Pallas kernels for 0%

commit v1 on v0

v1 whole, which is shorter than its diff:
```python
from functools import partial

import jax
import jax.numpy as jnp
from jax import lax
from jax.experimental import pallas as pl
from jax.experimental.pallas import tpu as pltpu
from jax.sharding import PartitionSpec as P

norm_eps = 1e-06
score_scale = 0.125
log2_e = 1.4426950408889634
masked_score = -1000000000.0
gelu_c = 0.7978845608028654
gelu_k = 0.044715
f32 = jnp.float32
bf16 = jnp.bfloat16
lanes = 128
chunk = 512


def mm(a, b, ca=1, cb=0):
    return lax.dot_general(a, b, (((ca,), (cb,)), ((), ())), preferred_element_type=f32)


def nt(a, b):
    return mm(a, b, 1, 1)


def tn(a, b):
    return mm(a, b, 0, 0)


def lane_marks(head_size, side):
    lane = lax.broadcasted_iota(jnp.int32, (1, lanes), 1)
    own = ((lane // head_size) == side).astype(f32)
    first = (1 - side) * head_size
    marks = [(lane == first + k).astype(f32) for k in range(3)]
    return own, marks


def fused_layers(dims, *refs):
    segs, rows, width, ff, slots, heads = dims
    (
        len_ref, u0_ref, dout_ref, gain_a, gain_f, bias_ref,
        wq_in, wo_in, wu_in, wd_in,
        y_ref, du_ref, gq_out, go_out, gu_out, gd_out,
        dga_ref, dgf_ref, dbias_ref, stat_ref,
        qkv_hbm, e_hbm, o_hbm, il_hbm, pre_hbm,
        wq, wo, wu, wd, ub, dy, qkv, ebuf, obuf, ilbuf, hbuf, pre, doa, dn, n2buf,
        sem_w, sem_spill, sem_back, sem_g, sem_io,
    ) = refs
    head_size = width // heads
    pairs = width // lanes
    all_rows = segs * rows
    tok_rows = rows - slots
    doc_len = len_ref[0]

    def weight_copies(layer, picks=range(4)):
        return [
            pltpu.make_async_copy(src.at[layer], dst.at[layer], sem_w.at[layer, k])
            for k, (src, dst) in enumerate(((wq_in, wq), (wo_in, wo), (wu_in, wu), (wd_in, wd)))
            if k in picks
        ]

    for layer in range(2):
        for copy in weight_copies(layer):
            copy.start()

    def seg_rows(s):
        return pl.ds(pl.multiple_of(s * rows, rows), rows)

    def spill_copies(s, back, picks=range(5)):
        at = seg_rows(s)
        pairs_of = (
            (qkv.at[at], qkv_hbm.at[at]),
            (ebuf.at[s], e_hbm.at[s]),
            (obuf.at[at], o_hbm.at[at]),
            (ilbuf.at[at], il_hbm.at[at]),
            (pre.at[at], pre_hbm.at[at]),
        )
        if back:
            return [
                pltpu.make_async_copy(hbm, vmem, sem_back.at[s, k])
                for k, (vmem, hbm) in enumerate(pairs_of)
                if k in picks
            ]
        return [
            pltpu.make_async_copy(vmem, hbm, sem_spill.at[s, k])
            for k, (vmem, hbm) in enumerate(pairs_of)
            if k in picks
        ]

    def valid_col(s):
        row = lax.broadcasted_iota(jnp.int32, (rows, 1), 0)
        return jnp.where(
            (row >= slots) & (s * tok_rows + row - slots < doc_len), 1.0, 0.0
        ).astype(f32)

    def mask_col(s):
        row = lax.broadcasted_iota(jnp.int32, (rows, 1), 0)
        return jnp.where(
            (row >= slots) & (s * tok_rows + row - slots >= doc_len), masked_score, 0.0
        ).astype(f32)

    loads = [
        pltpu.make_async_copy(u0_ref, ub.at[0], sem_io.at[0]),
        pltpu.make_async_copy(dout_ref, dy, sem_io.at[1]),
    ]
    y_copy = pltpu.make_async_copy(ub.at[2], y_ref, sem_io.at[2])
    du_copy = pltpu.make_async_copy(dy, du_ref, sem_io.at[3])
    for copy in loads:
        copy.start()
    stat_ref[...] = jnp.zeros_like(stat_ref)
    dga_ref[...] = jnp.zeros_like(dga_ref)
    dgf_ref[...] = jnp.zeros_like(dgf_ref)
    dbias_ref[...] = jnp.zeros_like(dbias_ref)

    for copy in loads:
        copy.wait()

    def add_stat(layer, k, row_sums, valid):
        total = jnp.sum(row_sums * valid, axis=0, keepdims=True)
        stat_ref[layer, k : k + 1, :] += jnp.broadcast_to(total, (1, lanes))

    def forward_attention(layer, s):
        at = seg_rows(s)
        mask = mask_col(s)
        for p in range(pairs):
            cols = slice(p * lanes, (p + 1) * lanes)
            qp = qkv[at, cols]
            kp = qkv[at, slice(width + p * lanes, width + (p + 1) * lanes)]
            vp = qkv[at, slice(2 * width + p * lanes, 2 * width + (p + 1) * lanes)]
            outs = []
            for side in range(2):
                h = 2 * p + side
                own, marks = lane_marks(head_size, side)
                bias = jnp.broadcast_to(bias_ref[layer, :, h : h + 1], (slots, lanes))
                hi = bias.astype(bf16).astype(f32)
                aux = jnp.concatenate([hi * marks[1] + (bias - hi) * marks[2], jnp.zeros((tok_rows, lanes), f32)], axis=0)
                aux = aux + mask * marks[0]
                every = marks[0] + marks[1] + marks[2]
                ka = kp * own.astype(bf16) + aux.astype(bf16)
                qa = qp * (1.0 - every).astype(bf16) + every.astype(bf16)
                scores = nt(qa, ka)
                top = jnp.max(scores, axis=1, keepdims=True)
                weights = jnp.exp2(scores - top).astype(bf16)
                ebuf[s, h] = weights
                va = vp * own.astype(bf16) + (1.0 - own).astype(bf16)
                outs.append(mm(weights, va))
            own, _ = lane_marks(head_size, 0)
            raw = jnp.where(own > 0, outs[0], outs[1])
            sums = pltpu.roll(jnp.where(own > 0, outs[1], outs[0]), head_size, 1)
            inv = 1.0 / sums
            ilbuf[at, cols] = inv.astype(ilbuf.dtype)
            obuf[at, cols] = (raw * inv).astype(bf16)

    def forward_seg(layer, s):
        at = seg_rows(s)

        @pl.when(layer == 1)
        def _():
            for copy in spill_copies(s, False):
                copy.wait()

        @pl.when(s == 0)
        def _():
            weight_copies(layer, (0,))[0].wait()

        valid = valid_col(s)
        x = ub[layer, at, :].astype(f32)
        squares = jnp.sum(x * x, axis=1, keepdims=True)
        add_stat(layer, 0, squares, valid)
        n1 = (x * lax.rsqrt(squares / width + norm_eps) * gain_a[layer]).astype(bf16)
        for k in range(3):
            part = mm(n1, wq[layer, :, k * width : (k + 1) * width])
            if k == 0:
                part = part * (score_scale * log2_e)
            qkv[at, k * width : (k + 1) * width] = part.astype(bf16)
        forward_attention(layer, s)

        @pl.when(layer == 0)
        def _():
            for copy in spill_copies(s, False, range(4)):
                copy.start()

        @pl.when(s == 0)
        def _():
            for copy in weight_copies(layer, (1, 2, 3)):
                copy.wait()

        z = mm(obuf[at, :], wo[layer])
        add_stat(layer, 1, jnp.sum(z * z, axis=1, keepdims=True), valid)
        h = ub[layer, at, :].astype(f32) + z
        hbuf[layer, at, :] = h.astype(bf16)
        dn[at, :] = h
        n2 = (h * lax.rsqrt(jnp.mean(h * h, axis=1, keepdims=True) + norm_eps) * gain_f[layer]).astype(bf16)
        n2buf[at, :] = n2
        out = None
        for c in range(ff // chunk):
            cols = slice(c * chunk, (c + 1) * chunk)
            before = mm(n2buf[at, :], wu[layer, :, cols])
            pre[at, cols] = before.astype(bf16)
            gate = 0.5 + 0.5 * jnp.tanh(before * (gelu_c + (gelu_c * gelu_k) * (before * before)))
            part = mm((before * gate).astype(bf16), wd[layer, cols, :])
            out = part if out is None else out + part
        add_stat(layer, 2, jnp.sum(out * out, axis=1, keepdims=True), valid)
        ub[layer + 1, at, :] = (dn[at, :] + out).astype(bf16)

        @pl.when(layer == 0)
        def _():
            spill_copies(s, False, (4,))[0].start()

    @pl.loop(0, 2 * segs)
    def _(step):
        forward_seg(step // segs, step % segs)

    y_copy.start()

    def norm_back(x, gain, grad):
        inv = lax.rsqrt(jnp.mean(x * x, axis=1, keepdims=True) + norm_eps)
        hat = x * inv
        dgain = jnp.sum(grad * hat, axis=0, keepdims=True)
        scaled = grad * gain
        return inv * (scaled - hat * jnp.mean(scaled * hat, axis=1, keepdims=True)), dgain

    def backward_ffn(layer):
        slot = layer + 1

        @pl.loop(0, segs)
        def _(s):
            at = seg_rows(s)
            h = hbuf[layer, at, :].astype(f32)
            n2buf[at, :] = (h * lax.rsqrt(jnp.mean(h * h, axis=1, keepdims=True) + norm_eps) * gain_f[layer]).astype(bf16)

        dn[...] = jnp.zeros_like(dn)

        @pl.loop(0, ff // chunk)
        def _(c):
            cols = pl.ds(pl.multiple_of(c * chunk, chunk), chunk)
            d_act = nt(dy[...], wd[layer, cols, :])
            x = pre[:, cols].astype(f32)
            sq = x * x
            gate = 0.5 + 0.5 * jnp.tanh(x * (gelu_c + (gelu_c * gelu_k) * sq))
            act = x * gate
            slope = gate + act * (1.0 - gate) * (2.0 * gelu_c + (6.0 * gelu_c * gelu_k) * sq)
            d_pre = (d_act * slope).astype(bf16)
            pre[:, cols] = d_pre
            wd[slot, cols, :] = tn(act.astype(bf16), dy[...]).astype(bf16)
            wu[slot, :, cols] = tn(n2buf[...], d_pre).astype(bf16)
            dn[...] += nt(d_pre, wu[layer, :, cols])

    def backward_middle(layer, s):
        at = seg_rows(s)
        dh, dgain = norm_back(hbuf[layer, at, :].astype(f32), gain_f[layer], dn[at, :])
        dgf_ref[layer] += dgain
        dh = dh + dy[at, :].astype(f32)
        dn[at, :] = dh
        dz = dh.astype(bf16)
        dy[at, :] = dz
        do = nt(dz, wo[layer]) * ilbuf[at, :].astype(f32)
        prod = do.astype(bf16).astype(f32) * obuf[at, :].astype(f32)
        for p in range(pairs):
            cols = slice(p * lanes, (p + 1) * lanes)
            for side in range(2):
                own, marks = lane_marks(head_size, side)
                delta = -jnp.sum(prod[:, cols] * own, axis=1, keepdims=True)
                hi = delta.astype(bf16).astype(f32)
                fill = hi * marks[0] + (delta - hi) * marks[1]
                doa[side, at, cols] = (do[:, cols] * (1.0 - marks[0] - marks[1]) + fill).astype(bf16)

    def backward_attention(layer, s):
        at = seg_rows(s)
        for p in range(pairs):
            cols = slice(p * lanes, (p + 1) * lanes)
            kcols = slice(width + p * lanes, width + (p + 1) * lanes)
            vcols = slice(2 * width + p * lanes, 2 * width + (p + 1) * lanes)
            qp = qkv[at, cols]
            kp = qkv[at, kcols]
            vp = qkv[at, vcols]
            q_turned = qp.T
            dq, dk, dv = [], [], []
            for side in range(2):
                h = 2 * p + side
                own, marks = lane_marks(head_size, side)
                do_h = doa[side, at, cols]
                va = vp * own.astype(bf16) + (marks[0] + marks[1]).astype(bf16)
                weights = ebuf[s, h]
                d_scores = weights.astype(f32) * nt(do_h, va)
                dbias_ref[layer, h : h + 1, :] += jnp.sum(d_scores[:, :lanes], axis=0, keepdims=True)
                d_scores = d_scores.astype(bf16)
                half = slice(side * head_size, (side + 1) * head_size)
                dq.append(mm(d_scores, kp))
                dk.append(mm(q_turned[half, :], d_scores))
                dv.append(mm(do_h.T[half, :], weights))
            own, _ = lane_marks(head_size, 0)
            qkv[at, cols] = (jnp.where(own > 0, dq[0], dq[1]) * score_scale).astype(bf16)
            qkv[at, kcols] = (jnp.concatenate(dk, axis=0).T * (1.0 / log2_e)).astype(bf16)
            qkv[at, vcols] = jnp.concatenate(dv, axis=0).T.astype(bf16)

    def backward_input(layer, s):
        at = seg_rows(s)
        x = ub[layer, at, :].astype(f32)
        du, dgain = norm_back(x, gain_a[layer], nt(qkv[at, :], wq[layer]))
        dga_ref[layer] += dgain
        dy[at, :] = (du + dn[at, :]).astype(bf16)
        n2buf[at, :] = (x * lax.rsqrt(jnp.mean(x * x, axis=1, keepdims=True) + norm_eps) * gain_a[layer]).astype(bf16)

    def grad_copies(layer, picks=range(4)):
        slot = layer + 1
        return [
            pltpu.make_async_copy(src.at[slot], dst.at[layer], sem_g.at[layer, k])
            for k, (src, dst) in enumerate(((wq, gq_out), (wo, go_out), (wu, gu_out), (wd, gd_out)))
            if k in picks
        ]

    @pl.loop(0, 2)
    def _(step):
        layer = 1 - step
        slot = layer + 1

        @pl.when(layer == 0)
        def _():
            for s in range(segs):
                for copy in spill_copies(s, True, (2, 3, 4)):
                    copy.wait()

        backward_ffn(layer)

        @pl.loop(0, segs)
        def _(s):
            backward_middle(layer, s)

        wo[slot] = tn(obuf[...], dy[...]).astype(bf16)
        for copy in grad_copies(layer, (1, 2, 3)):
            copy.start()

        @pl.when(layer == 1)
        def _():
            for s in range(segs):
                for copy in spill_copies(s, True, (2, 3, 4)):
                    copy.start()

        @pl.loop(0, segs)
        def _(s):
            @pl.when(layer == 0)
            def _():
                for copy in spill_copies(s, True, (0, 1)):
                    copy.wait()

            backward_attention(layer, s)

            @pl.when(layer == 1)
            def _():
                spill_copies(s, True, (1,))[0].start()

        @pl.loop(0, segs)
        def _(s):
            backward_input(layer, s)

        for k in range(3):
            part = slice(k * width, (k + 1) * width)
            wq[slot, :, part] = tn(n2buf[...], qkv[:, part]).astype(bf16)
        grad_copies(layer, (0,))[0].start()

        @pl.when(layer == 1)
        def _():
            for s in range(segs):
                spill_copies(s, True, (0,))[0].start()

        for copy in grad_copies(layer):
            copy.wait()

    du_copy.start()
    du_copy.wait()
    y_copy.wait()


def run_layers(doc_len, u0, dout, gains, bias, weights, heads, slots, segs):
    all_rows, width = u0.shape
    rows = all_rows // segs
    ff = weights[2].shape[2]
    dims = (segs, rows, width, ff, slots, heads)
    vmem = pl.BlockSpec(memory_space=pltpu.VMEM)
    smem = pl.BlockSpec(memory_space=pltpu.SMEM)
    hbm = pl.BlockSpec(memory_space=pl.ANY)
    shape = jax.ShapeDtypeStruct
    wide = (all_rows, width)
    spills = [
        shape((all_rows, 3 * width), bf16),
        shape((segs, heads, rows, rows), bf16),
        shape(wide, bf16),
        shape(wide, bf16),
        shape((all_rows, ff), bf16),
    ]
    out_shape = [
        shape(wide, bf16),
        shape(wide, bf16),
        shape((2, width, 3 * width), bf16),
        shape((2, width, width), bf16),
        shape((2, width, ff), bf16),
        shape((2, ff, width), bf16),
        shape((2, 1, width), f32),
        shape((2, 1, width), f32),
        shape((2, heads, lanes), f32),
        shape((2, 8, lanes), f32),
    ] + spills
    scratch = [
        pltpu.VMEM((3, width, 3 * width), bf16),
        pltpu.VMEM((3, width, width), bf16),
        pltpu.VMEM((3, width, ff), bf16),
        pltpu.VMEM((3, ff, width), bf16),
        pltpu.VMEM((3, *wide), bf16),
        pltpu.VMEM(wide, bf16),
        pltpu.VMEM((all_rows, 3 * width), bf16),
        pltpu.VMEM((segs, heads, rows, rows), bf16),
        pltpu.VMEM(wide, bf16),
        pltpu.VMEM(wide, bf16),
        pltpu.VMEM((2, *wide), bf16),
        pltpu.VMEM((all_rows, ff), bf16),
        pltpu.VMEM((2, *wide), bf16),
        pltpu.VMEM(wide, f32),
        pltpu.VMEM(wide, bf16),
        pltpu.SemaphoreType.DMA((2, 4)),
        pltpu.SemaphoreType.DMA((segs, 5)),
        pltpu.SemaphoreType.DMA((segs, 5)),
        pltpu.SemaphoreType.DMA((2, 4)),
        pltpu.SemaphoreType.DMA((4,)),
    ]
    return pl.pallas_call(
        partial(fused_layers, dims),
        out_shape=out_shape,
        in_specs=[smem] + [hbm] * 2 + [vmem] * 3 + [hbm] * 4,
        out_specs=[hbm] * 6 + [vmem] * 4 + [hbm] * 5,
        scratch_shapes=scratch,
        compiler_params=pltpu.CompilerParams(vmem_limit_bytes=63 * 2**20),
    )(doc_len, u0, dout, *gains, bias, *weights)[:10]


def swap(block):
    return lax.ppermute(block, "section", [(0, 1), (1, 0)])


def body(
    tokens,
    memory,
    lengths,
    w_qkv,
    w_out,
    w_up,
    w_down,
    gain_attn,
    gain_ffn,
    forget_bias,
    grad_tokens,
    grad_memory,
):
    section = lax.axis_index("section")
    is_first = section == 0
    micro = tokens.shape[0]
    segs = micro // 2
    half_tok = tokens.shape[1]
    half_mem = memory.shape[1]
    slots = 2 * half_mem
    seg_len = 2 * half_tok
    rows = slots + seg_len
    width = tokens.shape[2]

    def own_segs(halves):
        return lax.dynamic_slice_in_dim(halves, section * segs, segs, 0)

    def other_segs(halves):
        return lax.dynamic_slice_in_dim(halves, (1 - section) * segs, segs, 0)

    def both(kept, got):
        return jnp.concatenate(
            [jnp.where(is_first, kept, got), jnp.where(is_first, got, kept)], axis=1
        )

    inputs = (tokens, memory, grad_tokens, grad_memory)
    got = swap(tuple(other_segs(part) for part in inputs))
    full = [both(own_segs(part), other) for part, other in zip(inputs, got)]
    u0 = jnp.concatenate([full[1], full[0]], axis=1).reshape(segs * rows, width)
    dout = jnp.concatenate([full[3], full[2]], axis=1).reshape(segs * rows, width)

    def gather(piece):
        return lax.all_gather(piece, ("section", "dp"), axis=1, tiled=True).reshape(2, -1, *piece.shape[2:])

    weights = tuple(gather(piece) for piece in (w_qkv, w_out, w_up, w_down))
    gains = [gather(piece).astype(f32)[:, None, :] for piece in (gain_attn, gain_ffn)]
    bias_flat = gather(forget_bias).astype(f32)
    heads = bias_flat.shape[1] // slots
    bias = jnp.pad(bias_flat.reshape(2, slots, heads) * log2_e, ((0, 0), (0, 0), (0, lanes - heads)))
    per_doc = micro // lengths.shape[0]
    own_len = lax.dynamic_slice_in_dim(lengths, section * segs // per_doc, 1, 0)
    y, du, gq, go, gu, gd, dga, dgf, dbias, stats = run_layers(
        own_len, u0, dout, gains, bias, weights, heads, slots, segs
    )

    def scatter(grad):
        mine = lax.dynamic_index_in_dim(grad, section, 0, keepdims=True)
        other = lax.dynamic_index_in_dim(grad, 1 - section, 0, keepdims=True)
        chip = (mine.astype(f32) + swap(other).astype(f32)).astype(grad.dtype)
        return lax.psum_scatter(chip, "dp", scatter_dimension=1, tiled=True).astype(f32)

    grad_bias = jnp.swapaxes(dbias[:, :, :slots], 1, 2).reshape(2, slots * heads)
    shares = tuple(scatter(grad) for grad in (gq, go, gu, gd, dga[:, 0], dgf[:, 0], grad_bias))
    token_count = jnp.sum(own_len).astype(f32)
    sums = jnp.concatenate([stats[:, :3, 0].reshape(6), token_count[None]])
    totals = lax.psum(sums, ("section", "dp"))
    rms = jnp.sqrt(totals[:6].reshape(2, 3) / (totals[6] * width))

    result = jnp.stack([y.reshape(segs, rows, width), du.reshape(segs, rows, width)])

    def half_of(which):
        tok = lax.dynamic_slice_in_dim(result, slots + which * half_tok, half_tok, 2)
        mem = lax.dynamic_slice_in_dim(result, which * half_mem, half_mem, 2)
        return tok, mem

    kept = half_of(section)
    got = swap(half_of(1 - section))

    def order(mine, other):
        return jnp.concatenate(
            [jnp.where(is_first, mine, other), jnp.where(is_first, other, mine)], axis=0
        )

    toks = [order(kept[0][k], got[0][k]) for k in range(2)]
    mems = [order(kept[1][k], got[1][k]) for k in range(2)]
    return (toks[0], mems[0], toks[1], mems[1], *shares, rms)


def solution(mesh):
    rows = P("dp", "section", None)
    mats = P("section", "dp", None)
    vecs = P("section", "dp")
    return jax.shard_map(
        body,
        mesh=mesh,
        in_specs=(rows, rows, P("dp"), mats, mats, mats, mats, vecs, vecs, vecs, rows, rows),
        out_specs=(rows, rows, rows, rows, mats, mats, mats, mats, vecs, vecs, vecs, P()),
        check_vma=False,
    )
```

time: 1550 us -> 985 us (0.64)
  matrix products: 403 us -> 0 us
  Pallas kernels: 0 us -> 123 us
  other arithmetic: 144 us -> 26.2 us
  local copies, waits for them, and re-layouts: 130 us -> 24 us
  blocking collectives: 126 us -> 81.3 us
  waiting for transfers between devices: 666 us -> 709 us
  loops' own time: 32.2 us -> 0 us
  starting transfers between devices: 24 us -> 3.83 us
    dot_general x110 -> x0, matrix products: 403 us -> none  [the longest x20 104 us: inner_rows(): lax.dot_general(left_mat, right_mat, (((0,), (0,)), ((), ())), preferred_...]
    pallas_call x0 -> x1, Pallas kernels: none -> 123 us  [run_layers(): pl.pallas_call(partial(fused_layers, dims), out_shape=out_shape, in_specs...]
    all_gather x3 -> x4, waiting for transfers between devices: 92.5 us -> 192 us  [gather(): lax.all_gather(piece, ('section', 'dp'), axis=1, tiled=True)]
    reduce_sum x42 -> x0, other arithmetic: 52.4 us -> none  [the longest x10 26.9 us: layer_forward(): jnp.sum(jnp.exp(scores - row_max), axis=-1, keepdims=True)]
    while x405 -> x0, local copies, waits for them, and re-layouts: 49.3 us -> none
    reduce_scatter x4, waiting for transfers between devices: 400 us -> 353 us  [scatter(): lax.psum_scatter(chip, 'dp', scatter_dimension=1, tiled=True).astype(f32)]
    squeeze x1 -> x0, blocking collectives: 44.3 us -> none  [body(): weights = tuple((piece[0] for piece in gathered))]
    all_gather x1 -> x0, blocking collectives: 42.4 us -> none  [body(): lax.all_gather(w_out, 'dp', axis=1, tiled=True)]
  transfers between devices with their start and end apart: 24 -> 24, of which waited for: 9 -> 13; matrix products, arithmetic and copies ran while one was open for 11% -> 5% of each run, Pallas kernels for 0% -> 0%
where the time goes in v1:
time: 985 us; the launch traced here: 983 us
  waiting for transfers between devices  709 us (72%)
  Pallas kernels  123 us (12%)
  blocking collectives  81.3 us (8%)
  other arithmetic  26.2 us (3%)
  local copies, waits for them, and re-layouts  24 us (2%)
  between operations  15.5 us (2%)
    reduce_scatter x4, waiting for transfers between devices, scatter(): lax.psum_scatter(chip, 'dp', scatter_dimension=1, tiled=True).astype(f32)  353 us
    all_gather x4, waiting for transfers between devices, gather(): lax.all_gather(piece, ('section', 'dp'), axis=1, tiled=True)  192 us
    unnamed x14, waiting for transfers between devices  156 us
    pallas_call x1, Pallas kernels, run_layers(): pl.pallas_call(partial(fused_layers, dims), out_shape=out_shape, in_specs...  123 us
    unnamed x1, blocking collectives  42.1 us
    psum x1, blocking collectives, body(): totals = lax.psum(sums, ('section', 'dp'))  39.1 us
  transfers between devices with their start and end apart: 24, of which 13 were waited for; matrix products, arithmetic and copies ran while one was open for 5% of the time, Pallas kernels for 0%

profile of v1, /device:TPU:0, one launch (start us, length us, event | category | flops | bytes accessed | tf_op | source)
XLA Modules:
  0.0 983.5 jit_solution(4661359560951484123)
XLA Ops:
  15.6 42.1 %all-reduce.4 = (bf16[1024]{0:T(1024)(128)(2,1)S(1)}, bf16[1024]{0:T(1024)(128)(2,1)S(1)}, bf16[1024]{0:T(1024)(128)(2,1)S(1)}) all-reduce(bf16[1024]{0:T(1024)(128)(2,1)S(1)} %dynamic-update-slice, bf16[1024]{0:T(1024)(128)(2,1)S(1)} %dynamic-update-slice.1, ...), channel_id=1, replica_groups=mesh['section'=2,'dp'=16] {'section','dp'}, use_global_device_ids=true, to_apply=%add.1 | all-reduce | flops 3072 | bytes 12288
  64.7 3.0 all-gather.7.cloned.1.call-done
  67.7 61.2 %all-gather.5.cloned.1.call-done = bf16[1,1024,1536]{2,1,0:T(8,128)(2,1)} async-done(((bf16[1,32,1536]{2,1,0:T(8,128)(2,1)}), bf16[1,1024,1536]{2,1,0:T(8,128)(2,1)}) %all-gather.5.cloned.1.call-update) | async-done | bytes 3145744 | tf_op jit(solution)/shard_map/all_gather | solution.py:487
  128.8 63.9 %all-gather.9.cloned.1.call-done = bf16[1,1024,2048]{2,1,0:T(8,128)(2,1)} async-done(((bf16[1,32,2048]{2,1,0:T(8,128)(2,1)}), bf16[1,1024,2048]{2,1,0:T(8,128)(2,1)}) %all-gather.9.cloned.1.call-update) | async-done | bytes 4194320 | tf_op jit(solution)/shard_map/all_gather | solution.py:487
  192.7 63.5 %all-gather.11.cloned.1.call-done = bf16[1,4096,512]{2,1,0:T(8,128)(2,1)} async-done(((bf16[1,128,512]{2,1,0:T(8,128)(2,1)}), bf16[1,4096,512]{2,1,0:T(8,128)(2,1)}) %all-gather.11.cloned.1.call-update) | async-done | bytes 4194320 | tf_op jit(solution)/shard_map/all_gather | solution.py:487
  256.2 123.4 %shard_map.211 = (bf16[1152,512]{1,0:T(8,128)(2,1)}, bf16[1152,512]{1,0:T(8,128)(2,1)}, bf16[2,512,1536]{2,1,0:T(8,128)(2,1)}, bf16[2,512,512]{2,1,0:T(8,128)(2,...) custom-call(s32[1]{0:T(128)} %dynamic_slice.94.refs_0_, ...), custom_call_target="tpu_custom_call" | custom-call | tf_op jit(solution)/shard_map/pallas_call | solution.py:430
  381.9 2.7 constant_dynamic-slice_fusion.9
  389.2 2.1 add_convert_fusion.3
  391.4 3.0 add_convert_fusion.2
  394.4 1.9 constant_dynamic-slice_fusion.6
  396.6 3.9 collective-permute-done.9
  400.6 1.9 add_convert_fusion
  402.6 1.9 constant_dynamic-slice_fusion.7
  404.8 3.9 collective-permute-done.8
  408.7 2.1 add_convert_fusion.1
  414.4 39.1 %psum.7 = f32[7]{0:T(128)S(1)} all-reduce(f32[7]{0:T(128)S(1)} %pad_maximum_fusion.6), channel_id=1, replica_groups=mesh['section'=2,'dp'=16] {'section','dp'}, use_global_device_ids=true, to_apply=%region_7.8 | all-reduce | flops 7 | bytes 56 | tf_op jit(solution)/shard_map/psum | solution.py:510
  456.2 5.8 reduce-scatter.26.cloned.1.call-done
  463.3 73.9 %reduce-scatter.24.cloned.1.call-done = f32[32,1]{1,0:T(8,128)} async-done(((f32[512,1]{1,0:T(8,128)}), f32[32,1]{1,0:T(8,128)}) %reduce-scatter.24.cloned.1.call-update) | async-done | bytes 144
  538.5 73.9 %reduce-scatter.22.cloned.1.call-done = f32[32,1]{1,0:T(8,128)} async-done(((f32[512,1]{1,0:T(8,128)}), f32[32,1]{1,0:T(8,128)}) %reduce-scatter.22.cloned.1.call-update) | async-done | bytes 144
  617.3 70.4 %reduce-scatter.16.cloned.1.call-done = bf16[1,32,512]{2,1,0:T(8,128)(2,1)} async-done(((bf16[1,512,512]{2,1,0:T(8,128)(2,1)}), bf16[1,32,512]{2,1,0:T(8,128)(2,1)}) %reduce-scatter.16.cloned.1.call-update) | async-done | bytes 32784 | tf_op jit(solution)/shard_map/reduce_scatter | solution.py:504
  689.0 124.4 %reduce-scatter.14.cloned.1.call-done = bf16[1,32,1536]{2,1,0:T(8,128)(2,1)} async-done(((bf16[1,512,1536]{2,1,0:T(8,128)(2,1)}), bf16[1,32,1536]{2,1,0:T(8,128)(2,1)}) %reduce-scatter.14.cloned.1.call-update) | async-done | bytes 98320 | tf_op jit(solution)/shard_map/reduce_scatter | solution.py:504
  815.0 80.3 %reduce-scatter.20.cloned.1.call-done = bf16[1,128,512]{2,1,0:T(8,128)(2,1)} async-done(((bf16[1,2048,512]{2,1,0:T(8,128)(2,1)}), bf16[1,128,512]{2,1,0:T(8,128)(2,1)}) %reduce-scatter.20.cloned.1.call-update) | async-done | bytes 131088 | tf_op jit(solution)/shard_map/reduce_scatter | solution.py:504
  895.3 1.6 convert_element_type.105
  896.9 78.4 %reduce-scatter.18.cloned.1.call-done = bf16[1,32,2048]{2,1,0:T(8,128)(2,1)} async-done(((bf16[1,512,2048]{2,1,0:T(8,128)(2,1)}), bf16[1,32,2048]{2,1,0:T(8,128)(2,1)}) %reduce-scatter.18.cloned.1.call-update) | async-done | bytes 131088 | tf_op jit(solution)/shard_map/reduce_scatter | solution.py:504
  (133 shorter events, 39.5 us)
Async XLA Ops:
  7.3 60.4 %all-gather.7.cloned.1.call-start = ((), (), s32[]{:S(2)}) async-start(), calls=%async_computation.8 | async-start | bytes 1081344 | tf_op jit(solution)/shard_map/all_gather | solution.py:487
  8.0 120.8 %all-gather.5.cloned.1.call-start = ((), (), s32[]{:S(2)}) async-start(), calls=%async_computation.7 | async-start | bytes 3244032 | tf_op jit(solution)/shard_map/all_gather | solution.py:487
  8.7 184.0 %all-gather.9.cloned.1.call-start = ((), (), s32[]{:S(2)}) async-start(), calls=%async_computation.9 | async-start | bytes 4325376 | tf_op jit(solution)/shard_map/all_gather | solution.py:487
  9.5 246.7 %all-gather.11.cloned.1.call-start = ((), (), s32[]{:S(2)}) async-start(), calls=%async_computation.10 | async-start | bytes 4325376 | tf_op jit(solution)/shard_map/all_gather | solution.py:487
  10.0 452.0 %reduce-scatter.26.cloned.1.call-start = ((), (), s32[]{:S(2)}) async-start(), calls=%async_computation.17 | async-start | bytes 278528
  11.2 50.8 %collective-permute-start.3 = (bf16[2,256,512]{2,1,0:T(8,128)(2,1)S(1)}, bf16[2,256,512]{2,1,0:T(8,128)(2,1)S(1)}, u32[]{:S(2)}, u32[]{:S(2)}) collective-permute-start(bf16[2,256,512]{2,1,0:T(8,128)(2,1)S(1)} %constant_dynamic-slice_fusion.10), channel_id=1, source_target_pairs={{0,16},{16,0},{1,17},{17,1},{2,18},{18,2},{3,19},{19,3},{4,20},{20... | collective-permute-start | bytes 1572872 | tf_op jit(solution)/shard_map/ppermute | solution.py:441
  12.5 47.7 %collective-permute-start.2 = (bf16[2,32,512]{2,1,0:T(8,128)(2,1)S(1)}, bf16[2,32,512]{2,1,0:T(8,128)(2,1)}, u32[]{:S(2)}, u32[]{:S(2)}) collective-permute-start(bf16[2,32,512]{2,1,0:T(8,128)(2,1)S(1)} %constant_dynamic-slice_fusion.11), channel_id=1, source_target_pairs={{0,16},{16,0},{1,17},{17,1},{2,18},{18,2},{3,19},{19,3},{4,20},{20... | collective-permute-start | bytes 196616 | tf_op jit(solution)/shard_map/ppermute | solution.py:441
  13.7 49.5 %collective-permute-start.1 = (bf16[2,256,512]{2,1,0:T(8,128)(2,1)S(1)}, bf16[2,256,512]{2,1,0:T(8,128)(2,1)S(1)}, u32[]{:S(2)}, u32[]{:S(2)}) collective-permute-start(bf16[2,256,512]{2,1,0:T(8,128)(2,1)S(1)} %constant_dynamic-slice_fusion.12), channel_id=1, source_target_pairs={{0,16},{16,0},{1,17},{17,1},{2,18},{18,2},{3,19},{19,3},{4,20},{20... | collective-permute-start | bytes 1572872 | tf_op jit(solution)/shard_map/ppermute | solution.py:441
  14.8 46.3 %collective-permute-start = (bf16[2,32,512]{2,1,0:T(8,128)(2,1)}, bf16[2,32,512]{2,1,0:T(8,128)(2,1)}, u32[]{:S(2)}, u32[]{:S(2)}) collective-permute-start(bf16[2,32,512]{2,1,0:T(8,128)(2,1)} %constant_dynamic-slice_fusion.13), channel_id=1, source_target_pairs={{0,16},{16,0},{1,17},{17,1},{2,18},{18,2},{3,19},{19,3},{4,20},{20... | collective-permute-start | bytes 196616 | tf_op jit(solution)/shard_map/ppermute | solution.py:441
  380.7 5.6 collective-permute-start.12
  381.7 5.5 collective-permute-start.11
  384.6 6.7 collective-permute-start.6
  384.9 3.3 collective-permute-start.10
  386.0 3.2 collective-permute-start.7
  387.2 150.0 %reduce-scatter.24.cloned.1.call-start = ((), (), s32[]{:S(2)}) async-start(), calls=%async_computation.16 | async-start | bytes 278528
  388.1 224.2 %reduce-scatter.22.cloned.1.call-start = ((), (), s32[]{:S(2)}) async-start(), calls=%async_computation.15 | async-start | bytes 278528
  389.1 298.5 %reduce-scatter.16.cloned.1.call-start = ((), (), s32[]{:S(2)}) async-start(), calls=%async_computation.12 | async-start | bytes 557056 | tf_op jit(solution)/shard_map/reduce_scatter | solution.py:504
  391.3 422.1 %reduce-scatter.14.cloned.1.call-start = ((), (), s32[]{:S(2)}) async-start(), calls=%async_computation.11 | async-start | bytes 1671168 | tf_op jit(solution)/shard_map/reduce_scatter | solution.py:504
  394.4 500.9 %reduce-scatter.20.cloned.1.call-start = ((), (), s32[]{:S(2)}) async-start(), calls=%async_computation.14 | async-start | bytes 2228224 | tf_op jit(solution)/shard_map/reduce_scatter | solution.py:504
  396.3 4.2 collective-permute-start.9
  402.5 572.8 %reduce-scatter.18.cloned.1.call-start = ((), (), s32[]{:S(2)}) async-start(), calls=%async_computation.13 | async-start | bytes 2228224 | tf_op jit(solution)/shard_map/reduce_scatter | solution.py:504
  404.5 4.2 collective-permute-start.8
  413.3 201.1 %collective-permute-start.4 = (bf16[2,2,256,512]{3,2,1,0:T(8,128)(2,1)}, bf16[2,2,256,512]{3,2,1,0:T(8,128)(2,1)}, u32[]{:S(2)}, u32[]{:S(2)}) collective-permute-start(bf16[2,2,256,512]{3,2,1,0:T(8,128)(2,1)} %get-tuple-element.38), channel_id=1, source_target_pairs={{0,16},{16,0},{1,17},{17,1},{2,18},{18,2},{3,19},{19,3},{4,20},{20... | collective-permute-start | bytes 3145736 | tf_op jit(solution)/shard_map/ppermute | solution.py:441
  454.8 158.8 %collective-permute-start.5 = (bf16[2,2,32,512]{3,2,1,0:T(8,128)(2,1)}, bf16[2,2,32,512]{3,2,1,0:T(8,128)(2,1)S(1)}, u32[]{:S(2)}, u32[]{:S(2)}) collective-permute-start(bf16[2,2,32,512]{3,2,1,0:T(8,128)(2,1)} %get-tuple-element.36), channel_id=1, source_target_pairs={{0,16},{16,0},{1,17},{17,1},{2,18},{18,2},{3,19},{19,3},{4,20},{20... | collective-permute-start | bytes 393224 | tf_op jit(solution)/shard_map/ppermute | solution.py:441
  (17 other events, 231.0 us)
Sparse Core Ops, SparseCore 0:
  11.2 56.4 all-gather.6
  70.5 58.2 all-gather.4
  131.8 60.8 all-gather.8
  195.5 60.5 all-gather.10
  387.3 74.6 reduce-scatter.25
  464.8 72.3 reduce-scatter.23
  540.0 72.3 reduce-scatter.21
  614.7 72.8 reduce-scatter.15
  692.4 120.9 reduce-scatter.13
  815.5 79.7 reduce-scatter.19
  897.5 77.7 reduce-scatter.17

commit v2 on v1

--- a/solution.py
+++ b/solution.py
@@ -39,33 +39,241 @@
     return own, marks
 
 
-def fused_layers(dims, *refs):
+def fused_layers(dims, routed, *refs):
     segs, rows, width, ff, slots, heads = dims
     (
-        len_ref, u0_ref, dout_ref, gain_a, gain_f, bias_ref,
-        wq_in, wo_in, wu_in, wd_in,
+        len_ref, u0_ref, dout_ref, wq_in, wo_in, wu_in, wd_in,
         y_ref, du_ref, gq_out, go_out, gu_out, gd_out,
         dga_ref, dgf_ref, dbias_ref, stat_ref,
         qkv_hbm, e_hbm, o_hbm, il_hbm, pre_hbm,
         wq, wo, wu, wd, ub, dy, qkv, ebuf, obuf, ilbuf, hbuf, pre, doa, dn, n2buf,
-        sem_w, sem_spill, sem_back, sem_g, sem_io,
+        gains, bias_rows, ext, sem_spill, sem_back, sem_g, sem_io,
+        sem_own, sem_send, sem_recv,
     ) = refs
     head_size = width // heads
     pairs = width // lanes
-    all_rows = segs * rows
     tok_rows = rows - slots
     doc_len = len_ref[0]
-
-    def weight_copies(layer, picks=range(4)):
-        return [
-            pltpu.make_async_copy(src.at[layer], dst.at[layer], sem_w.at[layer, k])
-            for k, (src, dst) in enumerate(((wq_in, wq), (wo_in, wo), (wu_in, wu), (wd_in, wd)))
-            if k in picks
+    weight_in = (wq_in, wo_in, wu_in, wd_in)
+    weight_buf = (wq, wo, wu, wd)
+    every = slice(None)
+
+    def units_of(layer):
+        half_ff, half_deep = ff // 2, ff // 64
+        lead = [
+            (0, slice(0, lanes + width), every),
+            (0, slice(lanes + width, lanes + 2 * width), every),
+            (0, slice(lanes + 2 * width, lanes + 3 * width), every),
         ]
-
-    for layer in range(2):
-        for copy in weight_copies(layer):
-            copy.start()
+        if layer == 1:
+            lead = [(0, every, every)]
+        rest = [(1, every, every)]
+        rest += [(2, slice(k * half_ff, (k + 1) * half_ff), every) for k in range(2)]
+        rest += [(3, every, slice(k * half_deep, (k + 1) * half_deep)) for k in range(2)]
+        return [(layer, *unit) for unit in lead + rest]
+
+    units = units_of(0) + units_of(1)
+    first_units = [k for k, unit in enumerate(units) if unit[1] == 0]
+    later_units = [k for k, unit in enumerate(units) if unit[1] != 0]
+
+    def view(n, z, y, x, c):
+        layer, which, cols, part = units[n]
+        return weight_buf[which].at[layer, z, y, x, c, part, cols]
+
+    if routed:
+        core = lax.axis_index("section")
+        chip = lax.axis_index("dp")
+        z, y, x = chip // 4, (chip // 2) % 2, chip % 2
+        other = 1 - core
+
+        def place(pz, py, px):
+            return pz * 4 + py * 2 + px
+
+        mate = (other, chip)
+        near_x = (core, place(z, y, 1 - x))
+        near_y = (core, place(z, 1 - y, x))
+        along_z = [(core, place((z + k) % 4, y, x)) for k in range(1, 4)]
+
+        def remote(src, dst, n, k, target):
+            return pltpu.make_async_remote_copy(
+                src_ref=src,
+                dst_ref=dst,
+                send_sem=sem_send.at[n, k],
+                recv_sem=sem_recv.at[n, k],
+                device_id=target,
+                device_id_type=pl.DeviceIdType.MESH,
+            )
+
+        def own_shard(n):
+            layer, which, cols, part = units[n]
+            src = weight_in[which].at[every, part, cols]
+            return src, view(n, z, y, x, every)
+
+        def z_copy(n, k):
+            spot = view(n, z, y, x, core)
+            return remote(spot, spot, n, k, along_z[k - 1])
+
+        def plane_copy(n, k, x_first):
+            if k == 4:
+                spot = view(n, every, y, x, core)
+                return remote(spot, spot, n, 4, near_x if x_first else near_y)
+            spot = view(n, every, y, every, core) if x_first else view(n, every, every, x, core)
+            return remote(spot, spot, n, 5, near_y if x_first else near_x)
+
+        def mate_copy(n, k, x_first, half):
+            if k < 9:
+                from_z = (z + 4 - (k - 5)) % 4
+                spot = view(n, from_z, y, x, half)
+            elif k == 9:
+                spot = view(n, every, y, 1 - x, half) if x_first else view(n, every, 1 - y, x, half)
+            else:
+                spot = view(n, every, 1 - y, every, half) if x_first else view(n, every, every, 1 - x, half)
+            return remote(spot, spot, n, k, mate)
+
+        def by_route(n, act):
+            for side in range(2):
+                @pl.when(core == side)
+                def _(side=side):
+                    act((side + n) % 2 == 0)
+
+        def share_own(n):
+            src, dst = own_shard(n)
+
+            @pl.when(core == units[n][0])
+            def _():
+                pltpu.make_async_copy(src, dst, sem_own.at[n]).start()
+                remote(src, dst, n, 0, mate).start()
+
+        def start_z(n):
+            src, dst = own_shard(n)
+
+            @pl.when(core == units[n][0])
+            def _():
+                pltpu.make_async_copy(src, dst, sem_own.at[n]).wait()
+
+            @pl.when(core != units[n][0])
+            def _():
+                remote(src, dst, n, 0, mate).wait_recv()
+
+            for k in range(1, 4):
+                z_copy(n, k).start()
+
+        def first_hop(n):
+            for k in range(1, 4):
+                z_copy(n, k).wait_recv()
+
+            def act(x_first):
+                plane_copy(n, 4, x_first).start()
+                for k in range(6, 9):
+                    mate_copy(n, k, x_first, core).start()
+
+            by_route(n, act)
+
+        def second_hop(n):
+            def act(x_first):
+                plane_copy(n, 4, x_first).wait_recv()
+                plane_copy(n, 5, x_first).start()
+                mate_copy(n, 9, x_first, core).start()
+
+            by_route(n, act)
+
+        def last_share(n):
+            def act(x_first):
+                plane_copy(n, 5, x_first).wait_recv()
+                mate_copy(n, 10, x_first, core).start()
+
+            by_route(n, act)
+
+        def complete(n):
+            def act(x_first):
+                for k in range(6, 11):
+                    mate_copy(n, k, not x_first, other).wait_recv()
+
+            by_route(n, act)
+
+        def drain(n):
+            src, dst = own_shard(n)
+
+            @pl.when(core == units[n][0])
+            def _():
+                remote(src, dst, n, 0, mate).wait_send()
+
+            for k in range(1, 4):
+                z_copy(n, k).wait_send()
+
+            def act(x_first):
+                for k in (4, 5):
+                    plane_copy(n, k, x_first).wait_send()
+                for k in range(6, 11):
+                    mate_copy(n, k, x_first, core).wait_send()
+
+            by_route(n, act)
+
+        def tick(t):
+            if 0 <= t - 4 < len(units):
+                last_share(t - 4)
+            if 0 <= t - 2 < len(units):
+                second_hop(t - 2)
+            if 0 <= t < len(units):
+                first_hop(t)
+            ahead = t + 4
+            if ahead < len(units) and ahead >= lead_units:
+                start_z(ahead)
+
+        lead_units = 6
+        ticks_at = {
+            (0, 0, "qkv"): [7], (0, 0, "quad0"): [8], (0, 0, "quad1"): [9],
+            (0, 1, "qkv"): [10], (0, 1, "quad0"): [11], (0, 1, "quad1"): [12],
+            (0, 0, "ffn"): [13], (0, 1, "ffn"): [14],
+            (1, 0, "qkv"): [15], (1, 0, "quad0"): [16], (1, 0, "quad1"): [17],
+        }
+    else:
+        ticks_at = {}
+
+        def weight_copy(n):
+            layer, which, cols, part = units[n]
+            src = weight_in[which].at[layer, every, every, every, every, part, cols]
+            return pltpu.make_async_copy(src, view(n, every, every, every, every), sem_own.at[n])
+
+        def complete(n):
+            weight_copy(n).wait()
+
+    def after(layer, s, point):
+        for (at_layer, at_s, at_point), ticks in ticks_at.items():
+            if at_point == point:
+                @pl.when((layer == at_layer) & (s == at_s))
+                def _(ticks=ticks):
+                    for t in ticks:
+                        tick(t)
+
+    def need(layer, picks):
+        for at_layer in range(2):
+            @pl.when(layer == at_layer)
+            def _(at_layer=at_layer):
+                for n in picks:
+                    if units[n][0] == at_layer:
+                        complete(n)
+
+    def mat(which, slot, cols=every, planes=None):
+        if planes is None:
+            value = weight_buf[which][slot, :, :, :, :, :, cols]
+        else:
+            value = weight_buf[which][slot, planes, :, :, :, :, cols]
+        deep = 1
+        for size in value.shape[:-1]:
+            deep *= size
+        return value.reshape(deep, value.shape[-1])
+
+    def put_mat(which, slot, value, cols=every, planes=None):
+        buf = weight_buf[which]
+        shape = buf.shape[1:-1]
+        if planes is None:
+            buf[slot, :, :, :, :, :, cols] = value.reshape(*shape, value.shape[-1])
+        else:
+            buf[slot, planes] = value.reshape(1, *shape[1:], value.shape[-1])
+
+    def qkv_cols(k):
+        return slice(lanes + k * width, lanes + (k + 1) * width)
 
     def seg_rows(s):
         return pl.ds(pl.multiple_of(s * rows, rows), rows)
@@ -111,6 +319,21 @@
     du_copy = pltpu.make_async_copy(dy, du_ref, sem_io.at[3])
     for copy in loads:
         copy.start()
+    if routed:
+        barrier = pltpu.get_barrier_semaphore()
+        peers = [mate, near_x, near_y, *along_z]
+        for peer in peers:
+            pl.semaphore_signal(barrier, inc=1, device_id=peer, device_id_type=pl.DeviceIdType.MESH)
+        pl.semaphore_wait(barrier, len(peers))
+        for n in range(len(units)):
+            share_own(n)
+        for n in range(lead_units):
+            start_z(n)
+        for t in range(7):
+            tick(t)
+    else:
+        for n in range(len(units)):
+            weight_copy(n).start()
     stat_ref[...] = jnp.zeros_like(stat_ref)
     dga_ref[...] = jnp.zeros_like(dga_ref)
     dgf_ref[...] = jnp.zeros_like(dgf_ref)
@@ -135,13 +358,13 @@
             for side in range(2):
                 h = 2 * p + side
                 own, marks = lane_marks(head_size, side)
-                bias = jnp.broadcast_to(bias_ref[layer, :, h : h + 1], (slots, lanes))
+                bias = bias_rows[layer, h]
                 hi = bias.astype(bf16).astype(f32)
                 aux = jnp.concatenate([hi * marks[1] + (bias - hi) * marks[2], jnp.zeros((tok_rows, lanes), f32)], axis=0)
                 aux = aux + mask * marks[0]
-                every = marks[0] + marks[1] + marks[2]
+                extra = marks[0] + marks[1] + marks[2]
                 ka = kp * own.astype(bf16) + aux.astype(bf16)
-                qa = qp * (1.0 - every).astype(bf16) + every.astype(bf16)
+                qa = qp * (1.0 - extra).astype(bf16) + extra.astype(bf16)
                 scores = nt(qa, ka)
                 top = jnp.max(scores, axis=1, keepdims=True)
                 weights = jnp.exp2(scores - top).astype(bf16)
@@ -154,8 +377,19 @@
             inv = 1.0 / sums
             ilbuf[at, cols] = inv.astype(ilbuf.dtype)
             obuf[at, cols] = (raw * inv).astype(bf16)
-
-    def forward_seg(layer, s):
+            if p % 2 == 1:
+                after(layer, s, "quad" + str(p // 2))
+
+    def unpack_small(layer):
+        ext[...] = mat(0, layer, slice(0, lanes)).astype(f32)
+        turned = ext[...].T
+        for k in range(2):
+            gains[layer, k] = turned[k : k + 1, :]
+        for h in range(heads):
+            column = ext[pl.ds(h, slots, stride=heads), :][:, 2:3]
+            bias_rows[layer, h] = jnp.broadcast_to(column * log2_e, (slots, lanes))
+
+    def forward_attn(layer, s):
         at = seg_rows(s)
 
         @pl.when(layer == 1)
@@ -163,20 +397,17 @@
             for copy in spill_copies(s, False):
                 copy.wait()
 
-        @pl.when(s == 0)
-        def _():
-            weight_copies(layer, (0,))[0].wait()
-
         valid = valid_col(s)
         x = ub[layer, at, :].astype(f32)
         squares = jnp.sum(x * x, axis=1, keepdims=True)
         add_stat(layer, 0, squares, valid)
-        n1 = (x * lax.rsqrt(squares / width + norm_eps) * gain_a[layer]).astype(bf16)
+        n1 = (x * lax.rsqrt(squares / width + norm_eps) * gains[layer, 0]).astype(bf16)
         for k in range(3):
-            part = mm(n1, wq[layer, :, k * width : (k + 1) * width])
+            part = mm(n1, mat(0, layer, qkv_cols(k)))
             if k == 0:
                 part = part * (score_scale * log2_e)
             qkv[at, k * width : (k + 1) * width] = part.astype(bf16)
+        after(layer, s, "qkv")
         forward_attention(layer, s)
 
         @pl.when(layer == 0)
@@ -184,25 +415,23 @@
             for copy in spill_copies(s, False, range(4)):
                 copy.start()
 
-        @pl.when(s == 0)
-        def _():
-            for copy in weight_copies(layer, (1, 2, 3)):
-                copy.wait()
-
-        z = mm(obuf[at, :], wo[layer])
+    def forward_ffn(layer, s):
+        at = seg_rows(s)
+        valid = valid_col(s)
+        z = mm(obuf[at, :], mat(1, layer))
         add_stat(layer, 1, jnp.sum(z * z, axis=1, keepdims=True), valid)
         h = ub[layer, at, :].astype(f32) + z
         hbuf[layer, at, :] = h.astype(bf16)
         dn[at, :] = h
-        n2 = (h * lax.rsqrt(jnp.mean(h * h, axis=1, keepdims=True) + norm_eps) * gain_f[layer]).astype(bf16)
+        n2 = (h * lax.rsqrt(jnp.mean(h * h, axis=1, keepdims=True) + norm_eps) * gains[layer, 1]).astype(bf16)
         n2buf[at, :] = n2
         out = None
         for c in range(ff // chunk):
             cols = slice(c * chunk, (c + 1) * chunk)
-            before = mm(n2buf[at, :], wu[layer, :, cols])
+            before = mm(n2buf[at, :], mat(2, layer, cols))
             pre[at, cols] = before.astype(bf16)
             gate = 0.5 + 0.5 * jnp.tanh(before * (gelu_c + (gelu_c * gelu_k) * (before * before)))
-            part = mm((before * gate).astype(bf16), wd[layer, cols, :])
+            part = mm((before * gate).astype(bf16), mat(3, layer, planes=slice(c, c + 1)))
             out = part if out is None else out + part
         add_stat(layer, 2, jnp.sum(out * out, axis=1, keepdims=True), valid)
         ub[layer + 1, at, :] = (dn[at, :] + out).astype(bf16)
@@ -211,10 +440,26 @@
         def _():
             spill_copies(s, False, (4,))[0].start()
 
-    @pl.loop(0, 2 * segs)
-    def _(step):
-        forward_seg(step // segs, step % segs)
-
+        after(layer, s, "ffn")
+
+    @pl.loop(0, 2)
+    def _(layer):
+        need(layer, first_units)
+        unpack_small(layer)
+
+        @pl.loop(0, segs)
+        def _(s):
+            forward_attn(layer, s)
+
+        need(layer, later_units)
+
+        @pl.loop(0, segs)
+        def _(s):
+            forward_ffn(layer, s)
+
+    if routed:
+        for n in range(len(units)):
+            drain(n)
     y_copy.start()
 
     def norm_back(x, gain, grad):
@@ -231,14 +476,15 @@
         def _(s):
             at = seg_rows(s)
             h = hbuf[layer, at, :].astype(f32)
-            n2buf[at, :] = (h * lax.rsqrt(jnp.mean(h * h, axis=1, keepdims=True) + norm_eps) * gain_f[layer]).astype(bf16)
+            n2buf[at, :] = (h * lax.rsqrt(jnp.mean(h * h, axis=1, keepdims=True) + norm_eps) * gains[layer, 1]).astype(bf16)
 
         dn[...] = jnp.zeros_like(dn)
 
         @pl.loop(0, ff // chunk)
         def _(c):
             cols = pl.ds(pl.multiple_of(c * chunk, chunk), chunk)
-            d_act = nt(dy[...], wd[layer, cols, :])
+            planes = pl.ds(c, 1)
+            d_act = nt(dy[...], mat(3, layer, planes=planes))
             x = pre[:, cols].astype(f32)
             sq = x * x
             gate = 0.5 + 0.5 * jnp.tanh(x * (gelu_c + (gelu_c * gelu_k) * sq))
@@ -246,19 +492,19 @@
             slope = gate + act * (1.0 - gate) * (2.0 * gelu_c + (6.0 * gelu_c * gelu_k) * sq)
             d_pre = (d_act * slope).astype(bf16)
             pre[:, cols] = d_pre
-            wd[slot, cols, :] = tn(act.astype(bf16), dy[...]).astype(bf16)
-            wu[slot, :, cols] = tn(n2buf[...], d_pre).astype(bf16)
-            dn[...] += nt(d_pre, wu[layer, :, cols])
+            put_mat(3, slot, tn(act.astype(bf16), dy[...]).astype(bf16), planes=planes)
+            put_mat(2, slot, tn(n2buf[...], d_pre).astype(bf16), cols)
+            dn[...] += nt(d_pre, mat(2, layer, cols))
 
     def backward_middle(layer, s):
         at = seg_rows(s)
-        dh, dgain = norm_back(hbuf[layer, at, :].astype(f32), gain_f[layer], dn[at, :])
+        dh, dgain = norm_back(hbuf[layer, at, :].astype(f32), gains[layer, 1], dn[at, :])
         dgf_ref[layer] += dgain
         dh = dh + dy[at, :].astype(f32)
         dn[at, :] = dh
         dz = dh.astype(bf16)
         dy[at, :] = dz
-        do = nt(dz, wo[layer]) * ilbuf[at, :].astype(f32)
+        do = nt(dz, mat(1, layer)) * ilbuf[at, :].astype(f32)
         prod = do.astype(bf16).astype(f32) * obuf[at, :].astype(f32)
         for p in range(pairs):
             cols = slice(p * lanes, (p + 1) * lanes)
@@ -301,10 +547,10 @@
     def backward_input(layer, s):
         at = seg_rows(s)
         x = ub[layer, at, :].astype(f32)
-        du, dgain = norm_back(x, gain_a[layer], nt(qkv[at, :], wq[layer]))
+        du, dgain = norm_back(x, gains[layer, 0], nt(qkv[at, :], mat(0, layer, slice(lanes, lanes + 3 * width))))
         dga_ref[layer] += dgain
         dy[at, :] = (du + dn[at, :]).astype(bf16)
-        n2buf[at, :] = (x * lax.rsqrt(jnp.mean(x * x, axis=1, keepdims=True) + norm_eps) * gain_a[layer]).astype(bf16)
+        n2buf[at, :] = (x * lax.rsqrt(jnp.mean(x * x, axis=1, keepdims=True) + norm_eps) * gains[layer, 0]).astype(bf16)
 
     def grad_copies(layer, picks=range(4)):
         slot = layer + 1
@@ -331,7 +577,7 @@
         def _(s):
             backward_middle(layer, s)
 
-        wo[slot] = tn(obuf[...], dy[...]).astype(bf16)
+        put_mat(1, slot, tn(obuf[...], dy[...]).astype(bf16))
         for copy in grad_copies(layer, (1, 2, 3)):
             copy.start()
 
@@ -360,7 +606,7 @@
 
         for k in range(3):
             part = slice(k * width, (k + 1) * width)
-            wq[slot, :, part] = tn(n2buf[...], qkv[:, part]).astype(bf16)
+            put_mat(0, slot, tn(n2buf[...], qkv[:, part]).astype(bf16), qkv_cols(k))
         grad_copies(layer, (0,))[0].start()
 
         @pl.when(layer == 1)
@@ -376,16 +622,23 @@
     y_copy.wait()
 
 
-def run_layers(doc_len, u0, dout, gains, bias, weights, heads, slots, segs):
+def run_layers(doc_len, u0, dout, weights, routed, heads, slots, segs):
     all_rows, width = u0.shape
     rows = all_rows // segs
-    ff = weights[2].shape[2]
+    ff = weights[2].shape[-1]
     dims = (segs, rows, width, ff, slots, heads)
     vmem = pl.BlockSpec(memory_space=pltpu.VMEM)
     smem = pl.BlockSpec(memory_space=pltpu.SMEM)
     hbm = pl.BlockSpec(memory_space=pl.ANY)
     shape = jax.ShapeDtypeStruct
     wide = (all_rows, width)
+    grid = (4, 2, 2, 2)
+    mats = [
+        (*grid, width // 32, lanes + 3 * width),
+        (*grid, width // 32, width),
+        (*grid, width // 32, ff),
+        (*grid, ff // 32, width),
+    ]
     spills = [
         shape((all_rows, 3 * width), bf16),
         shape((segs, heads, rows, rows), bf16),
@@ -393,23 +646,17 @@
         shape(wide, bf16),
         shape((all_rows, ff), bf16),
     ]
-    out_shape = [
-        shape(wide, bf16),
-        shape(wide, bf16),
-        shape((2, width, 3 * width), bf16),
-        shape((2, width, width), bf16),
-        shape((2, width, ff), bf16),
-        shape((2, ff, width), bf16),
+    out_shape = [shape(wide, bf16)] * 2
+    out_shape += [shape((2, *mat), bf16) for mat in mats]
+    out_shape += [
         shape((2, 1, width), f32),
         shape((2, 1, width), f32),
         shape((2, heads, lanes), f32),
         shape((2, 8, lanes), f32),
     ] + spills
-    scratch = [
-        pltpu.VMEM((3, width, 3 * width), bf16),
-        pltpu.VMEM((3, width, width), bf16),
-        pltpu.VMEM((3, width, ff), bf16),
-        pltpu.VMEM((3, ff, width), bf16),
+    unit_count = 16
+    scratch = [pltpu.VMEM((3, *mat), bf16) for mat in mats]
+    scratch += [
         pltpu.VMEM((3, *wide), bf16),
         pltpu.VMEM(wide, bf16),
         pltpu.VMEM((all_rows, 3 * width), bf16),
@@ -421,20 +668,28 @@
         pltpu.VMEM((2, *wide), bf16),
         pltpu.VMEM(wide, f32),
         pltpu.VMEM(wide, bf16),
-        pltpu.SemaphoreType.DMA((2, 4)),
+        pltpu.VMEM((2, 2, 1, width), f32),
+        pltpu.VMEM((2, heads, slots, lanes), f32),
+        pltpu.VMEM((width, lanes), f32),
         pltpu.SemaphoreType.DMA((segs, 5)),
         pltpu.SemaphoreType.DMA((segs, 5)),
         pltpu.SemaphoreType.DMA((2, 4)),
         pltpu.SemaphoreType.DMA((4,)),
+        pltpu.SemaphoreType.DMA((unit_count,)),
+        pltpu.SemaphoreType.DMA((unit_count, 11)),
+        pltpu.SemaphoreType.DMA((unit_count, 11)),
     ]
+    params = dict(vmem_limit_bytes=63 * 2**20)
+    if routed:
+        params.update(collective_id=0, has_side_effects=True)
     return pl.pallas_call(
-        partial(fused_layers, dims),
+        partial(fused_layers, dims, routed),
         out_shape=out_shape,
-        in_specs=[smem] + [hbm] * 2 + [vmem] * 3 + [hbm] * 4,
+        in_specs=[smem] + [hbm] * 6,
         out_specs=[hbm] * 6 + [vmem] * 4 + [hbm] * 5,
         scratch_shapes=scratch,
-        compiler_params=pltpu.CompilerParams(vmem_limit_bytes=63 * 2**20),
-    )(doc_len, u0, dout, *gains, bias, *weights)[:10]
+        compiler_params=pltpu.CompilerParams(**params),
+    )(doc_len, u0, dout, *weights)[:10]
 
 
 def swap(block):
@@ -483,18 +738,24 @@
     u0 = jnp.concatenate([full[1], full[0]], axis=1).reshape(segs * rows, width)
     dout = jnp.concatenate([full[3], full[2]], axis=1).reshape(segs * rows, width)
 
+    heads = forget_bias.shape[1] * lax.axis_size("dp") // slots
+    small = jnp.stack([gain_attn, gain_ffn, forget_bias], axis=2)
+    small = jnp.pad(small, ((0, 0), (0, 0), (0, lanes - 3)))
+    pieces = (jnp.concatenate([small, w_qkv], axis=2), w_out, w_up, w_down)
+    routed = lax.axis_size("dp") == 16 and width == 512
+
     def gather(piece):
-        return lax.all_gather(piece, ("section", "dp"), axis=1, tiled=True).reshape(2, -1, *piece.shape[2:])
-
-    weights = tuple(gather(piece) for piece in (w_qkv, w_out, w_up, w_down))
-    gains = [gather(piece).astype(f32)[:, None, :] for piece in (gain_attn, gain_ffn)]
-    bias_flat = gather(forget_bias).astype(f32)
-    heads = bias_flat.shape[1] // slots
-    bias = jnp.pad(bias_flat.reshape(2, slots, heads) * log2_e, ((0, 0), (0, 0), (0, lanes - heads)))
+        whole = lax.all_gather(piece, ("section", "dp"), axis=1, tiled=True)
+        return whole.reshape(2, 4, 2, 2, 2, -1, piece.shape[2])
+
+    if routed:
+        weights = [piece.reshape(2, -1, piece.shape[2]) for piece in pieces]
+    else:
+        weights = [gather(piece) for piece in pieces]
     per_doc = micro // lengths.shape[0]
     own_len = lax.dynamic_slice_in_dim(lengths, section * segs // per_doc, 1, 0)
     y, du, gq, go, gu, gd, dga, dgf, dbias, stats = run_layers(
-        own_len, u0, dout, gains, bias, weights, heads, slots, segs
+        own_len, u0, dout, weights, routed, heads, slots, segs
     )
 
     def scatter(grad):
@@ -503,6 +764,9 @@
         chip = (mine.astype(f32) + swap(other).astype(f32)).astype(grad.dtype)
         return lax.psum_scatter(chip, "dp", scatter_dimension=1, tiled=True).astype(f32)
 
+    gq, go, gu, gd = (
+        grad.reshape(2, -1, grad.shape[-1]) for grad in (gq[..., lanes:], go, gu, gd)
+    )
     grad_bias = jnp.swapaxes(dbias[:, :, :slots], 1, 2).reshape(2, slots * heads)
     shares = tuple(scatter(grad) for grad in (gq, go, gu, gd, dga[:, 0], dgf[:, 0], grad_bias))
     token_count = jnp.sum(own_len).astype(f32)

time: 985 us -> 791 us (0.80)
  waiting for transfers between devices: 709 us -> 514 us
  Pallas kernels: 123 us -> 165 us
  blocking collectives: 81.3 us -> 41.3 us
    all_gather x4 -> x0, waiting for transfers between devices: 192 us -> none  [gather(): lax.all_gather(piece, ('section', 'dp'), axis=1, tiled=True)]
    unnamed x1 -> x0, blocking collectives: 42.1 us -> none
    pallas_call x1, Pallas kernels: 123 us -> 165 us  [run_layers(): pl.pallas_call(partial(fused_layers, dims, routed), out_shape=out_shape,...]
    unnamed x14 -> x10, waiting for transfers between devices: 156 us -> 153 us
  transfers between devices with their start and end apart: 24 -> 20, of which waited for: 13 -> 10; matrix products, arithmetic and copies ran while one was open for 5% -> 5% of each run, Pallas kernels for 0% -> 0%
where the time goes in v2:
time: 791 us; the launch traced here: 790 us
  waiting for transfers between devices  514 us (65%)
  Pallas kernels  165 us (21%)
  blocking collectives  41.3 us (5%)
  other arithmetic  25.7 us (3%)
  local copies, waits for them, and re-layouts  24.1 us (3%)
  between operations  15.8 us (2%)
    reduce_scatter x4, waiting for transfers between devices, scatter(): lax.psum_scatter(chip, 'dp', scatter_dimension=1, tiled=True).astype(f32)  353 us
    pallas_call x1, Pallas kernels, run_layers(): pl.pallas_call(partial(fused_layers, dims, routed), out_shape=out_shape,...  165 us
    unnamed x10, waiting for transfers between devices  153 us
    psum x1, blocking collectives, body(): totals = lax.psum(sums, ('section', 'dp'))  41.3 us
  transfers between devices with their start and end apart: 20, of which 10 were waited for; matrix products, arithmetic and copies ran while one was open for 5% of the time, Pallas kernels for 0%

profile of v2, /device:TPU:0, one launch (start us, length us, event | category | flops | bytes accessed | tf_op | source)
XLA Modules:
  0.0 789.5 jit_solution(5424971688584516133)
XLA Ops:
  9.1 1.5 constant_dynamic-slice_fusion.11
  18.7 164.8 %shard_map.211 = (bf16[1152,512]{1,0:T(8,128)(2,1)}, bf16[1152,512]{1,0:T(8,128)(2,1)}, bf16[2,4,2,2,2,16,1664]{6,5,4,3,2,1,0:T(8,128)(2,1)}, bf16[2,4,2,2,2,16,...) custom-call(s32[1]{0:T(128)} %dynamic_slice.94.refs_0_, ...), custom_call_target="tpu_custom_call" | custom-call | tf_op jit(solution)/shard_map/pallas_call | solution.py:685
  185.6 2.1 slice.47
  193.5 2.2 add_convert_fusion.3
  195.8 3.0 add_convert_fusion.2
  198.8 1.9 constant_dynamic-slice_fusion.6
  201.0 3.9 collective-permute-done.9
  204.9 1.9 add_convert_fusion
  207.0 1.9 constant_dynamic-slice_fusion.7
  209.2 3.9 collective-permute-done.8
  213.1 2.1 add_convert_fusion.1
  218.8 41.3 %psum.7 = f32[7]{0:T(128)S(1)} all-reduce(f32[7]{0:T(128)S(1)} %pad_maximum_fusion.7), channel_id=1, replica_groups=mesh['section'=2,'dp'=16] {'section','dp'}, use_global_device_ids=true, to_apply=%region_7.8 | all-reduce | flops 7 | bytes 56 | tf_op jit(solution)/shard_map/psum | solution.py:774
  262.7 5.3 reduce-scatter.26.cloned.1.call-done
  269.2 74.1 %reduce-scatter.24.cloned.1.call-done = f32[32,1]{1,0:T(8,128)} async-done(((f32[512,1]{1,0:T(8,128)}), f32[32,1]{1,0:T(8,128)}) %reduce-scatter.24.cloned.1.call-update) | async-done | bytes 144
  344.7 73.9 %reduce-scatter.22.cloned.1.call-done = f32[32,1]{1,0:T(8,128)} async-done(((f32[512,1]{1,0:T(8,128)}), f32[32,1]{1,0:T(8,128)}) %reduce-scatter.22.cloned.1.call-update) | async-done | bytes 144
  422.0 1.5 pad_maximum_fusion.2
  423.5 70.2 %reduce-scatter.16.cloned.1.call-done = bf16[1,32,512]{2,1,0:T(8,128)(2,1)} async-done(((bf16[1,512,512]{2,1,0:T(8,128)(2,1)}), bf16[1,32,512]{2,1,0:T(8,128)(2,1)}) %reduce-scatter.16.cloned.1.call-update) | async-done | bytes 32784 | tf_op jit(solution)/shard_map/reduce_scatter | solution.py:765
  493.7 1.4 convert_element_type.61
  495.1 124.2 %reduce-scatter.14.cloned.1.call-done = bf16[1,32,1536]{2,1,0:T(8,128)(2,1)} async-done(((bf16[1,512,1536]{2,1,0:T(8,128)(2,1)}), bf16[1,32,1536]{2,1,0:T(8,128)(2,1)}) %reduce-scatter.14.cloned.1.call-update) | async-done | bytes 98320 | tf_op jit(solution)/shard_map/reduce_scatter | solution.py:765
  619.3 1.6 convert_element_type.57
  620.9 80.0 %reduce-scatter.20.cloned.1.call-done = bf16[1,128,512]{2,1,0:T(8,128)(2,1)} async-done(((bf16[1,2048,512]{2,1,0:T(8,128)(2,1)}), bf16[1,128,512]{2,1,0:T(8,128)(2,1)}) %reduce-scatter.20.cloned.1.call-update) | async-done | bytes 131088 | tf_op jit(solution)/shard_map/reduce_scatter | solution.py:765
  700.9 1.6 convert_element_type.69
  702.6 78.5 %reduce-scatter.18.cloned.1.call-done = bf16[1,32,2048]{2,1,0:T(8,128)(2,1)} async-done(((bf16[1,512,2048]{2,1,0:T(8,128)(2,1)}), bf16[1,32,2048]{2,1,0:T(8,128)(2,1)}) %reduce-scatter.18.cloned.1.call-update) | async-done | bytes 131088 | tf_op jit(solution)/shard_map/reduce_scatter | solution.py:765
  781.1 1.6 convert_element_type.65
  (113 shorter events, 29.3 us)
Async XLA Ops:
  7.2 8.8 %copy-start.5 = (bf16[4,256,512]{2,1,0:T(8,128)(2,1)S(1)}, bf16[4,256,512]{2,1,0:T(8,128)(2,1)}, u32[]{:S(2)}) copy-start(bf16[4,256,512]{2,1,0:T(8,128)(2,1)} %param.22) | copy-start | bytes 3145732
  7.2 7.1 copy-start.7
  7.3 6.4 copy-start.16
  7.3 260.7 %reduce-scatter.26.cloned.1.call-start = ((), (), s32[]{:S(2)}) async-start(), calls=%async_computation.13 | async-start | bytes 278528
  8.6 7.5 collective-permute-start.3
  10.5 3.7 collective-permute-start.2
  11.7 5.5 collective-permute-start.1
  12.8 2.3 collective-permute-start
  184.4 6.1 collective-permute-start.12
  185.1 6.3 collective-permute-start.11
  189.0 6.8 collective-permute-start.6
  189.0 3.3 collective-permute-start.10
  190.4 3.2 collective-permute-start.7
  191.3 152.0 %reduce-scatter.24.cloned.1.call-start = ((), (), s32[]{:S(2)}) async-start(), calls=%async_computation.12 | async-start | bytes 278528
  192.3 226.3 %reduce-scatter.22.cloned.1.call-start = ((), (), s32[]{:S(2)}) async-start(), calls=%async_computation.11 | async-start | bytes 278528
  193.3 300.5 %reduce-scatter.16.cloned.1.call-start = ((), (), s32[]{:S(2)}) async-start(), calls=%async_computation.8 | async-start | bytes 557056 | tf_op jit(solution)/shard_map/reduce_scatter | solution.py:765
  195.7 423.6 %reduce-scatter.14.cloned.1.call-start = ((), (), s32[]{:S(2)}) async-start(), calls=%async_computation.7 | async-start | bytes 1671168 | tf_op jit(solution)/shard_map/reduce_scatter | solution.py:765
  198.8 502.2 %reduce-scatter.20.cloned.1.call-start = ((), (), s32[]{:S(2)}) async-start(), calls=%async_computation.10 | async-start | bytes 2228224 | tf_op jit(solution)/shard_map/reduce_scatter | solution.py:765
  200.7 4.2 collective-permute-start.9
  206.9 574.2 %reduce-scatter.18.cloned.1.call-start = ((), (), s32[]{:S(2)}) async-start(), calls=%async_computation.9 | async-start | bytes 2228224 | tf_op jit(solution)/shard_map/reduce_scatter | solution.py:765
  207.0 6.1 copy-start.2
  208.9 4.2 collective-permute-start.8
  217.7 203.0 %collective-permute-start.4 = (bf16[2,2,256,512]{3,2,1,0:T(8,128)(2,1)}, bf16[2,2,256,512]{3,2,1,0:T(8,128)(2,1)}, u32[]{:S(2)}, u32[]{:S(2)}) collective-permute-start(bf16[2,2,256,512]{3,2,1,0:T(8,128)(2,1)} %get-tuple-element.35), channel_id=1, source_target_pairs={{0,16},{16,0},{1,17},{17,1},{2,18},{18,2},{3,19},{19,3},{4,20},{20... | collective-permute-start | bytes 3145736 | tf_op jit(solution)/shard_map/ppermute | solution.py:696
  261.4 158.5 %collective-permute-start.5 = (bf16[2,2,32,512]{3,2,1,0:T(8,128)(2,1)}, bf16[2,2,32,512]{3,2,1,0:T(8,128)(2,1)S(1)}, u32[]{:S(2)}, u32[]{:S(2)}) collective-permute-start(bf16[2,2,32,512]{3,2,1,0:T(8,128)(2,1)} %get-tuple-element.33), channel_id=1, source_target_pairs={{0,16},{16,0},{1,17},{17,1},{2,18},{18,2},{3,19},{19,3},{4,20},{20... | collective-permute-start | bytes 393224 | tf_op jit(solution)/shard_map/ppermute | solution.py:696
  (13 other events, 47.7 us)
Sparse Core Ops, SparseCore 0:
  191.5 76.4 reduce-scatter.25
  270.8 72.4 reduce-scatter.23
  346.2 72.3 reduce-scatter.21
  420.8 72.9 reduce-scatter.15
  498.4 120.9 reduce-scatter.13
  621.5 79.4 reduce-scatter.19
  703.2 77.8 reduce-scatter.17

commit v3 on v2

--- a/solution.py
+++ b/solution.py
@@ -41,21 +41,33 @@
 
 def fused_layers(dims, routed, *refs):
     segs, rows, width, ff, slots, heads = dims
-    (
-        len_ref, u0_ref, dout_ref, wq_in, wo_in, wu_in, wd_in,
-        y_ref, du_ref, gq_out, go_out, gu_out, gd_out,
-        dga_ref, dgf_ref, dbias_ref, stat_ref,
-        qkv_hbm, e_hbm, o_hbm, il_hbm, pre_hbm,
-        wq, wo, wu, wd, ub, dy, qkv, ebuf, obuf, ilbuf, hbuf, pre, doa, dn, n2buf,
-        gains, bias_rows, ext, sem_spill, sem_back, sem_g, sem_io,
-        sem_own, sem_send, sem_recv,
-    ) = refs
+    refs = list(refs)
+
+    def take(count):
+        picked = refs[:count]
+        del refs[:count]
+        return picked
+
+    (len_ref,) = take(1)
+    rows_in = take(4 if routed else 2)
+    weight_in = take(4)
+    rows_out = take(4 if routed else 2)
+    grads_out = take(4)
+    (stat_out,) = take(1)
+    spill_hbm = take(5)
+    lands = [take(4) for _ in range(4)] if routed else None
+    weight_buf = take(4)
+    ub, dy, qkv, ebuf, obuf, ilbuf, hbuf, pre, doa, dn = take(10)
+    gains, bias_rows, ext, gain_sums, dbias, stat_ref = take(6)
+    sem_spill, sem_back, sem_g, sem_io, sem_own, sem_send, sem_recv = take(7)
+    if routed:
+        stage, fin = take(4), take(4)
+        stat_sum, stat_land = take(2)
+        sem_stage, rs_send, rs_recv, io_send, io_recv, stat_send, stat_recv = take(7)
     head_size = width // heads
     pairs = width // lanes
     tok_rows = rows - slots
     doc_len = len_ref[0]
-    weight_in = (wq_in, wo_in, wu_in, wd_in)
-    weight_buf = (wq, wo, wu, wd)
     every = slice(None)
 
     def units_of(layer):
@@ -280,13 +292,11 @@
 
     def spill_copies(s, back, picks=range(5)):
         at = seg_rows(s)
-        pairs_of = (
-            (qkv.at[at], qkv_hbm.at[at]),
-            (ebuf.at[s], e_hbm.at[s]),
-            (obuf.at[at], o_hbm.at[at]),
-            (ilbuf.at[at], il_hbm.at[at]),
-            (pre.at[at], pre_hbm.at[at]),
-        )
+        kept = (qkv.at[at], ebuf.at[s], obuf.at[at], ilbuf.at[at], pre.at[at])
+        pairs_of = [
+            (vmem, hbm.at[s] if k == 1 else hbm.at[at])
+            for k, (vmem, hbm) in enumerate(zip(kept, spill_hbm))
+        ]
         if back:
             return [
                 pltpu.make_async_copy(hbm, vmem, sem_back.at[s, k])
@@ -311,12 +321,50 @@
             (row >= slots) & (s * tok_rows + row - slots >= doc_len), masked_score, 0.0
         ).astype(f32)
 
-    loads = [
-        pltpu.make_async_copy(u0_ref, ub.at[0], sem_io.at[0]),
-        pltpu.make_async_copy(dout_ref, dy, sem_io.at[1]),
-    ]
-    y_copy = pltpu.make_async_copy(ub.at[2], y_ref, sem_io.at[2])
-    du_copy = pltpu.make_async_copy(dy, du_ref, sem_io.at[3])
+    if routed:
+        half_tok, half_mem = tok_rows // 2, slots // 2
+
+        def io_copies(buf, tok_ref, mem_ref, first, outward):
+            local, away = [], []
+            k = first
+            for s in range(segs):
+                mine, theirs = core * segs + s, other * segs + s
+                for ref, base, size in ((tok_ref, slots, half_tok), (mem_ref, 0, half_mem)):
+                    def rows_of(half):
+                        return buf.at[pl.ds(pl.multiple_of(s * rows + base + half * size, 16), size)]
+
+                    if outward:
+                        local.append(pltpu.make_async_copy(rows_of(core), ref.at[mine], sem_io.at[k]))
+                        src, dst = rows_of(other), ref.at[mine]
+                    else:
+                        local.append(pltpu.make_async_copy(ref.at[mine], rows_of(core), sem_io.at[k]))
+                        src, dst = ref.at[theirs], rows_of(core)
+                    away.append(
+                        pltpu.make_async_remote_copy(
+                            src_ref=src,
+                            dst_ref=dst,
+                            send_sem=io_send.at[k],
+                            recv_sem=io_recv.at[k],
+                            device_id=mate,
+                            device_id_type=pl.DeviceIdType.MESH,
+                        )
+                    )
+                    k += 1
+            return local, away
+
+        loads, shares = io_copies(ub.at[0], rows_in[0], rows_in[1], 0, False)
+        more = io_copies(dy, rows_in[2], rows_in[3], 2 * segs, False)
+        loads, shares = loads + more[0], shares + more[1]
+        y_copies = io_copies(doa.at[1], rows_out[0], rows_out[1], 4 * segs, True)
+        du_copies = io_copies(dy, rows_out[2], rows_out[3], 6 * segs, True)
+    else:
+        loads = [
+            pltpu.make_async_copy(rows_in[0], ub.at[0], sem_io.at[0]),
+            pltpu.make_async_copy(rows_in[1], dy, sem_io.at[1]),
+        ]
+        shares = []
+        y_copies = [pltpu.make_async_copy(doa.at[1], rows_out[0], sem_io.at[2])], []
+        du_copies = [pltpu.make_async_copy(dy, rows_out[1], sem_io.at[3])], []
     for copy in loads:
         copy.start()
     if routed:
@@ -327,6 +375,8 @@
         pl.semaphore_wait(barrier, len(peers))
         for n in range(len(units)):
             share_own(n)
+        for copy in shares:
+            copy.start()
         for n in range(lead_units):
             start_z(n)
         for t in range(7):
@@ -335,11 +385,10 @@
         for n in range(len(units)):
             weight_copy(n).start()
     stat_ref[...] = jnp.zeros_like(stat_ref)
-    dga_ref[...] = jnp.zeros_like(dga_ref)
-    dgf_ref[...] = jnp.zeros_like(dgf_ref)
-    dbias_ref[...] = jnp.zeros_like(dbias_ref)
 
     for copy in loads:
+        copy.wait()
+    for copy in shares:
         copy.wait()
 
     def add_stat(layer, k, row_sums, valid):
@@ -401,6 +450,7 @@
         x = ub[layer, at, :].astype(f32)
         squares = jnp.sum(x * x, axis=1, keepdims=True)
         add_stat(layer, 0, squares, valid)
+        add_stat(layer, 3, valid, valid)
         n1 = (x * lax.rsqrt(squares / width + norm_eps) * gains[layer, 0]).astype(bf16)
         for k in range(3):
             part = mm(n1, mat(0, layer, qkv_cols(k)))
@@ -423,18 +473,25 @@
         h = ub[layer, at, :].astype(f32) + z
         hbuf[layer, at, :] = h.astype(bf16)
         dn[at, :] = h
-        n2 = (h * lax.rsqrt(jnp.mean(h * h, axis=1, keepdims=True) + norm_eps) * gains[layer, 1]).astype(bf16)
-        n2buf[at, :] = n2
+        doa[0, at, :] = (h * lax.rsqrt(jnp.mean(h * h, axis=1, keepdims=True) + norm_eps) * gains[layer, 1]).astype(bf16)
         out = None
         for c in range(ff // chunk):
             cols = slice(c * chunk, (c + 1) * chunk)
-            before = mm(n2buf[at, :], mat(2, layer, cols))
+            before = mm(doa[0, at, :], mat(2, layer, cols))
             pre[at, cols] = before.astype(bf16)
             gate = 0.5 + 0.5 * jnp.tanh(before * (gelu_c + (gelu_c * gelu_k) * (before * before)))
             part = mm((before * gate).astype(bf16), mat(3, layer, planes=slice(c, c + 1)))
             out = part if out is None else out + part
         add_stat(layer, 2, jnp.sum(out * out, axis=1, keepdims=True), valid)
-        ub[layer + 1, at, :] = (dn[at, :] + out).astype(bf16)
+        result = (dn[at, :] + out).astype(bf16)
+
+        @pl.when(layer == 0)
+        def _():
+            ub[1, at, :] = result
+
+        @pl.when(layer == 1)
+        def _():
+            doa[1, at, :] = result
 
         @pl.when(layer == 0)
         def _():
@@ -460,14 +517,262 @@
     if routed:
         for n in range(len(units)):
             drain(n)
-    y_copy.start()
+    for copies in y_copies:
+        for copy in copies:
+            copy.start()
+
+    if routed:
+        def rs_copy(src, dst, layer, u, k, target):
+            return pltpu.make_async_remote_copy(
+                src_ref=src,
+                dst_ref=dst,
+                send_sem=rs_send.at[layer, u, k],
+                recv_sem=rs_recv.at[layer, u, k],
+                device_id=target,
+                device_id_type=pl.DeviceIdType.MESH,
+            )
+
+        def part(layer, u, pz, py, px, c):
+            return weight_buf[u].at[layer + 1, pz, py, px, c]
+
+        def rs_sends(layer, u, step, y_first):
+            land = lands[u][step].at[layer] if step < 4 else None
+            if step == 0:
+                return [rs_copy(part(layer, u, every, every, every, other), land, layer, u, 0, mate)]
+            if step == 1:
+                spot = part(layer, u, every, 1 - y, every, core) if y_first else part(layer, u, every, every, 1 - x, core)
+                return [rs_copy(spot, land, layer, u, 1, near_y if y_first else near_x)]
+            if step == 2:
+                spot = part(layer, u, every, y, 1 - x, core) if y_first else part(layer, u, every, 1 - y, x, core)
+                return [rs_copy(spot, land, layer, u, 2, near_x if y_first else near_y)]
+            if step == 3:
+                return [
+                    rs_copy(part(layer, u, (z + k) % 4, y, x, core), land.at[k - 1], layer, u, 2 + k, along_z[k - 1])
+                    for k in range(1, 4)
+                ]
+            return [rs_copy(fin[u].at[layer], grads_out[u].at[core], layer, u, 6, mate)]
+
+        def rs_route(u, act):
+            for side in range(2):
+                @pl.when(core == side)
+                def _(side=side):
+                    act((side + u) % 2 == 0)
+
+        def rs_start(layer, u, step):
+            def act(y_first):
+                for copy in rs_sends(layer, u, step, y_first):
+                    copy.start()
+
+            if step in (1, 2):
+                rs_route(u, act)
+            else:
+                act(True)
+
+        def stage_part(u, step):
+            if step == 0:
+                return stage[u]
+            if step == 1:
+                return stage[u].at[:, :, 0]
+            if step == 2:
+                return stage[u].at[:, 0, 0]
+            return stage[u].at[0:3, 0, 0]
+
+        def stage_copy(layer, u, step):
+            return pltpu.make_async_copy(lands[u][step].at[layer], stage_part(u, step), sem_stage.at[u])
+
+        def rs_arrive(layer, u, step):
+            def act(y_first):
+                for copy in rs_sends(layer, u, step, y_first):
+                    copy.wait_recv()
+
+            if step in (1, 2):
+                rs_route(u, act)
+            else:
+                act(True)
+            stage_copy(layer, u, step).start()
+
+        def rs_merge(layer, u, step):
+            stage_copy(layer, u, step).wait()
+            slot = layer + 1
+            buf, got = weight_buf[u], stage[u]
+            if step == 3:
+                total = buf[slot, z, y, x, core].astype(f32)
+                for k in range(3):
+                    total = total + got[k, 0, 0].astype(f32)
+                fin[u][layer] = total
+
+                @pl.when(core == layer)
+                def _():
+                    pltpu.make_async_copy(fin[u].at[layer], grads_out[u].at[core], sem_g.at[layer, u]).start()
+
+                @pl.when(core != layer)
+                def _():
+                    rs_start(layer, u, 4)
+
+                return
+
+            @pl.loop(0, 4)
+            def _(pz):
+                if step == 0:
+                    buf[slot, pz, :, :, core] += got[pz]
+                elif step == 2:
+                    buf[slot, pz, y, x, core] += got[pz, 0, 0]
+                else:
+                    def act(y_first):
+                        if y_first:
+                            buf[slot, pz, y, :, core] += got[pz, :, 0]
+                        else:
+                            buf[slot, pz, :, x, core] += got[pz, :, 0]
+
+                    rs_route(u, act)
+
+            rs_start(layer, u, step + 1)
+
+        def rs_finish(layer, u):
+            @pl.when(core == layer)
+            def _():
+                pltpu.make_async_copy(fin[u].at[layer], grads_out[u].at[core], sem_g.at[layer, u]).wait()
+                rs_sends(layer, u, 4, True)[0].wait_recv()
+
+            @pl.when(core != layer)
+            def _():
+                rs_sends(layer, u, 4, True)[0].wait_send()
+
+            for step in range(4):
+                def act(y_first, step=step):
+                    for copy in rs_sends(layer, u, step, y_first):
+                        copy.wait_send()
+
+                if step in (1, 2):
+                    rs_route(u, act)
+                else:
+                    act(True)
+
+        def stat_copy(step, k=0):
+            target = (mate, near_y, near_x)[step] if step < 3 else along_z[k]
+            spot = step if step < 3 else 3 + z
+            return pltpu.make_async_remote_copy(
+                src_ref=stat_sum.at[step],
+                dst_ref=stat_land.at[spot],
+                send_sem=stat_send.at[step + k],
+                recv_sem=stat_recv.at[step + k],
+                device_id=target,
+                device_id_type=pl.DeviceIdType.MESH,
+            )
+
+        def stat_step(step):
+            if step == 0:
+                stat_sum[0] = stat_ref[...]
+            elif step < 4:
+                stat_copy(step - 1).wait()
+                stat_sum[step] = stat_sum[step - 1] + stat_land[step - 1]
+            if step < 3:
+                stat_copy(step).start()
+            elif step == 3:
+                stat_land[3 + z] = stat_sum[3]
+                for k in range(3):
+                    stat_copy(3, k).start()
+            else:
+                for k in range(3):
+                    stat_copy(3, k).wait()
+                total = stat_land[3] + stat_land[4] + stat_land[5] + stat_land[6]
+                stat_ref[...] = total
+                stat_done()
+
+        stat_step(0)
+        wq_u, wo_u, wu_u, wd_u = range(4)
+
+        def arrive(layer, step, *us):
+            return [partial(rs_arrive, layer, u, step) for u in us]
+
+        def merge(layer, step, *us):
+            return [partial(rs_merge, layer, u, step) for u in us]
+
+        def send(layer, *us):
+            return [partial(rs_start, layer, u, 0) for u in us]
+
+        back_points = {
+            (1, "ffn0"): [partial(stat_step, 1)],
+            (1, "ffn1"): [partial(stat_step, 2)],
+            (1, "ffn2"): [partial(stat_step, 3)],
+            (1, "ffn3"): [partial(stat_step, 4)] + send(1, wd_u, wu_u),
+            (1, "mid"): arrive(1, 0, wd_u, wu_u),
+            (1, "wo"): merge(1, 0, wd_u, wu_u) + send(1, wo_u),
+            (1, "att0"): arrive(1, 0, wo_u),
+            (1, "quad"): merge(1, 0, wo_u),
+            (1, "att1"): arrive(1, 1, wd_u, wu_u),
+            (1, "wq"): send(1, wq_u) + merge(1, 1, wd_u, wu_u),
+            (1, "in0"): arrive(1, 1, wo_u),
+            (1, "in1"): merge(1, 1, wo_u) + arrive(1, 0, wq_u),
+            (0, "ffn0"): merge(1, 0, wq_u) + arrive(1, 2, wd_u, wu_u),
+            (0, "ffn1"): merge(1, 2, wd_u, wu_u) + arrive(1, 2, wo_u),
+            (0, "ffn2"): merge(1, 2, wo_u) + arrive(1, 1, wq_u),
+            (0, "ffn3"): merge(1, 1, wq_u) + arrive(1, 3, wd_u, wu_u, wo_u) + send(0, wd_u, wu_u),
+            (0, "mid"): merge(1, 3, wd_u, wu_u, wo_u) + arrive(1, 2, wq_u) + arrive(0, 0, wd_u, wu_u),
+            (0, "wo"): merge(1, 2, wq_u) + merge(0, 0, wd_u, wu_u) + send(0, wo_u),
+            (0, "att0"): arrive(0, 0, wo_u) + arrive(1, 3, wq_u),
+            (0, "quad"): merge(0, 0, wo_u) + merge(1, 3, wq_u) + arrive(0, 1, wd_u, wu_u),
+            (0, "att1"): merge(0, 1, wd_u, wu_u) + arrive(0, 1, wo_u),
+            (0, "wq"): send(0, wq_u) + merge(0, 1, wo_u),
+            (0, "in0"): arrive(0, 2, wd_u, wu_u),
+            (0, "in1"): merge(0, 2, wd_u, wu_u) + arrive(0, 0, wq_u) + arrive(0, 2, wo_u),
+            (0, "end"): merge(0, 0, wq_u)
+            + merge(0, 2, wo_u)
+            + arrive(0, 3, wd_u, wu_u)
+            + merge(0, 3, wd_u, wu_u)
+            + arrive(0, 1, wq_u)
+            + merge(0, 1, wq_u)
+            + arrive(0, 3, wo_u)
+            + merge(0, 3, wo_u)
+            + arrive(0, 2, wq_u)
+            + merge(0, 2, wq_u)
+            + arrive(0, 3, wq_u)
+            + merge(0, 3, wq_u),
+        }
+    else:
+        back_points = {}
+
+    def stat_done():
+        totals = stat_ref[...]
+        stat_out[...] = totals if not routed else jnp.sqrt(totals / (totals[0:1, 3:4, :] * width))
+
+    if not routed:
+        stat_done()
+
+    def back_point(layer, point, s=None, at=None):
+        for (at_layer, at_point), actions in back_points.items():
+            if at_point == point:
+                here = layer == at_layer
+                if s is not None:
+                    here = here & (s == at)
+
+                @pl.when(here)
+                def _(actions=actions):
+                    for action in actions:
+                        action()
 
     def norm_back(x, gain, grad):
         inv = lax.rsqrt(jnp.mean(x * x, axis=1, keepdims=True) + norm_eps)
         hat = x * inv
-        dgain = jnp.sum(grad * hat, axis=0, keepdims=True)
         scaled = grad * gain
-        return inv * (scaled - hat * jnp.mean(scaled * hat, axis=1, keepdims=True)), dgain
+        return inv * (scaled - hat * jnp.mean(scaled * hat, axis=1, keepdims=True))
+
+    def add_gain(k, d_weight, weight):
+        for p in range(d_weight.shape[1] // lanes):
+            cols = slice(p * lanes, (p + 1) * lanes)
+            gain_sums[k] += d_weight[:, cols] * weight[:, cols].astype(f32)
+
+    def pack_small(layer):
+        turned = dbias[...].T
+        for h in range(heads):
+            ext[pl.ds(h, slots, stride=heads), :] = jnp.broadcast_to(turned[:slots, h : h + 1], (slots, lanes))
+        lane = lax.broadcasted_iota(jnp.int32, (width, lanes), 1)
+        gain = mat(0, layer, slice(0, lanes)).astype(f32)
+        sums = [jnp.sum(gain_sums[k], axis=1, keepdims=True) for k in range(2)]
+        safe = jnp.where(lane < 2, gain, 1.0)
+        value = jnp.where(lane == 0, sums[0], jnp.where(lane == 1, sums[1], 0.0)) / safe
+        value = jnp.where(lane == 2, ext[...], value)
+        put_mat(0, layer + 1, value.astype(bf16), slice(0, lanes))
 
     def backward_ffn(layer):
         slot = layer + 1
@@ -476,9 +781,11 @@
         def _(s):
             at = seg_rows(s)
             h = hbuf[layer, at, :].astype(f32)
-            n2buf[at, :] = (h * lax.rsqrt(jnp.mean(h * h, axis=1, keepdims=True) + norm_eps) * gains[layer, 1]).astype(bf16)
+            doa[0, at, :] = (h * lax.rsqrt(jnp.mean(h * h, axis=1, keepdims=True) + norm_eps) * gains[layer, 1]).astype(bf16)
 
         dn[...] = jnp.zeros_like(dn)
+        gain_sums[...] = jnp.zeros_like(gain_sums)
+        dbias[...] = jnp.zeros_like(dbias)
 
         @pl.loop(0, ff // chunk)
         def _(c):
@@ -493,13 +800,16 @@
             d_pre = (d_act * slope).astype(bf16)
             pre[:, cols] = d_pre
             put_mat(3, slot, tn(act.astype(bf16), dy[...]).astype(bf16), planes=planes)
-            put_mat(2, slot, tn(n2buf[...], d_pre).astype(bf16), cols)
+            d_up = tn(doa[0], d_pre)
+            add_gain(1, d_up, mat(2, layer, cols))
+            put_mat(2, slot, d_up.astype(bf16), cols)
             dn[...] += nt(d_pre, mat(2, layer, cols))
+            for k in range(ff // chunk):
+                back_point(layer, "ffn" + str(k), c, k)
 
     def backward_middle(layer, s):
         at = seg_rows(s)
-        dh, dgain = norm_back(hbuf[layer, at, :].astype(f32), gains[layer, 1], dn[at, :])
-        dgf_ref[layer] += dgain
+        dh = norm_back(hbuf[layer, at, :].astype(f32), gains[layer, 1], dn[at, :])
         dh = dh + dy[at, :].astype(f32)
         dn[at, :] = dh
         dz = dh.astype(bf16)
@@ -533,7 +843,7 @@
                 va = vp * own.astype(bf16) + (marks[0] + marks[1]).astype(bf16)
                 weights = ebuf[s, h]
                 d_scores = weights.astype(f32) * nt(do_h, va)
-                dbias_ref[layer, h : h + 1, :] += jnp.sum(d_scores[:, :lanes], axis=0, keepdims=True)
+                dbias[h : h + 1, :] += jnp.sum(d_scores[:, :lanes], axis=0, keepdims=True)
                 d_scores = d_scores.astype(bf16)
                 half = slice(side * head_size, (side + 1) * head_size)
                 dq.append(mm(d_scores, kp))
@@ -543,21 +853,19 @@
             qkv[at, cols] = (jnp.where(own > 0, dq[0], dq[1]) * score_scale).astype(bf16)
             qkv[at, kcols] = (jnp.concatenate(dk, axis=0).T * (1.0 / log2_e)).astype(bf16)
             qkv[at, vcols] = jnp.concatenate(dv, axis=0).T.astype(bf16)
+            if p == pairs // 2 - 1:
+                back_point(layer, "quad", s, 1)
 
     def backward_input(layer, s):
         at = seg_rows(s)
         x = ub[layer, at, :].astype(f32)
-        du, dgain = norm_back(x, gains[layer, 0], nt(qkv[at, :], mat(0, layer, slice(lanes, lanes + 3 * width))))
-        dga_ref[layer] += dgain
+        du = norm_back(x, gains[layer, 0], nt(qkv[at, :], mat(0, layer, slice(lanes, lanes + 3 * width))))
         dy[at, :] = (du + dn[at, :]).astype(bf16)
-        n2buf[at, :] = (x * lax.rsqrt(jnp.mean(x * x, axis=1, keepdims=True) + norm_eps) * gains[layer, 0]).astype(bf16)
-
-    def grad_copies(layer, picks=range(4)):
-        slot = layer + 1
+
+    def grad_copies(layer):
         return [
-            pltpu.make_async_copy(src.at[slot], dst.at[layer], sem_g.at[layer, k])
-            for k, (src, dst) in enumerate(((wq, gq_out), (wo, go_out), (wu, gu_out), (wd, gd_out)))
-            if k in picks
+            pltpu.make_async_copy(buf.at[layer + 1], out.at[layer], sem_g.at[layer, k])
+            for k, (buf, out) in enumerate(zip(weight_buf, grads_out))
         ]
 
     @pl.loop(0, 2)
@@ -573,13 +881,19 @@
 
         backward_ffn(layer)
 
+        @pl.when(layer == 1)
+        def _():
+            for copies in y_copies:
+                for copy in copies:
+                    copy.wait()
+
         @pl.loop(0, segs)
         def _(s):
             backward_middle(layer, s)
 
+        back_point(layer, "mid")
         put_mat(1, slot, tn(obuf[...], dy[...]).astype(bf16))
-        for copy in grad_copies(layer, (1, 2, 3)):
-            copy.start()
+        back_point(layer, "wo")
 
         @pl.when(layer == 1)
         def _():
@@ -600,64 +914,89 @@
             def _():
                 spill_copies(s, True, (1,))[0].start()
 
+            for k in range(segs):
+                back_point(layer, "att" + str(k), s, k)
+
+        @pl.loop(0, segs)
+        def _(s):
+            at = seg_rows(s)
+            v = ub[layer, at, :].astype(f32)
+            doa[0, at, :] = (v * lax.rsqrt(jnp.mean(v * v, axis=1, keepdims=True) + norm_eps) * gains[layer, 0]).astype(bf16)
+
+        for k in range(3):
+            cols = slice(k * width, (k + 1) * width)
+            d_weight = tn(doa[0], qkv[:, cols])
+            add_gain(0, d_weight, mat(0, layer, qkv_cols(k)))
+            put_mat(0, slot, d_weight.astype(bf16), qkv_cols(k))
+        pack_small(layer)
+        back_point(layer, "wq")
+
         @pl.loop(0, segs)
         def _(s):
             backward_input(layer, s)
-
-        for k in range(3):
-            part = slice(k * width, (k + 1) * width)
-            put_mat(0, slot, tn(n2buf[...], qkv[:, part]).astype(bf16), qkv_cols(k))
-        grad_copies(layer, (0,))[0].start()
+            for k in range(segs):
+                back_point(layer, "in" + str(k), s, k)
 
         @pl.when(layer == 1)
         def _():
             for s in range(segs):
                 spill_copies(s, True, (0,))[0].start()
 
-        for copy in grad_copies(layer):
+        if not routed:
+            for copy in grad_copies(layer):
+                copy.start()
+            for copy in grad_copies(layer):
+                copy.wait()
+
+    for copies in du_copies:
+        for copy in copies:
+            copy.start()
+    back_point(0, "end")
+    if routed:
+        for layer in (1, 0):
+            for u in range(4):
+                rs_finish(layer, u)
+    for copies in du_copies:
+        for copy in copies:
             copy.wait()
 
-    du_copy.start()
-    du_copy.wait()
-    y_copy.wait()
-
-
-def run_layers(doc_len, u0, dout, weights, routed, heads, slots, segs):
-    all_rows, width = u0.shape
-    rows = all_rows // segs
-    ff = weights[2].shape[-1]
-    dims = (segs, rows, width, ff, slots, heads)
+
+def run_layers(dims, routed, doc_len, row_args, weights):
+    segs, rows, width, ff, slots, heads = dims
+    all_rows = segs * rows
     vmem = pl.BlockSpec(memory_space=pltpu.VMEM)
     smem = pl.BlockSpec(memory_space=pltpu.SMEM)
     hbm = pl.BlockSpec(memory_space=pl.ANY)
     shape = jax.ShapeDtypeStruct
+    dma = pltpu.SemaphoreType.DMA
     wide = (all_rows, width)
-    grid = (4, 2, 2, 2)
-    mats = [
-        (*grid, width // 32, lanes + 3 * width),
-        (*grid, width // 32, width),
-        (*grid, width // 32, ff),
-        (*grid, ff // 32, width),
+    tiles = [
+        (width // 32, lanes + 3 * width),
+        (width // 32, width),
+        (width // 32, ff),
+        (ff // 32, width),
     ]
-    spills = [
+    out_shape = [shape(part.shape, bf16) for part in row_args]
+    if routed:
+        out_shape += [shape((2, *tile), f32) for tile in tiles]
+    else:
+        out_shape += [shape((2, 4, 2, 2, 2, *tile), bf16) for tile in tiles]
+    row_outs = len(out_shape)
+    out_shape += [shape((2, 8, lanes), f32)]
+    out_shape += [
         shape((all_rows, 3 * width), bf16),
         shape((segs, heads, rows, rows), bf16),
         shape(wide, bf16),
         shape(wide, bf16),
         shape((all_rows, ff), bf16),
     ]
-    out_shape = [shape(wide, bf16)] * 2
-    out_shape += [shape((2, *mat), bf16) for mat in mats]
-    out_shape += [
-        shape((2, 1, width), f32),
-        shape((2, 1, width), f32),
-        shape((2, heads, lanes), f32),
-        shape((2, 8, lanes), f32),
-    ] + spills
+    if routed:
+        for tile in tiles:
+            out_shape += [shape((2, *lead, *tile), bf16) for lead in ((4, 2, 2), (4, 2), (4,), (3,))]
     unit_count = 16
-    scratch = [pltpu.VMEM((3, *mat), bf16) for mat in mats]
+    scratch = [pltpu.VMEM((3, 4, 2, 2, 2, *tile), bf16) for tile in tiles]
     scratch += [
-        pltpu.VMEM((3, *wide), bf16),
+        pltpu.VMEM((2, *wide), bf16),
         pltpu.VMEM(wide, bf16),
         pltpu.VMEM((all_rows, 3 * width), bf16),
         pltpu.VMEM((segs, heads, rows, rows), bf16),
@@ -667,29 +1006,44 @@
         pltpu.VMEM((all_rows, ff), bf16),
         pltpu.VMEM((2, *wide), bf16),
         pltpu.VMEM(wide, f32),
-        pltpu.VMEM(wide, bf16),
         pltpu.VMEM((2, 2, 1, width), f32),
         pltpu.VMEM((2, heads, slots, lanes), f32),
         pltpu.VMEM((width, lanes), f32),
-        pltpu.SemaphoreType.DMA((segs, 5)),
-        pltpu.SemaphoreType.DMA((segs, 5)),
-        pltpu.SemaphoreType.DMA((2, 4)),
-        pltpu.SemaphoreType.DMA((4,)),
-        pltpu.SemaphoreType.DMA((unit_count,)),
-        pltpu.SemaphoreType.DMA((unit_count, 11)),
-        pltpu.SemaphoreType.DMA((unit_count, 11)),
+        pltpu.VMEM((2, width, lanes), f32),
+        pltpu.VMEM((heads, lanes), f32),
+        pltpu.VMEM((2, 8, lanes), f32),
+        dma((segs, 5)),
+        dma((segs, 5)),
+        dma((2, 4)),
+        dma((8 * segs,)),
+        dma((unit_count,)),
+        dma((unit_count, 11)),
+        dma((unit_count, 11)),
     ]
     params = dict(vmem_limit_bytes=63 * 2**20)
     if routed:
         params.update(collective_id=0, has_side_effects=True)
+        scratch += [pltpu.VMEM((4, 2, 2, *tile), bf16) for tile in tiles]
+        scratch += [pltpu.VMEM((2, *tile), f32) for tile in tiles]
+        scratch += [
+            pltpu.VMEM((4, 2, 8, lanes), f32),
+            pltpu.VMEM((7, 2, 8, lanes), f32),
+            dma((4,)),
+            dma((2, 4, 7)),
+            dma((2, 4, 7)),
+            dma((8 * segs,)),
+            dma((8 * segs,)),
+            dma((6,)),
+            dma((6,)),
+        ]
     return pl.pallas_call(
         partial(fused_layers, dims, routed),
         out_shape=out_shape,
-        in_specs=[smem] + [hbm] * 6,
-        out_specs=[hbm] * 6 + [vmem] * 4 + [hbm] * 5,
+        in_specs=[smem] + [hbm] * (len(row_args) + 4),
+        out_specs=[hbm] * row_outs + [vmem] + [hbm] * (len(out_shape) - row_outs - 1),
         scratch_shapes=scratch,
         compiler_params=pltpu.CompilerParams(**params),
-    )(doc_len, u0, dout, *weights)[:10]
+    )(doc_len, *row_args, *weights)[: row_outs + 1]
 
 
 def swap(block):
@@ -717,9 +1071,26 @@
     half_tok = tokens.shape[1]
     half_mem = memory.shape[1]
     slots = 2 * half_mem
-    seg_len = 2 * half_tok
-    rows = slots + seg_len
+    rows = slots + 2 * half_tok
     width = tokens.shape[2]
+    ff = w_up.shape[2]
+    heads = forget_bias.shape[1] * lax.axis_size("dp") // slots
+    per_doc = micro // lengths.shape[0]
+    dims = (segs, rows, width, ff, slots, heads)
+    own_len = lax.dynamic_slice_in_dim(lengths, section * segs // per_doc, 1, 0)
+    small = jnp.stack([gain_attn, gain_ffn, forget_bias], axis=2)
+    small = jnp.pad(small, ((0, 0), (0, 0), (0, lanes - 3)))
+    pieces = (jnp.concatenate([small, w_qkv], axis=2), w_out, w_up, w_down)
+
+    def unpack(grads):
+        grad_q = grads[0]
+        return (grad_q[:, :, lanes:], *grads[1:], *(grad_q[:, :, k] for k in range(3)))
+
+    if lax.axis_size("dp") == 16 and w_qkv.shape[1] == 32:
+        weights = [piece.reshape(2, -1, piece.shape[2]) for piece in pieces]
+        *outs, rms = run_layers(dims, True, own_len, (tokens, memory, grad_tokens, grad_memory), weights)
+        grads = [grad.reshape(1, -1, grad.shape[2]) for grad in outs[4:]]
+        return (*outs[:4], *unpack(grads), rms[:, :3, 0])
 
     def own_segs(halves):
         return lax.dynamic_slice_in_dim(halves, section * segs, segs, 0)
@@ -738,42 +1109,22 @@
     u0 = jnp.concatenate([full[1], full[0]], axis=1).reshape(segs * rows, width)
     dout = jnp.concatenate([full[3], full[2]], axis=1).reshape(segs * rows, width)
 
-    heads = forget_bias.shape[1] * lax.axis_size("dp") // slots
-    small = jnp.stack([gain_attn, gain_ffn, forget_bias], axis=2)
-    small = jnp.pad(small, ((0, 0), (0, 0), (0, lanes - 3)))
-    pieces = (jnp.concatenate([small, w_qkv], axis=2), w_out, w_up, w_down)
-    routed = lax.axis_size("dp") == 16 and width == 512
-
     def gather(piece):
         whole = lax.all_gather(piece, ("section", "dp"), axis=1, tiled=True)
         return whole.reshape(2, 4, 2, 2, 2, -1, piece.shape[2])
 
-    if routed:
-        weights = [piece.reshape(2, -1, piece.shape[2]) for piece in pieces]
-    else:
-        weights = [gather(piece) for piece in pieces]
-    per_doc = micro // lengths.shape[0]
-    own_len = lax.dynamic_slice_in_dim(lengths, section * segs // per_doc, 1, 0)
-    y, du, gq, go, gu, gd, dga, dgf, dbias, stats = run_layers(
-        own_len, u0, dout, weights, routed, heads, slots, segs
-    )
+    y, du, *grads, stats = run_layers(dims, False, own_len, (u0, dout), [gather(piece) for piece in pieces])
 
     def scatter(grad):
+        grad = grad.reshape(2, -1, grad.shape[-1])
         mine = lax.dynamic_index_in_dim(grad, section, 0, keepdims=True)
         other = lax.dynamic_index_in_dim(grad, 1 - section, 0, keepdims=True)
         chip = (mine.astype(f32) + swap(other).astype(f32)).astype(grad.dtype)
         return lax.psum_scatter(chip, "dp", scatter_dimension=1, tiled=True).astype(f32)
 
-    gq, go, gu, gd = (
-        grad.reshape(2, -1, grad.shape[-1]) for grad in (gq[..., lanes:], go, gu, gd)
-    )
-    grad_bias = jnp.swapaxes(dbias[:, :, :slots], 1, 2).reshape(2, slots * heads)
-    shares = tuple(scatter(grad) for grad in (gq, go, gu, gd, dga[:, 0], dgf[:, 0], grad_bias))
-    token_count = jnp.sum(own_len).astype(f32)
-    sums = jnp.concatenate([stats[:, :3, 0].reshape(6), token_count[None]])
-    totals = lax.psum(sums, ("section", "dp"))
-    rms = jnp.sqrt(totals[:6].reshape(2, 3) / (totals[6] * width))
-
+    shares = unpack([scatter(grad) for grad in grads])
+    totals = lax.psum(stats[:, :4, 0], ("section", "dp"))
+    rms = jnp.sqrt(totals[:, :3] / (totals[0, 3] * width))
     result = jnp.stack([y.reshape(segs, rows, width), du.reshape(segs, rows, width)])
 
     def half_of(which):

time: 791 us -> 231 us (0.29)
  waiting for transfers between devices: 514 us -> 0 us
  Pallas kernels: 165 us -> 215 us
  blocking collectives: 41.3 us -> 0 us
  other arithmetic: 25.7 us -> 2.24 us
  between operations: 15.8 us -> 0.7 us
  local copies, waits for them, and re-layouts: 24.1 us -> 12.6 us
    reduce_scatter x4 -> x0, waiting for transfers between devices: 353 us -> none  [scatter(): lax.psum_scatter(chip, 'dp', scatter_dimension=1, tiled=True).astype(f32)]
    unnamed x10 -> x0, waiting for transfers between devices: 153 us -> none
    pallas_call x1, Pallas kernels: 165 us -> 215 us  [run_layers(): pl.pallas_call(partial(fused_layers, dims, routed), out_shape=out_shape,...]
    psum x1 -> x0, blocking collectives: 41.3 us -> none  [body(): totals = lax.psum(sums, ('section', 'dp'))]
    convert_element_type x8 -> x0, other arithmetic: 15.4 us -> none  [the longest x4 9.18 us: scatter(): chip = (mine.astype(f32) + swap(other).astype(f32)).astype(grad.dtype)]
    dynamic_slice x11 -> x0, local copies, waits for them, and re-layouts: 11 us -> none  [the longest x7 6.54 us: scatter(): other = lax.dynamic_index_in_dim(grad, 1 - section, 0, keepdims=True)]
    ppermute x13 -> x0, waiting for transfers between devices: 8.05 us -> none  [swap(): return lax.ppermute(block, 'section', [(0, 1), (1, 0)])]
  transfers between devices with their start and end apart: 20 -> 0, of which waited for: 10 -> 0; matrix products, arithmetic and copies ran while one was open for 5% -> 0% of each run, Pallas kernels for 0% -> 0%
where the time goes in v3:
time: 231 us
  Pallas kernels  215 us (93%)
  local copies, waits for them, and re-layouts  12.6 us (5%)
    pallas_call x1, Pallas kernels, run_layers(): pl.pallas_call(partial(fused_layers, dims, routed), out_shape=out_shape,...  215 us
    unnamed x20, local copies, waits for them, and re-layouts  6.76 us

profile of v3, /device:TPU:0, one launch (start us, length us, event | category | flops | bytes accessed | tf_op | source)
XLA Modules:
  0.0 230.6 jit_solution(10380344013419308955)
XLA Ops:
  0.7 1.2 dynamic_slice.3.refs_0_
  1.9 0.7 pad_maximum_fusion
  2.6 0.1 copy.26
  2.7 1.5 fusion.1
  4.2 215.1 %shard_map.211 = (bf16[4,256,512]{2,1,0:T(8,128)(2,1)}, bf16[4,32,512]{2,1,0:T(8,128)(2,1)}, bf16[4,256,512]{2,1,0:T(8,128)(2,1)}, bf16[4,32,512]{2,1,0:T(8,128)...) custom-call(s32[1]{0:T(128)} %dynamic_slice.3.refs_0_, ...), custom_call_target="tpu_custom_call" | custom-call | tf_op jit(solution)/shard_map/pallas_call | solution.py:1039
  219.3 0.0 copy-start.4
  219.3 0.0 copy-start
  219.3 1.4 slice_reduce_fusion.3
  220.8 1.6 slice_reduce_fusion
  222.3 1.6 slice.20
  224.0 0.0 copy-start.5
  224.0 2.3 %copy.34 = bf16[4,256,512]{2,1,0:T(8,128)(2,1)} copy(bf16[4,256,512]{2,1,0:T(8,128)(2,1)} %get-tuple-element.45) | data formatting | bytes 2097152
  226.3 0.0 copy-done.4
  226.3 0.7 copy.35
  226.9 0.0 copy-done
  227.0 1.0 copy.36
  227.9 0.0 copy-done.3
  227.9 0.7 copy.37
  228.6 0.0 copy-done.5
  228.6 0.6 copy.38
  229.2 0.0 copy-done.2
  229.2 0.7 copy.39
  229.9 0.0 copy-done.1
  229.9 0.7 copy.40
  (3 shorter events, 0.0 us)
Async XLA Ops:
  219.3 7.0 %copy-start.4 = (bf16[4,32,512]{2,1,0:T(8,128)(2,1)S(1)}, bf16[4,32,512]{2,1,0:T(8,128)(2,1)}, u32[]{:S(2)}) copy-start(bf16[4,32,512]{2,1,0:T(8,128)(2,1)} %get-tuple-element.46) | copy-start | bytes 393220
  219.3 7.6 %copy-start = (bf16[4,256,512]{2,1,0:T(8,128)(2,1)S(1)}, bf16[4,256,512]{2,1,0:T(8,128)(2,1)}, u32[]{:S(2)}) copy-start(bf16[4,256,512]{2,1,0:T(8,128)(2,1)} %get-tuple-element.47) | copy-start | bytes 3145732
  224.0 4.0 %copy-start.3 = (bf16[4,32,512]{2,1,0:T(8,128)(2,1)S(1)}, bf16[4,32,512]{2,1,0:T(8,128)(2,1)}, u32[]{:S(2)}) copy-start(bf16[4,32,512]{2,1,0:T(8,128)(2,1)} %get-tuple-element.48) | copy-start | bytes 393220
  224.0 4.6 %copy-start.5 = (f32[2,16,512]{2,1,0:T(8,128)S(1)}, f32[2,16,512]{2,1,0:T(8,128)}, u32[]{:S(2)}) copy-start(f32[2,16,512]{2,1,0:T(8,128)} %get-tuple-element.26) | copy-start | bytes 196612
  224.0 5.2 %copy-start.2 = (f32[2,16,2048]{2,1,0:T(8,128)S(1)}, f32[2,16,2048]{2,1,0:T(8,128)}, u32[]{:S(2)}) copy-start(f32[2,16,2048]{2,1,0:T(8,128)} %get-tuple-element.27) | copy-start | bytes 786436
  226.3 3.6 %copy-start.1 = (f32[2,64,512]{2,1,0:T(8,128)S(1)}, f32[2,64,512]{2,1,0:T(8,128)}, u32[]{:S(2)}) copy-start(f32[2,64,512]{2,1,0:T(8,128)} %get-tuple-element.28) | copy-start | bytes 786436

commit v4 on v3

v4 whole, which is shorter than its diff:
```python
from functools import partial

import jax
import jax.numpy as jnp
from jax import lax
from jax.experimental import pallas as pl
from jax.experimental.pallas import tpu as pltpu
from jax.sharding import PartitionSpec as P

norm_eps = 1e-06
score_scale = 0.125
log2_e = 1.4426950408889634
masked_score = -1000000000.0
gelu_c = 0.7978845608028654
gelu_k = 0.044715
f32 = jnp.float32
bf16 = jnp.bfloat16
lanes = 128
chunk = 512


def mm(a, b, ca=1, cb=0):
    return lax.dot_general(a, b, (((ca,), (cb,)), ((), ())), preferred_element_type=f32)


def nt(a, b):
    return mm(a, b, 1, 1)


def tn(a, b):
    return mm(a, b, 0, 0)


def lane_marks(head_size, side):
    lane = lax.broadcasted_iota(jnp.int32, (1, lanes), 1)
    own = ((lane // head_size) == side).astype(f32)
    first = (1 - side) * head_size
    marks = [(lane == first + k).astype(f32) for k in range(3)]
    return own, marks


def fused_layers(dims, routed, *refs):
    segs, rows, width, ff, slots, heads, per_doc = dims
    refs = list(refs)

    def take(count):
        picked = refs[:count]
        del refs[:count]
        return picked

    (len_ref,) = take(1)
    rows_in = take(4 if routed else 2)
    weight_in = take(5 if routed else 4)
    rows_out = take(4 if routed else 2)
    grads_out = take(5 if routed else 4)
    (stat_out,) = take(1)
    spill_hbm = take(8)
    weight_buf = take(4)
    ub, dy, qkv, ebuf, obuf, ilbuf, hbuf, slope, active, doa, dn = take(11)
    gains, bias_rows, ext, gain_sums, dbias, stat_ref = take(6)
    sem_spill, sem_back, sem_g, sem_io, sem_own, sem_send, sem_recv = take(7)
    if routed:
        lands = [take(4) for _ in range(5)]
        fin = take(5)
        stat_sum, stat_land = take(2)
        rs_send, rs_recv, rs_free, io_send, io_recv, stat_send, stat_recv = take(7)
    head_size = width // heads
    pairs = width // lanes
    tok_rows = rows - slots
    quads = width // (2 * lanes)
    quad = 2 * lanes
    first_doc = lax.axis_index("section") * segs // per_doc if routed else 0
    every = slice(None)

    def units_of(layer):
        half_ff, half_deep = ff // 2, ff // 64
        lead = [
            (0, slice(0, lanes + width), every),
            (0, slice(lanes + width, lanes + 2 * width), every),
            (0, slice(lanes + 2 * width, lanes + 3 * width), every),
        ]
        rest = [(1, every, every)]
        rest += [(3, every, slice(k * half_deep, (k + 1) * half_deep)) for k in range(2)]
        rest += [(2, slice(k * half_ff, (k + 1) * half_ff), every) for k in range(2)]
        return [(layer, *unit) for unit in lead + rest]

    units = units_of(0) + units_of(1)
    first_units = [k for k, unit in enumerate(units) if unit[1] == 0]
    last_units = [7, 15]
    later_units = [k for k, unit in enumerate(units) if unit[1] != 0 and k not in last_units]
    plane_first = (11, 15)

    def view(n, z, y, x, c):
        layer, which, cols, part = units[n]
        return weight_buf[which].at[layer, z, y, x, c, part, cols]

    if routed:
        core = lax.axis_index("section")
        chip = lax.axis_index("dp")
        z, y, x = chip // 4, (chip // 2) % 2, chip % 2
        other = 1 - core

        def place(pz, py, px):
            return pz * 4 + py * 2 + px

        mate = (other, chip)
        near_x = (core, place(z, y, 1 - x))
        near_y = (core, place(z, 1 - y, x))
        along_z = [(core, place((z + k) % 4, y, x)) for k in range(1, 4)]

        def remote(src, dst, n, k, target):
            return pltpu.make_async_remote_copy(
                src_ref=src,
                dst_ref=dst,
                send_sem=sem_send.at[n, k],
                recv_sem=sem_recv.at[n, k],
                device_id=target,
                device_id_type=pl.DeviceIdType.MESH,
            )

        def own_shards(n):
            layer, which, cols, part = units[n]
            home = weight_buf[which].at[layer, z, y, x]
            if which > 0:
                return [(weight_in[which].at[every, part, cols], home.at[every, part, cols], 0)]
            start = max(cols.start - lanes, 0)
            matrix = slice(start, cols.stop - lanes)
            pairs_of = [(weight_in[0].at[every, every, matrix], home.at[every, every, slice(start + lanes, cols.stop)], 0)]
            if cols.start == 0:
                pairs_of.append((weight_in[4], home.at[every, every, slice(0, lanes)], 11))
            return pairs_of

        def z_copy(n, k):
            where = view(n, z, every, every, core) if n in plane_first else view(n, z, y, x, core)
            return remote(where, where, n, k, along_z[k - 1])

        def plane_copy(n, k, x_first):
            planes = z if n in plane_first else every
            if k == 4:
                where = view(n, planes, y, x, core)
                return remote(where, where, n, 4, near_x if x_first else near_y)
            where = view(n, planes, y, every, core) if x_first else view(n, planes, every, x, core)
            return remote(where, where, n, 5, near_y if x_first else near_x)

        def mate_copy(n, k, x_first, half):
            planes = z if n in plane_first else every
            if k < 9:
                from_z = (z + 4 - (k - 5)) % 4
                where = view(n, from_z, every, every, half) if n in plane_first else view(n, from_z, y, x, half)
            elif k == 9:
                where = view(n, planes, y, 1 - x, half) if x_first else view(n, planes, 1 - y, x, half)
            else:
                where = view(n, planes, 1 - y, every, half) if x_first else view(n, planes, every, 1 - x, half)
            return remote(where, where, n, k, mate)

        def by_route(n, act):
            for side in range(2):
                @pl.when(core == side)
                def _(side=side):
                    act((side + n) % 2 == 0)

        def share_own(n):
            @pl.when(core == units[n][0])
            def _():
                for i, (src, dst, k) in enumerate(own_shards(n)):
                    pltpu.make_async_copy(src, dst, sem_own.at[n, i]).start()
                    remote(src, dst, n, k, mate).start()

        def start_z(n):
            @pl.when(core == units[n][0])
            def _():
                for i, (src, dst, k) in enumerate(own_shards(n)):
                    pltpu.make_async_copy(src, dst, sem_own.at[n, i]).wait()

            @pl.when(core != units[n][0])
            def _():
                for src, dst, k in own_shards(n):
                    remote(src, dst, n, k, mate).wait_recv()

            if n in plane_first:
                by_route(n, lambda x_first: plane_copy(n, 4, x_first).start())
            else:
                for k in range(1, 4):
                    z_copy(n, k).start()

        def first_hop(n):
            if n not in plane_first:
                for k in range(1, 4):
                    z_copy(n, k).wait_recv()

            def act(x_first):
                if n in plane_first:
                    plane_copy(n, 4, x_first).wait_recv()
                    plane_copy(n, 5, x_first).start()
                    mate_copy(n, 9, x_first, core).start()
                else:
                    plane_copy(n, 4, x_first).start()
                    for k in range(6, 9):
                        mate_copy(n, k, x_first, core).start()

            by_route(n, act)

        def second_hop(n):
            def act(x_first):
                if n in plane_first:
                    plane_copy(n, 5, x_first).wait_recv()
                    for k in range(1, 4):
                        z_copy(n, k).start()
                    mate_copy(n, 10, x_first, core).start()
                else:
                    plane_copy(n, 4, x_first).wait_recv()
                    plane_copy(n, 5, x_first).start()
                    mate_copy(n, 9, x_first, core).start()

            by_route(n, act)

        def last_share(n):
            def act(x_first):
                if n in plane_first:
                    for k in range(1, 4):
                        z_copy(n, k).wait_recv()
                        mate_copy(n, 5 + k, x_first, core).start()
                else:
                    plane_copy(n, 5, x_first).wait_recv()
                    mate_copy(n, 10, x_first, core).start()

            by_route(n, act)

        def complete(n):
            def act(x_first):
                for k in range(6, 11):
                    mate_copy(n, k, not x_first, other).wait_recv()

            by_route(n, act)

        def drain(n):
            @pl.when(core == units[n][0])
            def _():
                for src, dst, k in own_shards(n):
                    remote(src, dst, n, k, mate).wait_send()

            for k in range(1, 4):
                z_copy(n, k).wait_send()

            def act(x_first):
                for k in (4, 5):
                    plane_copy(n, k, x_first).wait_send()
                for k in range(6, 11):
                    mate_copy(n, k, x_first, core).wait_send()

            by_route(n, act)

        def hops(text):
            kinds = dict(z=start_z, f=first_hop, s=second_hop, l=last_share)
            for word in text.split():
                kinds[word[0]](int(word[1:]))

        opening = "z0 z1 z2 z3 z4 z5 f0 f1 s0 z6 f2 s1 z7 f3 s2 l0 f4 s3 l1 f5 s4 f6 l2"
        hops_at = {
            (0, 0, "qkv"): "s5 f7 z8 z9 z11 z15", (0, 0, "quad0"): "s6 z10 z12", (0, 0, "quad1"): "f8 z13 f11",
            (0, 1, "qkv"): "s7 f9", (0, 1, "quad0"): "s8 f10 z14 f15", (0, 1, "quad1"): "s9 s11",
            (0, 0, "gate"): "l3 l4 l5 l6 f12", (0, 0, "ffna"): "s10 f13", (0, 1, "ffna"): "s12 s15",
            (0, 0, "last"): "l7", (0, 0, "ffnb"): "s13 f14 l8", (0, 1, "ffnb"): "l9 l10",
            (1, 0, "qkv"): "s14",
            (1, 0, "gate"): "l11 l12 l13 l14", (1, 0, "last"): "l15",
        }
    else:
        hops_at = {}

        def weight_copy(n):
            layer, which, cols, part = units[n]
            src = weight_in[which].at[layer, every, every, every, every, part, cols]
            return pltpu.make_async_copy(src, view(n, every, every, every, every), sem_own.at[n, 0])

        def complete(n):
            weight_copy(n).wait()

    def after(layer, s, point):
        for (at_layer, at_s, at_point), text in hops_at.items():
            if at_point == point:
                @pl.when((layer == at_layer) & (s == at_s))
                def _(text=text):
                    hops(text)

    def need(layer, picks):
        for at_layer in range(2):
            @pl.when(layer == at_layer)
            def _(at_layer=at_layer):
                for n in picks:
                    if units[n][0] == at_layer:
                        complete(n)

    def mat(which, slot, cols=every, planes=None):
        if planes is None:
            value = weight_buf[which][slot, :, :, :, :, :, cols]
        else:
            value = weight_buf[which][slot, planes, :, :, :, :, cols]
        deep = 1
        for size in value.shape[:-1]:
            deep *= size
        return value.reshape(deep, value.shape[-1])

    def put_mat(which, slot, value, cols=every, planes=None):
        buf = weight_buf[which]
        shape = buf.shape[1:-1]
        if planes is None:
            buf[slot, :, :, :, :, :, cols] = value.reshape(*shape, value.shape[-1])
        else:
            buf[slot, planes] = value.reshape(1, *shape[1:], value.shape[-1])

    def qkv_cols(k):
        return slice(lanes + k * width, lanes + (k + 1) * width)

    def seg_rows(s):
        return pl.ds(pl.multiple_of(s * rows, rows), rows)

    def spill_copies(s, back, picks=range(7)):
        at = seg_rows(s)
        kept = (qkv.at[at], ebuf.at[s], obuf.at[at], ilbuf.at[at], slope.at[at], active.at[at], hbuf.at[at], ub.at[at])
        pairs_of = [
            (vmem, hbm.at[s] if k == 1 else hbm.at[at])
            for k, (vmem, hbm) in enumerate(zip(kept, spill_hbm))
        ]
        if back:
            return [
                pltpu.make_async_copy(hbm, vmem, sem_back.at[s, k])
                for k, (vmem, hbm) in enumerate(pairs_of)
                if k in picks
            ]
        return [
            pltpu.make_async_copy(vmem, hbm, sem_spill.at[s, k])
            for k, (vmem, hbm) in enumerate(pairs_of)
            if k in picks
        ]

    def doc_end(s):
        return len_ref[first_doc + s // per_doc] - (s % per_doc) * tok_rows

    def valid_col(s):
        row = lax.broadcasted_iota(jnp.int32, (rows, 1), 0)
        return jnp.where(
            (row >= slots) & (row - slots < doc_end(s)), 1.0, 0.0
        ).astype(f32)

    def mask_col(s):
        row = lax.broadcasted_iota(jnp.int32, (rows, 1), 0)
        return jnp.where(
            (row >= slots) & (row - slots >= doc_end(s)), masked_score, 0.0
        ).astype(f32)

    if routed:
        half_tok, half_mem = tok_rows // 2, slots // 2

        def io_copies(buf, tok_ref, mem_ref, first, outward):
            local, away = [], []
            k = first
            for s in range(segs):
                mine, theirs = core * segs + s, other * segs + s
                for ref, base, size in ((tok_ref, slots, half_tok), (mem_ref, 0, half_mem)):
                    def rows_of(half):
                        return buf.at[pl.ds(pl.multiple_of(s * rows + base + half * size, 16), size)]

                    if outward:
                        local.append(pltpu.make_async_copy(rows_of(core), ref.at[mine], sem_io.at[k]))
                        src, dst = rows_of(other), ref.at[mine]
                    else:
                        local.append(pltpu.make_async_copy(ref.at[mine], rows_of(core), sem_io.at[k]))
                        src, dst = ref.at[theirs], rows_of(core)
                    away.append(
                        pltpu.make_async_remote_copy(
                            src_ref=src,
                            dst_ref=dst,
                            send_sem=io_send.at[k],
                            recv_sem=io_recv.at[k],
                            device_id=mate,
                            device_id_type=pl.DeviceIdType.MESH,
                        )
                    )
                    k += 1
            return local, away

        loads, shares = io_copies(ub, rows_in[0], rows_in[1], 0, False)
        more = io_copies(dy, rows_in[2], rows_in[3], 2 * segs, False)
        loads, shares = loads + more[0], shares + more[1]
        y_copies = io_copies(doa.at[1], rows_out[0], rows_out[1], 4 * segs, True)
        du_copies = io_copies(dy, rows_out[2], rows_out[3], 6 * segs, True)
    else:
        loads = [
            pltpu.make_async_copy(rows_in[0], ub, sem_io.at[0]),
            pltpu.make_async_copy(rows_in[1], dy, sem_io.at[1]),
        ]
        shares = []
        y_copies = [pltpu.make_async_copy(doa.at[1], rows_out[0], sem_io.at[2])], []
        du_copies = [pltpu.make_async_copy(dy, rows_out[1], sem_io.at[3])], []
    for copy in loads:
        copy.start()
    if routed:
        barrier = pltpu.get_barrier_semaphore()
        peers = [mate, near_x, near_y, (core, place(z, 1 - y, 1 - x)), *along_z]
        peers += [(other, place((z + k) % 4, y, x)) for k in range(1, 4)]
        for peer in peers:
            pl.semaphore_signal(barrier, inc=1, device_id=peer, device_id_type=pl.DeviceIdType.MESH)
        pl.semaphore_wait(barrier, len(peers))
        for n in range(8):
            share_own(n)
        for copy in shares:
            copy.start()
        for n in range(8, len(units)):
            share_own(n)
        hops(opening)
    else:
        for n in range(len(units)):
            weight_copy(n).start()
    stat_ref[...] = jnp.zeros_like(stat_ref)

    for copy in loads:
        copy.wait()
    for copy in shares:
        copy.wait()

    def add_stat(layer, k, row_sums, valid):
        total = jnp.sum(row_sums * valid, axis=0, keepdims=True)
        stat_ref[layer, k : k + 1, :] += jnp.broadcast_to(total, (1, lanes))

    def forward_attention(layer, s):
        at = seg_rows(s)
        mask = mask_col(s)
        for p in range(pairs):
            cols = slice(p * lanes, (p + 1) * lanes)
            qp = qkv[at, cols]
            kp = qkv[at, slice(width + p * lanes, width + (p + 1) * lanes)]
            vp = qkv[at, slice(2 * width + p * lanes, 2 * width + (p + 1) * lanes)]
            outs = []
            for side in range(2):
                h = 2 * p + side
                own, marks = lane_marks(head_size, side)
                bias = bias_rows[h]
                hi = bias.astype(bf16).astype(f32)
                aux = jnp.concatenate([hi * marks[1] + (bias - hi) * marks[2], jnp.zeros((tok_rows, lanes), f32)], axis=0)
                aux = aux + mask * marks[0]
                extra = marks[0] + marks[1] + marks[2]
                ka = kp * own.astype(bf16) + aux.astype(bf16)
                qa = qp * (1.0 - extra).astype(bf16) + extra.astype(bf16)
                scores = nt(qa, ka)
                top = jnp.max(scores, axis=1, keepdims=True)
                weights = jnp.exp2(scores - top).astype(bf16)
                ebuf[s, h] = weights
                va = vp * own.astype(bf16) + (1.0 - own).astype(bf16)
                outs.append(mm(weights, va))
            own, _ = lane_marks(head_size, 0)
            raw = jnp.where(own > 0, outs[0], outs[1])
            sums = pltpu.roll(jnp.where(own > 0, outs[1], outs[0]), head_size, 1)
            inv = 1.0 / sums
            ilbuf[at, cols] = inv.astype(ilbuf.dtype)
            obuf[at, cols] = (raw * inv).astype(bf16)
            if p % 2 == 1:
                after(layer, s, "quad" + str(p // 2))

    def unpack_small(layer):
        ext[...] = mat(0, layer, slice(0, lanes)).astype(f32)
        turned = ext[...].T
        for k in range(2):
            gains[layer, k] = turned[k : k + 1, :]
        for h in range(heads):
            column = ext[pl.ds(h, slots, stride=heads), :][:, 2:3]
            bias_rows[h] = jnp.broadcast_to(column * log2_e, (slots, lanes))

    def forward_attn(layer, s):
        at = seg_rows(s)

        @pl.when(layer == 1)
        def _():
            for copy in spill_copies(s, False):
                copy.wait()

        @pl.when(layer == 0)
        def _():
            spill_copies(s, False, (7,))[0].start()

        valid = valid_col(s)
        x = ub[at, :].astype(f32)
        squares = jnp.sum(x * x, axis=1, keepdims=True)
        add_stat(layer, 0, squares, valid)
        add_stat(layer, 3, valid, valid)
        n1 = (x * lax.rsqrt(squares / width + norm_eps) * gains[layer, 0]).astype(bf16)
        for k in range(3):
            part = mm(n1, mat(0, layer, qkv_cols(k)))
            if k == 0:
                part = part * (score_scale * log2_e)
            qkv[at, k * width : (k + 1) * width] = part.astype(bf16)
        after(layer, s, "qkv")
        forward_attention(layer, s)

        @pl.when(layer == 0)
        def _():
            for copy in spill_copies(s, False, range(4)):
                copy.start()

    def ffn_part(s, layer, picks):
        at = seg_rows(s)

        def up(c):
            return mm(doa[0, at, :], mat(2, layer, slice(c * chunk, (c + 1) * chunk)))

        before = up(picks[0])
        for c in picks:
            cols = slice(c * chunk, (c + 1) * chunk)
            following = up(c + 1) if c + 1 in picks else None
            square = before * before
            gate = 0.5 + 0.5 * jnp.tanh(before * (gelu_c + (gelu_c * gelu_k) * square))
            act = before * gate
            slope[at, cols] = (gate + act * (1.0 - gate) * (2.0 * gelu_c + (6.0 * gelu_c * gelu_k) * square)).astype(bf16)
            act = act.astype(bf16)
            active[at, cols] = act
            part = mm(act, mat(3, layer, planes=slice(c, c + 1)))
            if c == 0:
                dn[at, :] = part
            else:
                dn[at, :] += part
            before = following

    def forward_ffn_a(layer, s):
        at = seg_rows(s)
        valid = valid_col(s)
        z = mm(obuf[at, :], mat(1, layer))
        add_stat(layer, 1, jnp.sum(z * z, axis=1, keepdims=True), valid)
        h = ub[at, :].astype(f32) + z
        hbuf[at, :] = h.astype(bf16)
        doa[0, at, :] = (h * lax.rsqrt(jnp.mean(h * h, axis=1, keepdims=True) + norm_eps) * gains[layer, 1]).astype(bf16)
        ffn_part(s, layer, range(ff // chunk // 2))
        after(layer, s, "ffna")

    def forward_ffn_b(layer, s):
        at = seg_rows(s)
        valid = valid_col(s)
        ffn_part(s, layer, range(ff // chunk // 2, ff // chunk))
        out = dn[at, :]
        add_stat(layer, 2, jnp.sum(out * out, axis=1, keepdims=True), valid)
        z = mm(obuf[at, :], mat(1, layer))
        result = (ub[at, :].astype(f32) + z + out).astype(bf16)

        @pl.when(layer == 0)
        def _():
            spill_copies(s, False, (7,))[0].wait()
            ub[at, :] = result

        @pl.when(layer == 1)
        def _():
            doa[1, at, :] = result

        @pl.when(layer == 0)
        def _():
            for copy in spill_copies(s, False, (4, 5, 6)):
                copy.start()

        after(layer, s, "ffnb")

    @pl.loop(0, 2)
    def _(layer):
        after(layer, 0, "open")
        need(layer, first_units)
        unpack_small(layer)

        @pl.loop(0, segs)
        def _(s):
            forward_attn(layer, s)

        after(layer, 0, "gate")
        need(layer, later_units)

        @pl.loop(0, segs)
        def _(s):
            forward_ffn_a(layer, s)

        after(layer, 0, "last")
        need(layer, last_units)

        @pl.loop(0, segs)
        def _(s):
            forward_ffn_b(layer, s)

    if routed:
        for n in range(len(units)):
            drain(n)
    for copies in y_copies:
        for copy in copies:
            copy.start()

    if routed:
        wqa_u, wo_u, wu_u, wd_u, wqb_u = range(5)
        half_cols = quads * 3 * lanes
        rs_cols = {wqa_u: slice(0, half_cols), wqb_u: slice(half_cols, 2 * half_cols + lanes)}
        rs_weight = (0, 1, 2, 3, 0)
        chunked = (wu_u, wd_u)
        fast = (wqa_u, wqb_u)
        plane_peers = [near_x, near_y, (core, place(z, 1 - y, 1 - x))]
        plane_spots = [(y, 1 - x), (1 - y, x), (1 - y, 1 - x)]
        chunks = ff // chunk

        def rs_copy(src, dst, layer, u, k, target):
            return pltpu.make_async_remote_copy(
                src_ref=src,
                dst_ref=dst,
                send_sem=rs_send.at[layer, u, k],
                recv_sem=rs_recv.at[layer, u, k],
                device_id=target,
                device_id_type=pl.DeviceIdType.MESH,
            )

        def chunk_cols(c):
            return slice(c * chunk, (c + 1) * chunk)

        def spot(layer, u, pz, py, px, c, piece=None):
            cols = rs_cols.get(u, every)
            if piece is not None and u == wd_u:
                pz = piece
            elif piece is not None:
                cols = chunk_cols(piece)
            return weight_buf[rs_weight[u]].at[layer + 1, pz, py, px, c, every, cols]

        def land_at(u, step, piece=None):
            ref = lands[u][step]
            if piece is None:
                return ref
            if u == wd_u:
                return ref.at[piece % 2 if step == 0 else piece]
            if step == 0:
                return ref.at[every, every, every, every, chunk_cols(piece % 2)]
            return ref.at[every, every, every, chunk_cols(piece)]

        def rs_copies(layer, u, step, y_first, piece=None):
            if step == 0:
                src = spot(layer, u, every, every, every, other, piece)
                return [rs_copy(src, land_at(u, 0, piece), layer, u, piece or 0, mate)]
            if step == 1 and u in fast:
                return [
                    rs_copy(spot(layer, u, every, *plane_spots[k], core), lands[u][1].at[k], layer, u, 4 + k, plane_peers[k])
                    for k in range(3)
                ]
            if step == 3 and u in fast:
                return [owner_copy(layer, u, k) for k in range(4)]
            if step == 1:
                at = (every, 1 - y, every) if y_first else (every, every, 1 - x)
                src = spot(layer, u, *at, core, piece)
                return [rs_copy(src, land_at(u, 1, piece), layer, u, 4 + (piece or 0), near_y if y_first else near_x)]
            if step == 2:
                at = (every, y, 1 - x) if y_first else (every, 1 - y, x)
                return [rs_copy(spot(layer, u, *at, core), lands[u][2], layer, u, 8, near_x if y_first else near_y)]
            if step == 3:
                return [
                    rs_copy(spot(layer, u, (z + k) % 4, y, x, core), lands[u][3].at[k - 1], layer, u, 8 + k, along_z[k - 1])
                    for k in range(1, 4)
                ]
            return [rs_copy(src, dst, layer, u, 12 + k, mate) for k, (src, dst) in enumerate(home_parts(layer, u))]

        def owner_copy(layer, u, k, half=None):
            away = (z + k + 1) % 4 if k < 3 else z
            half = core if half is None else half
            return pltpu.make_async_remote_copy(
                src_ref=spot(layer, u, away, y, x, core),
                dst_ref=lands[u][3].at[half, k],
                send_sem=rs_send.at[layer, u, 9 + k],
                recv_sem=rs_recv.at[layer, u, 9 + 4 * half + k],
                device_id=(layer, place(away, y, x)),
                device_id_type=pl.DeviceIdType.MESH,
            )

        def start_owner(layer, u):
            for k in range(3):
                owner_copy(layer, u, k).start()

            @pl.when(core != layer)
            def _():
                owner_copy(layer, u, 3).start()

        def merge_owner(layer, u):
            @pl.when(core == layer)
            def _():
                for k in range(3):
                    owner_copy(layer, u, k, layer).wait_recv()
                for k in range(4):
                    owner_copy(layer, u, k, 1 - layer).wait_recv()
                got = lands[u][3]
                cols = rs_cols[u]
                for half in range(2):
                    if half == layer:
                        total = weight_buf[0][layer + 1, z, y, x, half, :, cols].astype(f32)
                    else:
                        total = got[half, 3].astype(f32)
                    for k in range(3):
                        total = total + got[half, k].astype(f32)
                    if u == wqb_u:
                        small = total[:, :lanes].T
                        turned = jnp.concatenate([small[:8, :], jnp.zeros((8, lanes - small.shape[1]), f32)], axis=1)
                        fin[u][half, 0:8, 0:lanes] = turned
                        fin[u][half, :, lanes:] = total[:, lanes:]
                    else:
                        fin[u][half] = total
                for k, (src, dst) in enumerate(home_parts(layer, u)):
                    pltpu.make_async_copy(src, dst, sem_g.at[layer, u, k]).start()

        def home_parts(layer, u):
            if u not in rs_cols:
                return [(fin[u], grads_out[u].at[core])]
            base, q = (0, 0) if u == wqa_u else (lanes, 1)
            parts = [
                (
                    fin[u].at[:, :, base + k * quad : base + (k + 1) * quad],
                    grads_out[0].at[:, :, k * width + q * quad : k * width + (q + 1) * quad],
                )
                for k in range(3)
            ]
            if u == wqb_u:
                parts.append((fin[u].at[:, 0:8, 0:lanes], grads_out[4]))
            return parts

        def rs_route(u, act):
            for side in range(2):
                @pl.when(core == side)
                def _(side=side):
                    act((side + u) % 2 == 0)

        def on_route(u, step, act):
            if step in (1, 2):
                rs_route(u, act)
            else:
                act(True)

        def rs_pieces(u, step):
            return list(range(chunks)) if u in chunked and step < 2 else [None]

        def rs_start(layer, u, step, piece=None):
            if step == 3 and u in fast:
                start_owner(layer, u)
                return
            used = layer == 0 and not piece
            if step == 0 and u in chunked:
                used = layer == 0 or piece >= 2
            if used and step < 4:
                pl.semaphore_wait(rs_free.at[u, step], 3 if step == 3 or (step == 1 and u in fast) else 1)

            def act(y_first):
                for copy in rs_copies(layer, u, step, y_first, piece):
                    copy.start()

            on_route(u, step, act)

        def give_back(u, step):
            def act(y_first):
                if step == 0:
                    peers = [mate]
                elif step == 3:
                    peers = along_z
                elif u in fast:
                    peers = plane_peers
                else:
                    peers = [near_y if y_first == (step == 1) else near_x]
                for peer in peers:
                    pl.semaphore_signal(rs_free.at[u, step], inc=1, device_id=peer, device_id_type=pl.DeviceIdType.MESH)

            on_route(u, step, act)

        def rs_merge(layer, u, step, piece=None):
            if step == 3 and u in fast:
                merge_owner(layer, u)
                return

            def act(y_first):
                for wait_piece in [piece] if step == 0 else rs_pieces(u, step):
                    for copy in rs_copies(layer, u, step, y_first, wait_piece):
                        copy.wait_recv()

            on_route(u, step, act)
            slot = layer + 1
            buf, got = weight_buf[rs_weight[u]], lands[u][step]
            cols = rs_cols.get(u, every)
            if step == 3:
                if layer == 0:
                    rs_home(1, u)
                total = buf[slot, z, y, x, core, :, cols].astype(f32)
                for k in range(3):
                    total = total + got[k].astype(f32)
                fin[u][...] = total
                if layer == 1:
                    give_back(u, 3)

                @pl.when(core == layer)
                def _():
                    for k, (src, dst) in enumerate(home_parts(layer, u)):
                        pltpu.make_async_copy(src, dst, sem_g.at[layer, u, k]).start()

                @pl.when(core != layer)
                def _():
                    rs_start(layer, u, 4)

                return
            if step == 0 and piece is not None and u == wd_u:
                buf[slot, piece, :, :, core] += got[piece % 2]
            else:
                got_cols = every
                if step == 0 and piece is not None:
                    cols, got_cols = chunk_cols(piece), chunk_cols(piece % 2)

                @pl.loop(0, 4)
                def _(pz):
                    if step == 0:
                        buf[slot, pz, :, :, core, :, cols] += got[pz, :, :, :, got_cols]
                    elif u in fast:
                        total = buf[slot, pz, y, x, core, :, cols].astype(f32)
                        for k in range(3):
                            total = total + got[k, pz].astype(f32)
                        buf[slot, pz, y, x, core, :, cols] = total.astype(bf16)
                    elif step == 2:
                        buf[slot, pz, y, x, core, :, cols] += got[pz]
                    else:
                        def add(y_first):
                            if y_first:
                                buf[slot, pz, y, :, core, :, cols] += got[pz]
                            else:
                                buf[slot, pz, :, x, core, :, cols] += got[pz]

                        rs_route(u, add)

            if layer == 1 or (step == 0 and u in chunked and piece < 2):
                give_back(u, step)
            rs_start(layer, u, 3 if u in fast and step == 1 else step + 1, piece)

        def rs_home(layer, u):
            @pl.when(core == layer)
            def _():
                for k, (src, dst) in enumerate(home_parts(layer, u)):
                    pltpu.make_async_copy(src, dst, sem_g.at[layer, u, k]).wait()
                if u not in fast:
                    for copy in rs_copies(layer, u, 4, True):
                        copy.wait_recv()

            if u not in fast:
                @pl.when(core != layer)
                def _():
                    for copy in rs_copies(layer, u, 4, True):
                        copy.wait_send()

        def rs_finish(layer, u):
            if u in fast:
                for step in range(2):
                    for copy in rs_copies(layer, u, step, True):
                        copy.wait_send()
                for k in range(3):
                    owner_copy(layer, u, k).wait_send()

                @pl.when(core != layer)
                def _():
                    owner_copy(layer, u, 3).wait_send()

                return
            for step in range(4):
                def act(y_first, step=step):
                    for piece in rs_pieces(u, step):
                        for copy in rs_copies(layer, u, step, y_first, piece):
                            copy.wait_send()

                on_route(u, step, act)

        def stat_copy(step, k=0):
            target = (mate, near_y, near_x)[step] if step < 3 else along_z[k]
            place_at = step if step < 3 else 3 + z
            return pltpu.make_async_remote_copy(
                src_ref=stat_sum.at[step],
                dst_ref=stat_land.at[place_at],
                send_sem=stat_send.at[step + k],
                recv_sem=stat_recv.at[step + k],
                device_id=target,
                device_id_type=pl.DeviceIdType.MESH,
            )

        def stat_step(step):
            if step == 0:
                stat_sum[0] = stat_ref[...]
            elif step < 4:
                stat_copy(step - 1).wait()
                stat_sum[step] = stat_sum[step - 1] + stat_land[step - 1]
            if step < 3:
                stat_copy(step).start()
            elif step == 3:
                stat_land[3 + z] = stat_sum[3]
                for k in range(3):
                    stat_copy(3, k).start()
            else:
                for k in range(3):
                    stat_copy(3, k).wait()
                total = stat_land[3] + stat_land[4] + stat_land[5] + stat_land[6]
                stat_ref[...] = total
                stat_done()

        stat_step(0)
        names = dict(a=wqa_u, o=wo_u, u=wu_u, d=wd_u, b=wqb_u)

        def run_events(layer, text):
            for word in text.split():
                if word[0] == "t":
                    stat_step(int(word[1]))
                    continue
                at_layer = layer
                if word[0] == "p":
                    at_layer, word = layer + 1, word[1:]
                step, u = int(word[1]), names[word[2]]
                piece = int(word[3]) if len(word) > 3 else None
                (rs_start if word[0] == "S" else rs_merge)(at_layer, u, step, piece)

        back_points = {
            (1, "ffn0"): "t1 S0d0 S0u0",
            (1, "ffn1"): "t2 M0d0 M0u0 S0d1 S0u1",
            (1, "ffn2"): "t3 M0d1 M0u1 S0d2 S0u2",
            (1, "ffn3"): "t4 M0d2 M0u2 S0d3 S0u3",
            (1, "mid"): "M0d3 M0u3",
            (1, "wo"): "S0o",
            (1, "att00"): "M0o",
            (1, "att01"): "M1d M1u",
            (1, "wq0"): "S0a",
            (1, "att10"): "M0a M1o",
            (1, "att11"): "M2d M2u",
            (1, "wq1"): "S0b",
            (1, "in0"): "M0b M2o",
            (1, "in1"): "M1a",
            (0, "ffn0"): "S0d0 S0u0",
            (0, "ffn1"): "M0d0 M0u0 S0d1 S0u1 pM1b pM3d pM3u",
            (0, "ffn2"): "M0d1 M0u1 S0d2 S0u2 pM3o pM3a",
            (0, "ffn3"): "M0d2 M0u2 S0d3 S0u3 pM3b",
            (0, "mid"): "M0d3 M0u3",
            (0, "wo"): "S0o",
            (0, "att00"): "M0o",
            (0, "att01"): "M1d M1u",
            (0, "wq0"): "S0a",
            (0, "att10"): "M0a M1o",
            (0, "att11"): "M2d M2u",
            (0, "wq1"): "S0b M1a M0b",
            (0, "in0"): "M2o",
            (0, "end"): "M3d M3u M1b M3o M3a M3b",
        }
    else:
        back_points = {}

    def stat_done():
        totals = stat_ref[...]
        stat_out[...] = totals if not routed else jnp.sqrt(totals / (totals[0:1, 3:4, :] * width))

    if not routed:
        stat_done()

    def back_point(layer, point, s=None, at=None):
        for (at_layer, at_point), text in back_points.items():
            if at_point == point:
                here = layer == at_layer
                if s is not None:
                    here = here & (s == at)

                @pl.when(here)
                def _(at_layer=at_layer, text=text):
                    run_events(at_layer, text)

    def norm_back(x, gain, grad):
        inv = lax.rsqrt(jnp.mean(x * x, axis=1, keepdims=True) + norm_eps)
        hat = x * inv
        scaled = grad * gain
        return inv * (scaled - hat * jnp.mean(scaled * hat, axis=1, keepdims=True))

    def add_gain(k, d_weight, weight):
        for p in range(d_weight.shape[1] // lanes):
            cols = slice(p * lanes, (p + 1) * lanes)
            gain_sums[k] += d_weight[:, cols] * weight[:, cols].astype(f32)

    def pack_small(layer):
        turned = dbias[...].T
        for h in range(heads):
            ext[pl.ds(h, slots, stride=heads), :] = jnp.broadcast_to(turned[:slots, h : h + 1], (slots, lanes))
        lane = lax.broadcasted_iota(jnp.int32, (width, lanes), 1)
        gain = mat(0, layer, slice(0, lanes)).astype(f32)
        sums = [jnp.sum(gain_sums[k], axis=1, keepdims=True) for k in range(2)]
        safe = jnp.where(lane < 2, gain, 1.0)
        value = jnp.where(lane == 0, sums[0], jnp.where(lane == 1, sums[1], 0.0)) / safe
        value = jnp.where(lane == 2, ext[...], value)
        put_mat(0, layer + 1, value.astype(bf16), slice(3 * quad, 3 * quad + lanes))

    def backward_ffn(layer):
        slot = layer + 1

        @pl.loop(0, segs)
        def _(s):
            at = seg_rows(s)
            h = hbuf[at, :].astype(f32)
            doa[0, at, :] = (h * lax.rsqrt(jnp.mean(h * h, axis=1, keepdims=True) + norm_eps) * gains[layer, 1]).astype(bf16)

        dn[...] = jnp.zeros_like(dn)
        gain_sums[...] = jnp.zeros_like(gain_sums)
        dbias[...] = jnp.zeros_like(dbias)
        turned_cols = slice(0, segs * rows)
        put_mat(0, slot, doa[0].T, turned_cols)

        @pl.loop(0, ff // chunk)
        def _(c):
            cols = pl.ds(pl.multiple_of(c * chunk, chunk), chunk)
            planes = pl.ds(c, 1)
            d_pre = (nt(dy[...], mat(3, layer, planes=planes)) * slope[:, cols].astype(f32)).astype(bf16)
            put_mat(3, slot, tn(active[:, cols], dy[...]).astype(bf16), planes=planes)
            d_up = mm(mat(0, slot, turned_cols), d_pre)
            add_gain(1, d_up, mat(2, layer, cols))
            put_mat(2, slot, d_up.astype(bf16), cols)
            dn[...] += nt(d_pre, mat(2, layer, cols))
            for k in range(ff // chunk):
                back_point(layer, "ffn" + str(k), c, k)

    def backward_middle(layer, s):
        at = seg_rows(s)
        dh = norm_back(hbuf[at, :].astype(f32), gains[layer, 1], dn[at, :])
        dh = dh + dy[at, :].astype(f32)
        dn[at, :] = dh
        dz = dh.astype(bf16)
        dy[at, :] = dz
        do = nt(dz, mat(1, layer)) * ilbuf[at, :].astype(f32)
        prod = do.astype(bf16).astype(f32) * obuf[at, :].astype(f32)
        for p in range(pairs):
            cols = slice(p * lanes, (p + 1) * lanes)
            for side in range(2):
                own, marks = lane_marks(head_size, side)
                delta = -jnp.sum(prod[:, cols] * own, axis=1, keepdims=True)
                hi = delta.astype(bf16).astype(f32)
                fill = hi * marks[0] + (delta - hi) * marks[1]
                doa[side, at, cols] = (do[:, cols] * (1.0 - marks[0] - marks[1]) + fill).astype(bf16)

    def backward_attention(layer, q, s):
        at = seg_rows(s)
        for p in range(2):
            cols, kcols, vcols = (
                pl.ds(pl.multiple_of(k * width + q * quad + p * lanes, lanes), lanes) for k in range(3)
            )
            qp = qkv[at, cols]
            kp = qkv[at, kcols]
            vp = qkv[at, vcols]
            q_turned = qp.T
            dq, dk, dv = [], [], []
            for side in range(2):
                h = 4 * q + 2 * p + side
                own, marks = lane_marks(head_size, side)
                do_h = doa[side, at, cols]
                va = vp * own.astype(bf16) + (marks[0] + marks[1]).astype(bf16)
                weights = ebuf[s, h]
                d_scores = weights.astype(f32) * nt(do_h, va)
                dbias[pl.ds(h, 1), :] += jnp.sum(d_scores[:, :lanes], axis=0, keepdims=True)
                d_scores = d_scores.astype(bf16)
                half = slice(side * head_size, (side + 1) * head_size)
                dq.append(mm(d_scores, kp))
                dk.append(mm(q_turned[half, :], d_scores))
                dv.append(mm(do_h.T[half, :], weights))
            own, _ = lane_marks(head_size, 0)
            qkv[at, cols] = (jnp.where(own > 0, dq[0], dq[1]) * score_scale).astype(bf16)
            qkv[at, kcols] = (jnp.concatenate(dk, axis=0).T * (1.0 / log2_e)).astype(bf16)
            qkv[at, vcols] = jnp.concatenate(dv, axis=0).T.astype(bf16)

    def backward_input(layer, s):
        at = seg_rows(s)
        x = ub[at, :].astype(f32)
        du = norm_back(x, gains[layer, 0], nt(qkv[at, :], mat(0, layer, slice(lanes, lanes + 3 * width))))
        dy[at, :] = (du + dn[at, :]).astype(bf16)

    def grad_col(q, k):
        return q * (3 * quad + lanes) + k * quad

    def grad_copies(layer):
        return [
            pltpu.make_async_copy(buf.at[layer + 1], out.at[layer], sem_g.at[layer, k, 0])
            for k, (buf, out) in enumerate(zip(weight_buf, grads_out))
        ]

    @pl.loop(0, 2)
    def _(step):
        layer = 1 - step
        slot = layer + 1

        @pl.when(layer == 0)
        def _():
            for s in range(segs):
                for copy in spill_copies(s, True, (2, 3, 4, 5, 6)):
                    copy.wait()

        backward_ffn(layer)

        @pl.when(layer == 1)
        def _():
            for copies in y_copies:
                for copy in copies:
                    copy.wait()

        @pl.loop(0, segs)
        def _(s):
            backward_middle(layer, s)

        back_point(layer, "mid")
        put_mat(1, slot, tn(obuf[...], dy[...]).astype(bf16))
        back_point(layer, "wo")

        @pl.when(layer == 1)
        def _():
            for s in range(segs):
                for copy in spill_copies(s, True, (2, 3, 4, 5, 6)):
                    copy.start()

        @pl.loop(0, segs)
        def _(s):
            at = seg_rows(s)

            @pl.when(layer == 0)
            def _():
                spill_copies(s, True, (7,))[0].wait()

            v = ub[at, :].astype(f32)
            dy[at, :] = (v * lax.rsqrt(jnp.mean(v * v, axis=1, keepdims=True) + norm_eps) * gains[layer, 0]).astype(bf16)

        @pl.loop(0, quads)
        def _(q):
            @pl.loop(0, segs)
            def _(s):
                @pl.when((layer == 0) & (q == 0))
                def _():
                    for copy in spill_copies(s, True, (0, 1)):
                        copy.wait()

                backward_attention(layer, q, s)

                @pl.when((layer == 1) & (q == quads - 1))
                def _():
                    spill_copies(s, True, (1,))[0].start()

                for i in range(quads):
                    for k in range(segs):
                        back_point(layer, "att" + str(i) + str(k), q * segs + s, i * segs + k)

            for k in range(3):
                d_weight = tn(dy[...], qkv[:, pl.ds(pl.multiple_of(k * width + q * quad, quad), quad)])
                add_gain(0, d_weight, mat(0, layer, pl.ds(pl.multiple_of(lanes + k * width + q * quad, lanes), quad)))
                put_mat(0, slot, d_weight.astype(bf16), pl.ds(pl.multiple_of(grad_col(q, k), lanes), quad))

            @pl.when(q == quads - 1)
            def _():
                pack_small(layer)

            for i in range(quads):
                back_point(layer, "wq" + str(i), q, i)

        @pl.loop(0, segs)
        def _(s):
            backward_input(layer, s)
            for k in range(segs):
                back_point(layer, "in" + str(k), s, k)

        @pl.when(layer == 1)
        def _():
            for s in range(segs):
                for copy in spill_copies(s, True, (0, 7)):
                    copy.start()

        if not routed:
            for copy in grad_copies(layer):
                copy.start()
            for copy in grad_copies(layer):
                copy.wait()

    for copies in du_copies:
        for copy in copies:
            copy.start()
    back_point(0, "end")
    if routed:
        for layer in (1, 0):
            for u in range(5):
                rs_finish(layer, u)
    if routed:
        for u in range(5):
            rs_home(0, u)
        for u in (0, 4):
            rs_home(1, u)
    for copies in du_copies:
        for copy in copies:
            copy.wait()


def run_layers(dims, routed, doc_len, row_args, weights):
    segs, rows, width, ff, slots, heads, per_doc = dims
    all_rows = segs * rows
    vmem = pl.BlockSpec(memory_space=pltpu.VMEM)
    smem = pl.BlockSpec(memory_space=pltpu.SMEM)
    hbm = pl.BlockSpec(memory_space=pl.ANY)
    shape = jax.ShapeDtypeStruct
    dma = pltpu.SemaphoreType.DMA
    wide = (all_rows, width)
    tiles = [
        (width // 32, lanes + 3 * width),
        (width // 32, width),
        (width // 32, ff),
        (ff // 32, width),
    ]
    out_shape = [shape(part.shape, bf16) for part in row_args]
    if routed:
        out_shape += [shape((2, width // 32, 3 * width), f32)]
        out_shape += [shape((2, *tile), f32) for tile in tiles[1:]]
        out_shape += [shape((2, 8, lanes), f32)]
    else:
        out_shape += [shape((2, 4, 2, 2, 2, *tile), bf16) for tile in tiles]
    row_outs = len(out_shape)
    out_shape += [shape((2, 8, lanes), f32)]
    out_shape += [
        shape((all_rows, 3 * width), bf16),
        shape((segs, heads, rows, rows), bf16),
        shape(wide, bf16),
        shape(wide, bf16),
        shape((all_rows, ff), bf16),
        shape((all_rows, ff), bf16),
        shape(wide, bf16),
        shape(wide, bf16),
    ]
    unit_count = 16
    scratch = [pltpu.VMEM((3, 4, 2, 2, 2, *tile), bf16) for tile in tiles]
    scratch += [
        pltpu.VMEM(wide, bf16),
        pltpu.VMEM(wide, bf16),
        pltpu.VMEM((all_rows, 3 * width), bf16),
        pltpu.VMEM((segs, heads, rows, rows), bf16),
        pltpu.VMEM(wide, bf16),
        pltpu.VMEM(wide, bf16),
        pltpu.VMEM(wide, bf16),
        pltpu.VMEM((all_rows, ff), bf16),
        pltpu.VMEM((all_rows, ff), bf16),
        pltpu.VMEM((2, *wide), bf16),
        pltpu.VMEM(wide, f32),
        pltpu.VMEM((2, 2, 1, width), f32),
        pltpu.VMEM((heads, slots, lanes), f32),
        pltpu.VMEM((width, lanes), f32),
        pltpu.VMEM((2, width, lanes), f32),
        pltpu.VMEM((heads, lanes), f32),
        pltpu.VMEM((2, 8, lanes), f32),
        dma((segs, 8)),
        dma((segs, 8)),
        dma((2, 5, 4)),
        dma((8 * segs,)),
        dma((unit_count, 2)),
        dma((unit_count, 12)),
        dma((unit_count, 12)),
    ]
    params = dict(vmem_limit_bytes=127 * 2**19)
    if routed:
        params.update(collective_id=0, has_side_effects=True)
        half_cols = 3 * width // 2
        rs_tiles = [(width // 32, half_cols), *tiles[1:], (width // 32, half_cols + lanes)]
        first_tiles = [(4, 2, 2, *tile) for tile in rs_tiles]
        first_tiles[2] = (4, 2, 2, width // 32, 2 * chunk)
        first_tiles[3] = (2, 2, 2, ff // 32, width)
        for u, (first, tile) in enumerate(zip(first_tiles, rs_tiles)):
            leads = ((3, 4), (1,), (2, 4)) if u in (0, 4) else ((4, 2), (4,), (3,))
            scratch += [pltpu.VMEM(first, bf16)]
            scratch += [pltpu.VMEM((*lead, *tile), bf16) for lead in leads]
        scratch += [pltpu.VMEM((2, *tile) if u in (0, 4) else tile, f32) for u, tile in enumerate(rs_tiles)]
        scratch += [
            pltpu.VMEM((4, 2, 8, lanes), f32),
            pltpu.VMEM((7, 2, 8, lanes), f32),
            dma((2, 5, 17)),
            dma((2, 5, 17)),
            pltpu.SemaphoreType.REGULAR((5, 4)),
            dma((8 * segs,)),
            dma((8 * segs,)),
            dma((6,)),
            dma((6,)),
        ]
    return pl.pallas_call(
        partial(fused_layers, dims, routed),
        out_shape=out_shape,
        in_specs=[smem] + [hbm] * (len(row_args) + len(weights)),
        out_specs=[hbm] * row_outs + [vmem] + [hbm] * (len(out_shape) - row_outs - 1),
        scratch_shapes=scratch,
        compiler_params=pltpu.CompilerParams(**params),
    )(doc_len, *row_args, *weights)[: row_outs + 1]


def settle_kernel(*refs):
    count = (len(refs) - 7) // 3
    srcs, (small, stats) = refs[:count], refs[count : count + 2]
    dsts = refs[count + 2 : 2 * count + 2]
    vectors, rms = refs[2 * count + 2 : 2 * count + 5], refs[2 * count + 5]
    mids, sems = refs[2 * count + 6 : -1], refs[-1]
    inward = [pltpu.make_async_copy(src, mid, sems.at[0, k]) for k, (src, mid) in enumerate(zip(srcs, mids))]
    outward = [pltpu.make_async_copy(mid, dst, sems.at[1, k]) for k, (mid, dst) in enumerate(zip(mids, dsts))]
    for copy in inward:
        copy.start()
    for k, vector in enumerate(vectors):
        size = vector.shape[1] // 2
        vector[...] = jnp.concatenate([small[half, k : k + 1, :size] for half in range(2)], axis=1)
    lane = lax.broadcasted_iota(jnp.int32, (1, lanes), 1)
    for layer in range(2):
        row = sum(jnp.where(lane == k, stats[layer, k : k + 1, :], 0.0) for k in range(3))
        rms[layer : layer + 1, :] = row[:, :3]
    for into, out in zip(inward, outward):
        into.wait()
        out.start()
    for out in outward:
        out.wait()


def settle(big, small, stats):
    vmem = pl.BlockSpec(memory_space=pltpu.VMEM)
    hbm = pl.BlockSpec(memory_space=pl.ANY)
    shape = jax.ShapeDtypeStruct
    size = 2 * big[4].shape[1]
    return pl.pallas_call(
        settle_kernel,
        out_shape=[shape(part.shape, part.dtype) for part in big] + [shape((1, size), f32)] * 3 + [shape((2, 3), f32)],
        in_specs=[hbm] * len(big) + [vmem] * 2,
        out_specs=[hbm] * len(big) + [vmem] * 4,
        scratch_shapes=[pltpu.VMEM(part.shape, part.dtype) for part in big] + [pltpu.SemaphoreType.DMA((2, len(big)))],
    )(*big, small, stats)


def swap(block):
    return lax.ppermute(block, "section", [(0, 1), (1, 0)])


def body(
    tokens,
    memory,
    lengths,
    w_qkv,
    w_out,
    w_up,
    w_down,
    gain_attn,
    gain_ffn,
    forget_bias,
    grad_tokens,
    grad_memory,
):
    section = lax.axis_index("section")
    is_first = section == 0
    micro = tokens.shape[0]
    segs = micro // 2
    half_tok = tokens.shape[1]
    half_mem = memory.shape[1]
    slots = 2 * half_mem
    rows = slots + 2 * half_tok
    width = tokens.shape[2]
    ff = w_up.shape[2]
    heads = forget_bias.shape[1] * lax.axis_size("dp") // slots
    per_doc = micro // lengths.shape[0]
    dims = (segs, rows, width, ff, slots, heads, per_doc)
    small = jnp.stack([gain_attn, gain_ffn, forget_bias], axis=2)
    small = jnp.pad(small, ((0, 0), (0, 0), (0, lanes - 3)))

    if lax.axis_size("dp") == 16 and w_qkv.shape[1] == 32:
        pieces = (w_qkv, w_out, w_up, w_down, small)
        weights = [piece.reshape(2, -1, piece.shape[2]) for piece in pieces]
        row_args = (tokens, memory, grad_tokens, grad_memory)
        *outs, small_grads, stats = run_layers(dims, True, lengths, row_args, weights)
        outs = settle(outs, small_grads, stats)
        mats = [grad.reshape(1, -1, grad.shape[2]) for grad in outs[4:8]]
        return (*outs[:4], *mats, *outs[8:])

    own_len = lax.dynamic_slice_in_dim(lengths, section * segs // per_doc, segs // per_doc, 0)
    pieces = (jnp.concatenate([small, w_qkv], axis=2), w_out, w_up, w_down)

    def unpack(grads):
        mat = grads[0]
        half = 3 * width // 2
        parts = [mat[:, :, :half], mat[:, :, half + lanes :]]
        parts = [part.reshape(1, -1, 3, width // 2) for part in parts]
        whole = jnp.concatenate(parts, axis=3).reshape(1, -1, 3 * width)
        return (whole, *grads[1:], *(mat[:, :, half + k] for k in range(3)))

    def own_segs(halves):
        return lax.dynamic_slice_in_dim(halves, section * segs, segs, 0)

    def other_segs(halves):
        return lax.dynamic_slice_in_dim(halves, (1 - section) * segs, segs, 0)

    def both(kept, got):
        return jnp.concatenate(
            [jnp.where(is_first, kept, got), jnp.where(is_first, got, kept)], axis=1
        )

    inputs = (tokens, memory, grad_tokens, grad_memory)
    got = swap(tuple(other_segs(part) for part in inputs))
    full = [both(own_segs(part), other) for part, other in zip(inputs, got)]
    u0 = jnp.concatenate([full[1], full[0]], axis=1).reshape(segs * rows, width)
    dout = jnp.concatenate([full[3], full[2]], axis=1).reshape(segs * rows, width)

    def gather(piece):
        whole = lax.all_gather(piece, ("section", "dp"), axis=1, tiled=True)
        return whole.reshape(2, 4, 2, 2, 2, -1, piece.shape[2])

    y, du, *grads, stats = run_layers(dims, False, own_len, (u0, dout), [gather(piece) for piece in pieces])

    def scatter(grad):
        grad = grad.reshape(2, -1, grad.shape[-1])
        mine = lax.dynamic_index_in_dim(grad, section, 0, keepdims=True)
        other = lax.dynamic_index_in_dim(grad, 1 - section, 0, keepdims=True)
        chip = (mine.astype(f32) + swap(other).astype(f32)).astype(grad.dtype)
        return lax.psum_scatter(chip, "dp", scatter_dimension=1, tiled=True).astype(f32)

    shares = unpack([scatter(grad) for grad in grads])
    totals = lax.psum(stats[:, :4, 0], ("section", "dp"))
    rms = jnp.sqrt(totals[:, :3] / (totals[0, 3] * width))
    result = jnp.stack([y.reshape(segs, rows, width), du.reshape(segs, rows, width)])

    def half_of(which):
        tok = lax.dynamic_slice_in_dim(result, slots + which * half_tok, half_tok, 2)
        mem = lax.dynamic_slice_in_dim(result, which * half_mem, half_mem, 2)
        return tok, mem

    kept = half_of(section)
    got = swap(half_of(1 - section))

    def order(mine, other):
        return jnp.concatenate(
            [jnp.where(is_first, mine, other), jnp.where(is_first, other, mine)], axis=0
        )

    toks = [order(kept[0][k], got[0][k]) for k in range(2)]
    mems = [order(kept[1][k], got[1][k]) for k in range(2)]
    return (toks[0], mems[0], toks[1], mems[1], *shares, rms)


def solution(mesh):
    rows = P("dp", "section", None)
    mats = P("section", "dp", None)
    vecs = P("section", "dp")
    return jax.shard_map(
        body,
        mesh=mesh,
        in_specs=(rows, rows, P("dp"), mats, mats, mats, mats, vecs, vecs, vecs, rows, rows),
        out_specs=(rows, rows, rows, rows, mats, mats, mats, mats, vecs, vecs, vecs, P()),
        check_vma=False,
    )
```

time: 231 us -> 199 us (0.86)
  Pallas kernels: 215 us -> 196 us
  local copies, waits for them, and re-layouts: 12.6 us -> 0.71 us
    pallas_call x1, Pallas kernels: 215 us -> 192 us  [run_layers(): pl.pallas_call(partial(fused_layers, dims, routed), out_shape=out_shape,...]
    unnamed x20 -> x1, local copies, waits for them, and re-layouts: 6.76 us -> 0.1 us
    slice x3 -> x0, local copies, waits for them, and re-layouts: 4.62 us -> none  [the longest x1 1.62 us: unpack(): grad_q[:, :, lanes:]]
    pallas_call x0 -> x1, Pallas kernels: none -> 4.31 us  [settle(): pl.pallas_call(settle_kernel, out_shape=[shape(part.shape, part.dtype) fo...]
where the time goes in v4:
time: 199 us
  Pallas kernels  196 us (98%)
    pallas_call x1, Pallas kernels, run_layers(): pl.pallas_call(partial(fused_layers, dims, routed), out_shape=out_shape,...  192 us
    pallas_call x1, Pallas kernels, settle(): pl.pallas_call(settle_kernel, out_shape=[shape(part.shape, part.dtype) fo...  4.31 us

profile of v4, /device:TPU:0, one launch (start us, length us, event | category | flops | bytes accessed | tf_op | source)
XLA Modules:
  0.0 198.6 jit_solution(12660384901085156950)
XLA Ops:
  0.6 0.7 pad_maximum_fusion
  1.3 0.1 copy.25
  1.4 0.6 pad.4.clone
  2.1 192.0 %shard_map.211 = (bf16[4,256,512]{2,1,0:T(8,128)(2,1)}, bf16[4,32,512]{2,1,0:T(8,128)(2,1)}, bf16[4,256,512]{2,1,0:T(8,128)(2,1)}, bf16[4,32,512]{2,1,0:T(8,128)...) custom-call(s32[2]{0:T(128)} %refs_0_.1, ...), custom_call_target="tpu_custom_call" | custom-call | tf_op jit(solution)/shard_map/pallas_call | solution.py:1271
  194.1 4.3 %shard_map.212 = (bf16[4,256,512]{2,1,0:T(8,128)(2,1)}, bf16[4,32,512]{2,1,0:T(8,128)(2,1)}, bf16[4,256,512]{2,1,0:T(8,128)(2,1)}, bf16[4,32,512]{2,1,0:T(8,128)...) custom-call(bf16[4,256,512]{2,1,0:T(8,128)(2,1)} %get-tuple-element., ...), custom_call_target="tpu_custom_call" | custom-call | tf_op jit(solution)/shard_map/pallas_call | solution.py:1310

commit v5 on v4

--- a/solution.py
+++ b/solution.py
@@ -58,12 +58,12 @@
     weight_buf = take(4)
     ub, dy, qkv, ebuf, obuf, ilbuf, hbuf, slope, active, doa, dn = take(11)
     gains, bias_rows, ext, gain_sums, dbias, stat_ref = take(6)
-    sem_spill, sem_back, sem_g, sem_io, sem_own, sem_send, sem_recv = take(7)
+    sem_spill, sem_back, sem_g, sem_io, sem_send, sem_recv = take(6)
     if routed:
         lands = [take(4) for _ in range(5)]
         fin = take(5)
         stat_sum, stat_land = take(2)
-        rs_send, rs_recv, rs_free, io_send, io_recv, stat_send, stat_recv = take(7)
+        rs_send, rs_recv, rs_free, stat_send, stat_recv = take(5)
     head_size = width // heads
     pairs = width // lanes
     tok_rows = rows - slots
@@ -71,6 +71,9 @@
     quad = 2 * lanes
     first_doc = lax.axis_index("section") * segs // per_doc if routed else 0
     every = slice(None)
+
+    def wait_bytes(ref, sem):
+        pltpu.make_async_copy(ref, ref, sem).wait()
 
     def units_of(layer):
         half_ff, half_deep = ff // 2, ff // 64
@@ -109,14 +112,19 @@
         along_z = [(core, place((z + k) % 4, y, x)) for k in range(1, 4)]
 
         def remote(src, dst, n, k, target):
+            far = k in (4, 5, 9, 10) or (k in (0, 11) and n in plane_first)
+            arrived = {0: 0, 11: 0, 1: 1, 2: 1, 3: 1, 4: 2, 5: 3, 6: 4, 7: 4, 8: 4, 9: 5, 10: 5}[k]
             return pltpu.make_async_remote_copy(
                 src_ref=src,
                 dst_ref=dst,
-                send_sem=sem_send.at[n, k],
-                recv_sem=sem_recv.at[n, k],
+                send_sem=sem_send.at[n, int(far)],
+                recv_sem=sem_recv.at[n, arrived],
                 device_id=target,
                 device_id_type=pl.DeviceIdType.MESH,
             )
+
+        def some(n, shards, half):
+            return view(n, slice(0, 3), y, x, half) if shards == 3 else view(n, slice(0, 3), every, every, half)
 
         def own_shards(n):
             layer, which, cols, part = units[n]
@@ -162,21 +170,12 @@
         def share_own(n):
             @pl.when(core == units[n][0])
             def _():
-                for i, (src, dst, k) in enumerate(own_shards(n)):
-                    pltpu.make_async_copy(src, dst, sem_own.at[n, i]).start()
+                for src, dst, k in own_shards(n):
+                    pltpu.make_async_copy(src, dst, sem_recv.at[n, 0]).start()
                     remote(src, dst, n, k, mate).start()
 
         def start_z(n):
-            @pl.when(core == units[n][0])
-            def _():
-                for i, (src, dst, k) in enumerate(own_shards(n)):
-                    pltpu.make_async_copy(src, dst, sem_own.at[n, i]).wait()
-
-            @pl.when(core != units[n][0])
-            def _():
-                for src, dst, k in own_shards(n):
-                    remote(src, dst, n, k, mate).wait_recv()
-
+            wait_bytes(view(n, z, y, x, every), sem_recv.at[n, 0])
             if n in plane_first:
                 by_route(n, lambda x_first: plane_copy(n, 4, x_first).start())
             else:
@@ -185,8 +184,7 @@
 
         def first_hop(n):
             if n not in plane_first:
-                for k in range(1, 4):
-                    z_copy(n, k).wait_recv()
+                wait_bytes(some(n, 3, core), sem_recv.at[n, 1])
 
             def act(x_first):
                 if n in plane_first:
@@ -217,9 +215,9 @@
         def last_share(n):
             def act(x_first):
                 if n in plane_first:
-                    for k in range(1, 4):
-                        z_copy(n, k).wait_recv()
-                        mate_copy(n, 5 + k, x_first, core).start()
+                    wait_bytes(some(n, 12, core), sem_recv.at[n, 1])
+                    for k in range(6, 9):
+                        mate_copy(n, k, x_first, core).start()
                 else:
                     plane_copy(n, 5, x_first).wait_recv()
                     mate_copy(n, 10, x_first, core).start()
@@ -227,42 +225,44 @@
             by_route(n, act)
 
         def complete(n):
-            def act(x_first):
-                for k in range(6, 11):
-                    mate_copy(n, k, not x_first, other).wait_recv()
-
-            by_route(n, act)
+            near, rest = (12, 3) if n in plane_first else (3, 12)
+            wait_bytes(some(n, near, other), sem_recv.at[n, 4])
+            wait_bytes(some(n, rest, other), sem_recv.at[n, 5])
 
         def drain(n):
+            few, many = (1, 0) if n in plane_first else (0, 1)
+            wait_bytes(view(n, slice(0, 3), every, every, every), sem_send.at[n, many])
+
             @pl.when(core == units[n][0])
             def _():
-                for src, dst, k in own_shards(n):
-                    remote(src, dst, n, k, mate).wait_send()
-
-            for k in range(1, 4):
-                z_copy(n, k).wait_send()
-
-            def act(x_first):
-                for k in (4, 5):
-                    plane_copy(n, k, x_first).wait_send()
-                for k in range(6, 11):
-                    mate_copy(n, k, x_first, core).wait_send()
-
-            by_route(n, act)
+                wait_bytes(view(n, every, y, x, every), sem_send.at[n, few])
+
+            @pl.when(core != units[n][0])
+            def _():
+                wait_bytes(view(n, slice(0, 3), y, x, every), sem_send.at[n, few])
 
         def hops(text):
             kinds = dict(z=start_z, f=first_hop, s=second_hop, l=last_share)
-            for word in text.split():
+            for word in text:
                 kinds[word[0]](int(word[1:]))
 
-        opening = "z0 z1 z2 z3 z4 z5 f0 f1 s0 z6 f2 s1 z7 f3 s2 l0 f4 s3 l1 f5 s4 f6 l2"
+        opening = ("z0", "z1", "z2", "z3", "z4", "z5", "f0", "f1", "s0", "z6", "f2", "s1", "z7", "f3", "s2", "l0", "f4", "s3", "l1", "f5", "s4", "f6", "l2")
         hops_at = {
-            (0, 0, "qkv"): "s5 f7 z8 z9 z11 z15", (0, 0, "quad0"): "s6 z10 z12", (0, 0, "quad1"): "f8 z13 f11",
-            (0, 1, "qkv"): "s7 f9", (0, 1, "quad0"): "s8 f10 z14 f15", (0, 1, "quad1"): "s9 s11",
-            (0, 0, "gate"): "l3 l4 l5 l6 f12", (0, 0, "ffna"): "s10 f13", (0, 1, "ffna"): "s12 s15",
-            (0, 0, "last"): "l7", (0, 0, "ffnb"): "s13 f14 l8", (0, 1, "ffnb"): "l9 l10",
-            (1, 0, "qkv"): "s14",
-            (1, 0, "gate"): "l11 l12 l13 l14", (1, 0, "last"): "l15",
+            (0, 0, "qkv"): ("s5", "f7", "z8", "z9", "z11", "z15"),
+            (0, 0, "quad0"): ("s6", "z10", "z12", "l3"),
+            (0, 0, "quad1"): ("f8", "z13", "f11"),
+            (0, 1, "qkv"): ("s7", "f9", "l4"),
+            (0, 1, "quad0"): ("s8", "f10", "z14", "f15", "l5"),
+            (0, 1, "quad1"): ("l6", "s9", "s11"),
+            (0, 0, "gate"): ("f12",),
+            (0, 0, "ffna"): ("l7", "s10", "f13"),
+            (0, 1, "ffna"): ("s12", "s15"),
+            (0, 0, "ffnb"): ("l8", "s13", "f14"),
+            (0, 1, "ffnb"): ("l9", "l10"),
+            (1, 0, "quad0"): ("s14", "l11"),
+            (1, 0, "quad1"): ("l12",),
+            (1, 1, "qkv"): ("l13",),
+            (1, 1, "quad0"): ("l14", "l15"),
         }
     else:
         hops_at = {}
@@ -270,7 +270,7 @@
         def weight_copy(n):
             layer, which, cols, part = units[n]
             src = weight_in[which].at[layer, every, every, every, every, part, cols]
-            return pltpu.make_async_copy(src, view(n, every, every, every, every), sem_own.at[n, 0])
+            return pltpu.make_async_copy(src, view(n, every, every, every, every), sem_recv.at[n, 0])
 
         def complete(n):
             weight_copy(n).wait()
@@ -351,9 +351,9 @@
     if routed:
         half_tok, half_mem = tok_rows // 2, slots // 2
 
-        def io_copies(buf, tok_ref, mem_ref, first, outward):
+        def io_copies(buf, tok_ref, mem_ref, sems, outward):
             local, away = [], []
-            k = first
+            own_sem, send_sem, recv_sem = (sem_io.at[k] for k in sems)
             for s in range(segs):
                 mine, theirs = core * segs + s, other * segs + s
                 for ref, base, size in ((tok_ref, slots, half_tok), (mem_ref, 0, half_mem)):
@@ -361,37 +361,39 @@
                         return buf.at[pl.ds(pl.multiple_of(s * rows + base + half * size, 16), size)]
 
                     if outward:
-                        local.append(pltpu.make_async_copy(rows_of(core), ref.at[mine], sem_io.at[k]))
+                        local.append(pltpu.make_async_copy(rows_of(core), ref.at[mine], own_sem))
                         src, dst = rows_of(other), ref.at[mine]
                     else:
-                        local.append(pltpu.make_async_copy(ref.at[mine], rows_of(core), sem_io.at[k]))
+                        local.append(pltpu.make_async_copy(ref.at[mine], rows_of(core), own_sem))
                         src, dst = ref.at[theirs], rows_of(core)
                     away.append(
                         pltpu.make_async_remote_copy(
                             src_ref=src,
                             dst_ref=dst,
-                            send_sem=io_send.at[k],
-                            recv_sem=io_recv.at[k],
+                            send_sem=send_sem,
+                            recv_sem=recv_sem,
                             device_id=mate,
                             device_id_type=pl.DeviceIdType.MESH,
                         )
                     )
-                    k += 1
             return local, away
 
-        loads, shares = io_copies(ub, rows_in[0], rows_in[1], 0, False)
-        more = io_copies(dy, rows_in[2], rows_in[3], 2 * segs, False)
+        def half_rows(buf):
+            return buf.at[pl.ds(0, segs * rows // 2)]
+
+        loads, shares = io_copies(ub, rows_in[0], rows_in[1], (0, 2, 0), False)
+        more = io_copies(dy, rows_in[2], rows_in[3], (1, 2, 1), False)
         loads, shares = loads + more[0], shares + more[1]
-        y_copies = io_copies(doa.at[1], rows_out[0], rows_out[1], 4 * segs, True)
-        du_copies = io_copies(dy, rows_out[2], rows_out[3], 6 * segs, True)
+        y_copies = io_copies(doa.at[1], rows_out[0], rows_out[1], (3, 4, 5), True)
+        du_copies = io_copies(dy, rows_out[2], rows_out[3], (6, 7, 8), True)
     else:
         loads = [
             pltpu.make_async_copy(rows_in[0], ub, sem_io.at[0]),
             pltpu.make_async_copy(rows_in[1], dy, sem_io.at[1]),
         ]
         shares = []
-        y_copies = [pltpu.make_async_copy(doa.at[1], rows_out[0], sem_io.at[2])], []
-        du_copies = [pltpu.make_async_copy(dy, rows_out[1], sem_io.at[3])], []
+        y_copies = [pltpu.make_async_copy(doa.at[1], rows_out[0], sem_io.at[3])], []
+        du_copies = [pltpu.make_async_copy(dy, rows_out[1], sem_io.at[6])], []
     for copy in loads:
         copy.start()
     if routed:
@@ -413,10 +415,17 @@
             weight_copy(n).start()
     stat_ref[...] = jnp.zeros_like(stat_ref)
 
-    for copy in loads:
-        copy.wait()
-    for copy in shares:
-        copy.wait()
+    wait_bytes(ub, sem_io.at[0])
+    wait_bytes(dy, sem_io.at[1])
+    if routed:
+        wait_bytes(ub, sem_io.at[2])
+
+    def wait_rows(buf, first):
+        if routed:
+            for k in range(3):
+                wait_bytes(half_rows(buf), sem_io.at[first + k])
+        else:
+            wait_bytes(buf, sem_io.at[first])
 
     def add_stat(layer, k, row_sums, valid):
         total = jnp.sum(row_sums * valid, axis=0, keepdims=True)
@@ -597,44 +606,48 @@
         plane_spots = [(y, 1 - x), (1 - y, x), (1 - y, 1 - x)]
         chunks = ff // chunk
 
-        def rs_copy(src, dst, layer, u, k, target):
+        def rs_copy(src, dst, u, step, k, target):
             return pltpu.make_async_remote_copy(
                 src_ref=src,
                 dst_ref=dst,
-                send_sem=rs_send.at[layer, u, k],
-                recv_sem=rs_recv.at[layer, u, k],
+                send_sem=rs_send.at[u, step],
+                recv_sem=rs_recv.at[u, k],
                 device_id=target,
                 device_id_type=pl.DeviceIdType.MESH,
             )
 
-        def chunk_cols(c):
-            return slice(c * chunk, (c + 1) * chunk)
-
-        def spot(layer, u, pz, py, px, c, piece=None):
+        def piece_cols(step, piece, u):
+            size = chunk if step < 2 else ff // 2
+            return slice(piece * size, (piece + 1) * size)
+
+        def piece_planes(step, piece):
+            return piece if step < 2 else slice(2 * piece, 2 * piece + 2)
+
+        def spot(layer, u, pz, py, px, c, piece=None, step=0):
             cols = rs_cols.get(u, every)
             if piece is not None and u == wd_u:
-                pz = piece
+                pz = piece_planes(step, piece)
             elif piece is not None:
-                cols = chunk_cols(piece)
+                cols = piece_cols(step, piece, u)
             return weight_buf[rs_weight[u]].at[layer + 1, pz, py, px, c, every, cols]
 
         def land_at(u, step, piece=None):
             ref = lands[u][step]
             if piece is None:
                 return ref
+            ring = piece % 2 if step == 0 else piece
             if u == wd_u:
-                return ref.at[piece % 2 if step == 0 else piece]
-            if step == 0:
-                return ref.at[every, every, every, every, chunk_cols(piece % 2)]
-            return ref.at[every, every, every, chunk_cols(piece)]
+                return ref.at[piece_planes(step, ring)]
+            lead = (every,) * (len(ref.shape) - 1)
+            return ref.at[(*lead, piece_cols(step, ring, u))]
 
         def rs_copies(layer, u, step, y_first, piece=None):
             if step == 0:
                 src = spot(layer, u, every, every, every, other, piece)
-                return [rs_copy(src, land_at(u, 0, piece), layer, u, piece or 0, mate)]
+                return [rs_copy(src, land_at(u, 0, piece), u, 0, (piece or 0) % 2, mate)]
             if step == 1 and u in fast:
                 return [
-                    rs_copy(spot(layer, u, every, *plane_spots[k], core), lands[u][1].at[k], layer, u, 4 + k, plane_peers[k])
+                    rs_copy(spot(layer, u, every, *plane_spots[k], core), lands[u][1].at[k], u, 1, 2, plane_peers[k])
                     for k in range(3)
                 ]
             if step == 3 and u in fast:
@@ -642,25 +655,30 @@
             if step == 1:
                 at = (every, 1 - y, every) if y_first else (every, every, 1 - x)
                 src = spot(layer, u, *at, core, piece)
-                return [rs_copy(src, land_at(u, 1, piece), layer, u, 4 + (piece or 0), near_y if y_first else near_x)]
+                return [rs_copy(src, land_at(u, 1, piece), u, 1, 2 + (piece or 0) // 2, near_y if y_first else near_x)]
             if step == 2:
                 at = (every, y, 1 - x) if y_first else (every, 1 - y, x)
-                return [rs_copy(spot(layer, u, *at, core), lands[u][2], layer, u, 8, near_x if y_first else near_y)]
+                src = spot(layer, u, *at, core, piece, 2)
+                return [rs_copy(src, land_at(u, 2, piece), u, 2, 4 + (piece or 0), near_x if y_first else near_y)]
             if step == 3:
+                cols = piece_cols(3, piece, u) if piece is not None else every
                 return [
-                    rs_copy(spot(layer, u, (z + k) % 4, y, x, core), lands[u][3].at[k - 1], layer, u, 8 + k, along_z[k - 1])
+                    rs_copy(
+                        weight_buf[rs_weight[u]].at[layer + 1, (z + k) % 4, y, x, core, every, cols],
+                        lands[u][3].at[k - 1, every, cols], u, 3, 6, along_z[k - 1],
+                    )
                     for k in range(1, 4)
                 ]
-            return [rs_copy(src, dst, layer, u, 12 + k, mate) for k, (src, dst) in enumerate(home_parts(layer, u))]
-
-        def owner_copy(layer, u, k, half=None):
+            return [rs_copy(src, dst, u, 4, 7, mate) for src, dst in home_parts(layer, u)]
+
+        def owner_copy(layer, u, k):
             away = (z + k + 1) % 4 if k < 3 else z
-            half = core if half is None else half
+            half = core
             return pltpu.make_async_remote_copy(
                 src_ref=spot(layer, u, away, y, x, core),
                 dst_ref=lands[u][3].at[half, k],
-                send_sem=rs_send.at[layer, u, 9 + k],
-                recv_sem=rs_recv.at[layer, u, 9 + 4 * half + k],
+                send_sem=rs_send.at[u, 3],
+                recv_sem=rs_recv.at[u, 6 + half],
                 device_id=(layer, place(away, y, x)),
                 device_id_type=pl.DeviceIdType.MESH,
             )
@@ -676,11 +694,9 @@
         def merge_owner(layer, u):
             @pl.when(core == layer)
             def _():
-                for k in range(3):
-                    owner_copy(layer, u, k, layer).wait_recv()
-                for k in range(4):
-                    owner_copy(layer, u, k, 1 - layer).wait_recv()
                 got = lands[u][3]
+                wait_bytes(got.at[layer, pl.ds(0, 3)], rs_recv.at[u, 6 + layer])
+                wait_bytes(got.at[1 - layer], rs_recv.at[u, 7 - layer])
                 cols = rs_cols[u]
                 for half in range(2):
                     if half == layer:
@@ -697,7 +713,7 @@
                     else:
                         fin[u][half] = total
                 for k, (src, dst) in enumerate(home_parts(layer, u)):
-                    pltpu.make_async_copy(src, dst, sem_g.at[layer, u, k]).start()
+                    pltpu.make_async_copy(src, dst, sem_g.at[5 if k == 3 else u]).start()
 
         def home_parts(layer, u):
             if u not in rs_cols:
@@ -727,17 +743,29 @@
                 act(True)
 
         def rs_pieces(u, step):
-            return list(range(chunks)) if u in chunked and step < 2 else [None]
+            if u in chunked and step < 3:
+                return list(range(chunks if step < 2 else 2))
+            return [0, 1] if u == wu_u and step == 3 else [None]
 
         def rs_start(layer, u, step, piece=None):
+            if layer == 0 and step < 4 and not piece:
+                rs_sent(1, u, step)
             if step == 3 and u in fast:
                 start_owner(layer, u)
                 return
             used = layer == 0 and not piece
-            if step == 0 and u in chunked:
-                used = layer == 0 or piece >= 2
+            if u in chunked and step < 3:
+                used = (layer == 0 or piece >= 2, layer == 0 and piece % 2 == 0, layer == 0)[step]
             if used and step < 4:
                 pl.semaphore_wait(rs_free.at[u, step], 3 if step == 3 or (step == 1 and u in fast) else 1)
+
+            if u == wd_u and step == 3:
+                for k, copy in enumerate(rs_copies(layer, u, 3, True)):
+                    @pl.when((z + k + 1) % 4 // 2 == piece)
+                    def _(copy=copy):
+                        copy.start()
+
+                return
 
             def act(y_first):
                 for copy in rs_copies(layer, u, step, y_first, piece):
@@ -765,14 +793,14 @@
                 merge_owner(layer, u)
                 return
 
-            def act(y_first):
-                for wait_piece in [piece] if step == 0 else rs_pieces(u, step):
-                    for copy in rs_copies(layer, u, step, y_first, wait_piece):
-                        copy.wait_recv()
-
-            on_route(u, step, act)
+            got = lands[u][step]
+            sem = (piece or 0) % 2 if step < 3 else 0
+            wait_at = land_at(u, step, piece) if step in (0, 2) else got
+            if u in chunked and step == 1:
+                wait_at = got.at[piece_planes(2, piece)] if u == wd_u else got.at[:, :, :, piece_cols(2, piece, u)]
+            wait_bytes(wait_at, rs_recv.at[u, 2 * step + sem])
             slot = layer + 1
-            buf, got = weight_buf[rs_weight[u]], lands[u][step]
+            buf = weight_buf[rs_weight[u]]
             cols = rs_cols.get(u, every)
             if step == 3:
                 if layer == 0:
@@ -786,8 +814,8 @@
 
                 @pl.when(core == layer)
                 def _():
-                    for k, (src, dst) in enumerate(home_parts(layer, u)):
-                        pltpu.make_async_copy(src, dst, sem_g.at[layer, u, k]).start()
+                    for src, dst in home_parts(layer, u):
+                        pltpu.make_async_copy(src, dst, sem_g.at[u]).start()
 
                 @pl.when(core != layer)
                 def _():
@@ -797,11 +825,14 @@
             if step == 0 and piece is not None and u == wd_u:
                 buf[slot, piece, :, :, core] += got[piece % 2]
             else:
-                got_cols = every
-                if step == 0 and piece is not None:
-                    cols, got_cols = chunk_cols(piece), chunk_cols(piece % 2)
-
-                @pl.loop(0, 4)
+                got_cols, planes = every, (0, 4)
+                if piece is not None and u == wd_u:
+                    planes = (2 * piece, 2 * piece + 2)
+                elif piece is not None:
+                    cols = piece_cols(step if step != 1 else 2, piece, u)
+                    got_cols = piece_cols(0, piece % 2, u) if step == 0 else cols
+
+                @pl.loop(*planes)
                 def _(pz):
                     if step == 0:
                         buf[slot, pz, :, :, core, :, cols] += got[pz, :, :, :, got_cols]
@@ -811,13 +842,13 @@
                             total = total + got[k, pz].astype(f32)
                         buf[slot, pz, y, x, core, :, cols] = total.astype(bf16)
                     elif step == 2:
-                        buf[slot, pz, y, x, core, :, cols] += got[pz]
+                        buf[slot, pz, y, x, core, :, cols] += got[pz, :, got_cols]
                     else:
                         def add(y_first):
                             if y_first:
-                                buf[slot, pz, y, :, core, :, cols] += got[pz]
+                                buf[slot, pz, y, :, core, :, cols] += got[pz, :, :, got_cols]
                             else:
-                                buf[slot, pz, :, x, core, :, cols] += got[pz]
+                                buf[slot, pz, :, x, core, :, cols] += got[pz, :, :, got_cols]
 
                         rs_route(u, add)
 
@@ -828,8 +859,11 @@
         def rs_home(layer, u):
             @pl.when(core == layer)
             def _():
-                for k, (src, dst) in enumerate(home_parts(layer, u)):
-                    pltpu.make_async_copy(src, dst, sem_g.at[layer, u, k]).wait()
+                if u == wqb_u:
+                    wait_bytes(fin[u].at[:, :, lanes:], sem_g.at[u])
+                    wait_bytes(fin[u].at[:, 0:8, 0:lanes], sem_g.at[5])
+                else:
+                    wait_bytes(fin[u], sem_g.at[u])
                 if u not in fast:
                     for copy in rs_copies(layer, u, 4, True):
                         copy.wait_recv()
@@ -840,26 +874,30 @@
                     for copy in rs_copies(layer, u, 4, True):
                         copy.wait_send()
 
-        def rs_finish(layer, u):
-            if u in fast:
-                for step in range(2):
-                    for copy in rs_copies(layer, u, step, True):
-                        copy.wait_send()
-                for k in range(3):
-                    owner_copy(layer, u, k).wait_send()
+        def rs_sent(layer, u, step):
+            three = slice(0, 3)
+            if step == 0:
+                wait_bytes(spot(layer, u, every, every, every, other), rs_send.at[u, 0])
+            elif step == 1 and u in fast:
+                wait_bytes(spot(layer, u, three, every, every, core), rs_send.at[u, 1])
+            elif step == 1:
+                wait_bytes(spot(layer, u, every, y, every, core), rs_send.at[u, 1])
+            elif step == 2:
+                wait_bytes(spot(layer, u, every, y, x, core), rs_send.at[u, 2])
+            elif u not in fast:
+                wait_bytes(spot(layer, u, three, y, x, core), rs_send.at[u, 3])
+            else:
+                @pl.when(core == layer)
+                def _():
+                    wait_bytes(spot(layer, u, three, y, x, core), rs_send.at[u, 3])
 
                 @pl.when(core != layer)
                 def _():
-                    owner_copy(layer, u, 3).wait_send()
-
-                return
-            for step in range(4):
-                def act(y_first, step=step):
-                    for piece in rs_pieces(u, step):
-                        for copy in rs_copies(layer, u, step, y_first, piece):
-                            copy.wait_send()
-
-                on_route(u, step, act)
+                    wait_bytes(spot(layer, u, every, y, x, core), rs_send.at[u, 3])
+
+        def rs_finish(layer, u):
+            for step in (0, 1, 3) if u in fast else range(4):
+                rs_sent(layer, u, step)
 
         def stat_copy(step, k=0):
             target = (mate, near_y, near_x)[step] if step < 3 else along_z[k]
@@ -867,8 +905,8 @@
             return pltpu.make_async_remote_copy(
                 src_ref=stat_sum.at[step],
                 dst_ref=stat_land.at[place_at],
-                send_sem=stat_send.at[step + k],
-                recv_sem=stat_recv.at[step + k],
+                send_sem=stat_send.at[step],
+                recv_sem=stat_recv.at[step],
                 device_id=target,
                 device_id_type=pl.DeviceIdType.MESH,
             )
@@ -886,8 +924,8 @@
                 for k in range(3):
                     stat_copy(3, k).start()
             else:
-                for k in range(3):
-                    stat_copy(3, k).wait()
+                wait_bytes(stat_land.at[pl.ds(3, 3)], stat_recv.at[3])
+                wait_bytes(stat_land.at[pl.ds(3, 3)], stat_send.at[3])
                 total = stat_land[3] + stat_land[4] + stat_land[5] + stat_land[6]
                 stat_ref[...] = total
                 stat_done()
@@ -896,7 +934,7 @@
         names = dict(a=wqa_u, o=wo_u, u=wu_u, d=wd_u, b=wqb_u)
 
         def run_events(layer, text):
-            for word in text.split():
+            for word in text:
                 if word[0] == "t":
                     stat_step(int(word[1]))
                     continue
@@ -908,34 +946,32 @@
                 (rs_start if word[0] == "S" else rs_merge)(at_layer, u, step, piece)
 
         back_points = {
-            (1, "ffn0"): "t1 S0d0 S0u0",
-            (1, "ffn1"): "t2 M0d0 M0u0 S0d1 S0u1",
-            (1, "ffn2"): "t3 M0d1 M0u1 S0d2 S0u2",
-            (1, "ffn3"): "t4 M0d2 M0u2 S0d3 S0u3",
-            (1, "mid"): "M0d3 M0u3",
-            (1, "wo"): "S0o",
-            (1, "att00"): "M0o",
-            (1, "att01"): "M1d M1u",
-            (1, "wq0"): "S0a",
-            (1, "att10"): "M0a M1o",
-            (1, "att11"): "M2d M2u",
-            (1, "wq1"): "S0b",
-            (1, "in0"): "M0b M2o",
-            (1, "in1"): "M1a",
-            (0, "ffn0"): "S0d0 S0u0",
-            (0, "ffn1"): "M0d0 M0u0 S0d1 S0u1 pM1b pM3d pM3u",
-            (0, "ffn2"): "M0d1 M0u1 S0d2 S0u2 pM3o pM3a",
-            (0, "ffn3"): "M0d2 M0u2 S0d3 S0u3 pM3b",
-            (0, "mid"): "M0d3 M0u3",
-            (0, "wo"): "S0o",
-            (0, "att00"): "M0o",
-            (0, "att01"): "M1d M1u",
-            (0, "wq0"): "S0a",
-            (0, "att10"): "M0a M1o",
-            (0, "att11"): "M2d M2u",
-            (0, "wq1"): "S0b M1a M0b",
-            (0, "in0"): "M2o",
-            (0, "end"): "M3d M3u M1b M3o M3a M3b",
+            (1, "ffn0"): ("t1", "S0d0", "S0u0"),
+            (1, "ffn1"): ("t2", "M0d0", "M0u0", "S0d1", "S0u1"),
+            (1, "ffn2"): ("t3", "M0d1", "M0u1", "S0d2", "S0u2"),
+            (1, "ffn3"): ("t4", "M0d2", "M0u2", "S0d3", "S0u3"),
+            (1, "mid0"): ("M0d3", "M0u3"),
+            (1, "wo"): ("S0o", "M1d0", "M1u0"),
+            (1, "att00"): ("M0o", "M1d1", "M1u1"),
+            (1, "att01"): ("M2d0", "M2u0"),
+            (1, "wq0"): ("S0a",),
+            (1, "att10"): ("M0a", "M1o", "M2d1", "M2u1"),
+            (1, "wq1"): ("S0b",),
+            (1, "in0"): ("M0b", "M2o"),
+            (1, "in1"): ("M1a",),
+            (0, "ffn0"): ("S0d0", "S0u0"),
+            (0, "ffn1"): ("M0d0", "M0u0", "S0d1", "S0u1", "pM1b", "pM3d", "pM3u"),
+            (0, "ffn2"): ("M0d1", "M0u1", "S0d2", "S0u2", "pM3o", "pM3a"),
+            (0, "ffn3"): ("M0d2", "M0u2", "S0d3", "S0u3", "pM3b"),
+            (0, "mid0"): ("M0d3", "M0u3"),
+            (0, "wo"): ("S0o", "M1d0", "M1u0"),
+            (0, "att00"): ("M0o", "M1d1", "M1u1"),
+            (0, "att01"): ("M2d0", "M2u0"),
+            (0, "wq0"): ("S0a",),
+            (0, "att10"): ("M0a", "M1o", "M2d1", "M2u1"),
+            (0, "wq1"): ("S0b", "M1a", "M0b"),
+            (0, "in0"): ("M2o",),
+            (0, "end"): ("M1b", "M3d", "M3u", "M3o", "M3a", "M3b"),
         }
     else:
         back_points = {}
@@ -1067,7 +1103,7 @@
 
     def grad_copies(layer):
         return [
-            pltpu.make_async_copy(buf.at[layer + 1], out.at[layer], sem_g.at[layer, k, 0])
+            pltpu.make_async_copy(buf.at[layer + 1], out.at[layer], sem_g.at[k])
             for k, (buf, out) in enumerate(zip(weight_buf, grads_out))
         ]
 
@@ -1086,15 +1122,13 @@
 
         @pl.when(layer == 1)
         def _():
-            for copies in y_copies:
-                for copy in copies:
-                    copy.wait()
+            wait_rows(doa.at[1], 3)
 
         @pl.loop(0, segs)
         def _(s):
             backward_middle(layer, s)
-
-        back_point(layer, "mid")
+            back_point(layer, "mid0", s, 0)
+
         put_mat(1, slot, tn(obuf[...], dy[...]).astype(bf16))
         back_point(layer, "wo")
 
@@ -1169,17 +1203,14 @@
             copy.start()
     back_point(0, "end")
     if routed:
-        for layer in (1, 0):
-            for u in range(5):
-                rs_finish(layer, u)
+        for u in range(5):
+            rs_finish(0, u)
     if routed:
         for u in range(5):
             rs_home(0, u)
         for u in (0, 4):
             rs_home(1, u)
-    for copies in du_copies:
-        for copy in copies:
-            copy.wait()
+    wait_rows(dy, 6)
 
 
 def run_layers(dims, routed, doc_len, row_args, weights):
@@ -1238,11 +1269,10 @@
         pltpu.VMEM((2, 8, lanes), f32),
         dma((segs, 8)),
         dma((segs, 8)),
-        dma((2, 5, 4)),
-        dma((8 * segs,)),
+        dma((8,)),
+        dma((9,)),
         dma((unit_count, 2)),
-        dma((unit_count, 12)),
-        dma((unit_count, 12)),
+        dma((unit_count, 6)),
     ]
     params = dict(vmem_limit_bytes=127 * 2**19)
     if routed:
@@ -1260,13 +1290,11 @@
         scratch += [
             pltpu.VMEM((4, 2, 8, lanes), f32),
             pltpu.VMEM((7, 2, 8, lanes), f32),
-            dma((2, 5, 17)),
-            dma((2, 5, 17)),
+            dma((5, 5)),
+            dma((5, 8)),
             pltpu.SemaphoreType.REGULAR((5, 4)),
-            dma((8 * segs,)),
-            dma((8 * segs,)),
-            dma((6,)),
-            dma((6,)),
+            dma((4,)),
+            dma((4,)),
         ]
     return pl.pallas_call(
         partial(fused_layers, dims, routed),

time: 199 us -> 180 us (0.905)
  Pallas kernels: 196 us -> 178 us
    pallas_call x1, Pallas kernels: 192 us -> 174 us  [run_layers(): pl.pallas_call(partial(fused_layers, dims, routed), out_shape=out_shape,...]
where the time goes in v5:
time: 180 us
  Pallas kernels  178 us (99%)
    pallas_call x1, Pallas kernels, run_layers(): pl.pallas_call(partial(fused_layers, dims, routed), out_shape=out_shape,...  174 us
    pallas_call x1, Pallas kernels, settle(): pl.pallas_call(settle_kernel, out_shape=[shape(part.shape, part.dtype) fo...  4.31 us

profile of v5, /device:TPU:0, one launch (start us, length us, event | category | flops | bytes accessed | tf_op | source)
XLA Modules:
  0.0 180.0 jit_solution(9941613587101048875)
XLA Ops:
  0.6 0.7 pad_maximum_fusion
  1.3 0.1 copy.25
  1.4 0.6 pad.4.clone
  2.1 173.5 %shard_map.211 = (bf16[4,256,512]{2,1,0:T(8,128)(2,1)}, bf16[4,32,512]{2,1,0:T(8,128)(2,1)}, bf16[4,256,512]{2,1,0:T(8,128)(2,1)}, bf16[4,32,512]{2,1,0:T(8,128)...) custom-call(s32[2]{0:T(128)} %refs_0_.1, ...), custom_call_target="tpu_custom_call" | custom-call | tf_op jit(solution)/shard_map/pallas_call | solution.py:1299
  175.6 4.3 %shard_map.212 = (bf16[4,256,512]{2,1,0:T(8,128)(2,1)}, bf16[4,32,512]{2,1,0:T(8,128)(2,1)}, bf16[4,256,512]{2,1,0:T(8,128)(2,1)}, bf16[4,32,512]{2,1,0:T(8,128)...) custom-call(bf16[4,256,512]{2,1,0:T(8,128)(2,1)} %get-tuple-element., ...), custom_call_target="tpu_custom_call" | custom-call | tf_op jit(solution)/shard_map/pallas_call | solution.py:1338

commit v6 on v5

--- a/solution.py
+++ b/solution.py
@@ -50,19 +50,21 @@
 
     (len_ref,) = take(1)
     rows_in = take(4 if routed else 2)
-    weight_in = take(5 if routed else 4)
+    weight_in = take(4)
+    vectors_in = take(3) if routed else []
     rows_out = take(4 if routed else 2)
     grads_out = take(5 if routed else 4)
     (stat_out,) = take(1)
     spill_hbm = take(8)
     weight_buf = take(4)
     ub, dy, qkv, ebuf, obuf, ilbuf, hbuf, slope, active, doa, dn = take(11)
-    gains, bias_rows, ext, gain_sums, dbias, stat_ref = take(6)
-    sem_spill, sem_back, sem_g, sem_io, sem_send, sem_recv = take(6)
+    gains, gain_sums, dbias, stat_ref = take(4)
+    sem_spill, sem_g, sem_io, sem_send, sem_recv = take(5)
     if routed:
         lands = [take(4) for _ in range(5)]
         fin = take(5)
-        stat_sum, stat_land = take(2)
+        stat_sum, stat_land, small_buf = take(3)
+        weight_in = [*weight_in, small_buf]
         rs_send, rs_recv, rs_free, stat_send, stat_recv = take(5)
     head_size = width // heads
     pairs = width // lanes
@@ -246,23 +248,23 @@
             for word in text:
                 kinds[word[0]](int(word[1:]))
 
-        opening = ("z0", "z1", "z2", "z3", "z4", "z5", "f0", "f1", "s0", "z6", "f2", "s1", "z7", "f3", "s2", "l0", "f4", "s3", "l1", "f5", "s4", "f6", "l2")
+        opening = ("z0", "z1", "z2", "z3", "z4", "z5", "f0", "f1", "s0", "z6", "f2", "s1", "z7", "f3", "s2", "l0", "f4", "s3", "l1", "f5", "s4", "f6", "l2", "z8", "z9", "z11")
         hops_at = {
-            (0, 0, "qkv"): ("s5", "f7", "z8", "z9", "z11", "z15"),
-            (0, 0, "quad0"): ("s6", "z10", "z12", "l3"),
-            (0, 0, "quad1"): ("f8", "z13", "f11"),
+            (0, 0, "qkv"): ("s5", "f7", "z10", "z15"),
+            (0, 0, "quad0"): ("s6", "z12", "l3"),
+            (0, 0, "quad1"): ("f8", "f11", "z13"),
             (0, 1, "qkv"): ("s7", "f9", "l4"),
-            (0, 1, "quad0"): ("s8", "f10", "z14", "f15", "l5"),
+            (0, 1, "quad0"): ("f10", "s8", "z14", "f15", "l5"),
             (0, 1, "quad1"): ("l6", "s9", "s11"),
             (0, 0, "gate"): ("f12",),
             (0, 0, "ffna"): ("l7", "s10", "f13"),
-            (0, 1, "ffna"): ("s12", "s15"),
-            (0, 0, "ffnb"): ("l8", "s13", "f14"),
-            (0, 1, "ffnb"): ("l9", "l10"),
-            (1, 0, "quad0"): ("s14", "l11"),
-            (1, 0, "quad1"): ("l12",),
-            (1, 1, "qkv"): ("l13",),
-            (1, 1, "quad0"): ("l14", "l15"),
+            (0, 1, "ffna"): ("s15",),
+            (0, 0, "ffnb"): ("s12", "l8", "f14"),
+            (0, 1, "ffnb"): ("s13", "l9", "l10"),
+            (1, 0, "quad0"): ("s14",),
+            (1, 1, "qkv"): ("l12", "l13"),
+            (1, 1, "quad0"): ("l11", "l14"),
+            (1, 1, "quad1"): ("l15",),
         }
     else:
         hops_at = {}
@@ -323,7 +325,7 @@
         ]
         if back:
             return [
-                pltpu.make_async_copy(hbm, vmem, sem_back.at[s, k])
+                pltpu.make_async_copy(hbm, vmem, sem_spill.at[s, k])
                 for k, (vmem, hbm) in enumerate(pairs_of)
                 if k in picks
             ]
@@ -336,8 +338,8 @@
     def doc_end(s):
         return len_ref[first_doc + s // per_doc] - (s % per_doc) * tok_rows
 
-    def valid_col(s):
-        row = lax.broadcasted_iota(jnp.int32, (rows, 1), 0)
+    def valid_rows(s):
+        row = lax.broadcasted_iota(jnp.int32, (rows, lanes), 0)
         return jnp.where(
             (row >= slots) & (row - slots < doc_end(s)), 1.0, 0.0
         ).astype(f32)
@@ -397,6 +399,12 @@
     for copy in loads:
         copy.start()
     if routed:
+        vectors = [ref[...].astype(f32) for ref in vectors_in]
+        count = vectors[0].shape[1]
+        tile = jnp.concatenate([*vectors, jnp.zeros((5, count), f32)], axis=0)
+        tile = jnp.concatenate([tile, jnp.zeros((8, lanes - count), f32)], axis=1).T[:count]
+        tile = jnp.concatenate([tile, jnp.zeros((count, lanes - 8), f32)], axis=1)
+        small_buf[...] = tile.astype(bf16).reshape(small_buf.shape)
         barrier = pltpu.get_barrier_semaphore()
         peers = [mate, near_x, near_y, (core, place(z, 1 - y, 1 - x)), *along_z]
         peers += [(other, place((z + k) % 4, y, x)) for k in range(1, 4)]
@@ -427,9 +435,12 @@
         else:
             wait_bytes(buf, sem_io.at[first])
 
-    def add_stat(layer, k, row_sums, valid):
-        total = jnp.sum(row_sums * valid, axis=0, keepdims=True)
-        stat_ref[layer, k : k + 1, :] += jnp.broadcast_to(total, (1, lanes))
+    def add_stat(layer, k, values, valid):
+        total = jnp.zeros((1, lanes), f32)
+        for p in range(values.shape[1] // lanes):
+            part = values[:, p * lanes : (p + 1) * lanes]
+            total = total + jnp.sum(part * part * valid, axis=0, keepdims=True)
+        stat_ref[layer, k : k + 1, :] += total
 
     def forward_attention(layer, s):
         at = seg_rows(s)
@@ -443,7 +454,7 @@
             for side in range(2):
                 h = 2 * p + side
                 own, marks = lane_marks(head_size, side)
-                bias = bias_rows[h]
+                bias = gain_sums[0, h * slots : (h + 1) * slots]
                 hi = bias.astype(bf16).astype(f32)
                 aux = jnp.concatenate([hi * marks[1] + (bias - hi) * marks[2], jnp.zeros((tok_rows, lanes), f32)], axis=0)
                 aux = aux + mask * marks[0]
@@ -466,13 +477,14 @@
                 after(layer, s, "quad" + str(p // 2))
 
     def unpack_small(layer):
-        ext[...] = mat(0, layer, slice(0, lanes)).astype(f32)
-        turned = ext[...].T
+        small = mat(0, layer, slice(0, lanes)).astype(f32)
+        gain_sums[1] = small
+        turned = small.T
         for k in range(2):
             gains[layer, k] = turned[k : k + 1, :]
         for h in range(heads):
-            column = ext[pl.ds(h, slots, stride=heads), :][:, 2:3]
-            bias_rows[h] = jnp.broadcast_to(column * log2_e, (slots, lanes))
+            column = gain_sums[1, pl.ds(h, slots, stride=heads)][:, 2:3]
+            gain_sums[0, h * slots : (h + 1) * slots] = jnp.broadcast_to(column * log2_e, (slots, lanes))
 
     def forward_attn(layer, s):
         at = seg_rows(s)
@@ -486,10 +498,10 @@
         def _():
             spill_copies(s, False, (7,))[0].start()
 
-        valid = valid_col(s)
+        valid = valid_rows(s)
         x = ub[at, :].astype(f32)
         squares = jnp.sum(x * x, axis=1, keepdims=True)
-        add_stat(layer, 0, squares, valid)
+        add_stat(layer, 0, x, valid)
         add_stat(layer, 3, valid, valid)
         n1 = (x * lax.rsqrt(squares / width + norm_eps) * gains[layer, 0]).astype(bf16)
         for k in range(3):
@@ -530,9 +542,9 @@
 
     def forward_ffn_a(layer, s):
         at = seg_rows(s)
-        valid = valid_col(s)
+        valid = valid_rows(s)
         z = mm(obuf[at, :], mat(1, layer))
-        add_stat(layer, 1, jnp.sum(z * z, axis=1, keepdims=True), valid)
+        add_stat(layer, 1, z, valid)
         h = ub[at, :].astype(f32) + z
         hbuf[at, :] = h.astype(bf16)
         doa[0, at, :] = (h * lax.rsqrt(jnp.mean(h * h, axis=1, keepdims=True) + norm_eps) * gains[layer, 1]).astype(bf16)
@@ -541,12 +553,11 @@
 
     def forward_ffn_b(layer, s):
         at = seg_rows(s)
-        valid = valid_col(s)
+        valid = valid_rows(s)
         ffn_part(s, layer, range(ff // chunk // 2, ff // chunk))
         out = dn[at, :]
-        add_stat(layer, 2, jnp.sum(out * out, axis=1, keepdims=True), valid)
-        z = mm(obuf[at, :], mat(1, layer))
-        result = (ub[at, :].astype(f32) + z + out).astype(bf16)
+        add_stat(layer, 2, out, valid)
+        result = (hbuf[at, :].astype(f32) + out).astype(bf16)
 
         @pl.when(layer == 0)
         def _():
@@ -946,24 +957,23 @@
                 (rs_start if word[0] == "S" else rs_merge)(at_layer, u, step, piece)
 
         back_points = {
-            (1, "ffn0"): ("t1", "S0d0", "S0u0"),
-            (1, "ffn1"): ("t2", "M0d0", "M0u0", "S0d1", "S0u1"),
-            (1, "ffn2"): ("t3", "M0d1", "M0u1", "S0d2", "S0u2"),
-            (1, "ffn3"): ("t4", "M0d2", "M0u2", "S0d3", "S0u3"),
+            (1, "ffn0"): ("S0d0", "S0u0"),
+            (1, "ffn1"): ("t1", "M0d0", "M0u0", "S0d1", "S0u1"),
+            (1, "ffn2"): ("M0d1", "M0u1", "S0d2", "S0u2"),
+            (1, "ffn3"): ("t2", "M0d2", "M0u2", "S0d3", "S0u3"),
             (1, "mid0"): ("M0d3", "M0u3"),
-            (1, "wo"): ("S0o", "M1d0", "M1u0"),
+            (1, "wo"): ("t3", "S0o", "M1d0", "M1u0"),
             (1, "att00"): ("M0o", "M1d1", "M1u1"),
-            (1, "att01"): ("M2d0", "M2u0"),
+            (1, "att01"): ("t4", "M2d0", "M2u0"),
             (1, "wq0"): ("S0a",),
             (1, "att10"): ("M0a", "M1o", "M2d1", "M2u1"),
             (1, "wq1"): ("S0b",),
-            (1, "in0"): ("M0b", "M2o"),
-            (1, "in1"): ("M1a",),
-            (0, "ffn0"): ("S0d0", "S0u0"),
-            (0, "ffn1"): ("M0d0", "M0u0", "S0d1", "S0u1", "pM1b", "pM3d", "pM3u"),
-            (0, "ffn2"): ("M0d1", "M0u1", "S0d2", "S0u2", "pM3o", "pM3a"),
-            (0, "ffn3"): ("M0d2", "M0u2", "S0d3", "S0u3", "pM3b"),
-            (0, "mid0"): ("M0d3", "M0u3"),
+            (1, "in0"): ("M0b",),
+            (0, "ffn0"): ("S0d0", "S0u0", "pM1a", "pM2o"),
+            (0, "ffn1"): ("M0d0", "M0u0", "S0d1", "S0u1", "pM1b"),
+            (0, "ffn2"): ("M0d1", "M0u1", "S0d2", "S0u2", "pM3d", "pM3u"),
+            (0, "ffn3"): ("M0d2", "M0u2", "S0d3", "S0u3", "pM3o", "pM3a"),
+            (0, "mid0"): ("M0d3", "M0u3", "pM3b"),
             (0, "wo"): ("S0o", "M1d0", "M1u0"),
             (0, "att00"): ("M0o", "M1d1", "M1u1"),
             (0, "att01"): ("M2d0", "M2u0"),
@@ -978,7 +988,9 @@
 
     def stat_done():
         totals = stat_ref[...]
-        stat_out[...] = totals if not routed else jnp.sqrt(totals / (totals[0:1, 3:4, :] * width))
+        stat_out[...] = totals if not routed else jnp.broadcast_to(
+            jnp.sqrt(jnp.sum(totals, axis=2, keepdims=True) / (totals[0:1, 3:4, 0:1] * width)), totals.shape
+        )
 
     if not routed:
         stat_done()
@@ -1001,20 +1013,22 @@
         return inv * (scaled - hat * jnp.mean(scaled * hat, axis=1, keepdims=True))
 
     def add_gain(k, d_weight, weight):
+        total = gain_sums[k]
         for p in range(d_weight.shape[1] // lanes):
             cols = slice(p * lanes, (p + 1) * lanes)
-            gain_sums[k] += d_weight[:, cols] * weight[:, cols].astype(f32)
+            total = total + d_weight[:, cols] * weight[:, cols].astype(f32)
+        gain_sums[k] = total
 
     def pack_small(layer):
+        sums = [jnp.sum(gain_sums[k], axis=1, keepdims=True) for k in range(2)]
         turned = dbias[...].T
         for h in range(heads):
-            ext[pl.ds(h, slots, stride=heads), :] = jnp.broadcast_to(turned[:slots, h : h + 1], (slots, lanes))
+            gain_sums[1, pl.ds(h, slots, stride=heads)] = jnp.broadcast_to(turned[:slots, h : h + 1], (slots, lanes))
         lane = lax.broadcasted_iota(jnp.int32, (width, lanes), 1)
         gain = mat(0, layer, slice(0, lanes)).astype(f32)
-        sums = [jnp.sum(gain_sums[k], axis=1, keepdims=True) for k in range(2)]
         safe = jnp.where(lane < 2, gain, 1.0)
         value = jnp.where(lane == 0, sums[0], jnp.where(lane == 1, sums[1], 0.0)) / safe
-        value = jnp.where(lane == 2, ext[...], value)
+        value = jnp.where(lane == 2, gain_sums[1], value)
         put_mat(0, layer + 1, value.astype(bf16), slice(3 * quad, 3 * quad + lanes))
 
     def backward_ffn(layer):
@@ -1026,7 +1040,6 @@
             h = hbuf[at, :].astype(f32)
             doa[0, at, :] = (h * lax.rsqrt(jnp.mean(h * h, axis=1, keepdims=True) + norm_eps) * gains[layer, 1]).astype(bf16)
 
-        dn[...] = jnp.zeros_like(dn)
         gain_sums[...] = jnp.zeros_like(gain_sums)
         dbias[...] = jnp.zeros_like(dbias)
         turned_cols = slice(0, segs * rows)
@@ -1036,32 +1049,41 @@
         def _(c):
             cols = pl.ds(pl.multiple_of(c * chunk, chunk), chunk)
             planes = pl.ds(c, 1)
-            d_pre = (nt(dy[...], mat(3, layer, planes=planes)) * slope[:, cols].astype(f32)).astype(bf16)
+            d_pre = nt(dy[...], mat(3, layer, planes=planes)).astype(bf16) * slope[:, cols]
+            slope[:, cols] = d_pre
             put_mat(3, slot, tn(active[:, cols], dy[...]).astype(bf16), planes=planes)
             d_up = mm(mat(0, slot, turned_cols), d_pre)
             add_gain(1, d_up, mat(2, layer, cols))
             put_mat(2, slot, d_up.astype(bf16), cols)
-            dn[...] += nt(d_pre, mat(2, layer, cols))
             for k in range(ff // chunk):
                 back_point(layer, "ffn" + str(k), c, k)
 
     def backward_middle(layer, s):
         at = seg_rows(s)
-        dh = norm_back(hbuf[at, :].astype(f32), gains[layer, 1], dn[at, :])
+        dh = norm_back(hbuf[at, :].astype(f32), gains[layer, 1], nt(slope[at, :], mat(2, layer)))
+        v = ub[at, :].astype(f32)
+        hbuf[at, :] = (v * lax.rsqrt(jnp.mean(v * v, axis=1, keepdims=True) + norm_eps) * gains[layer, 0]).astype(bf16)
         dh = dh + dy[at, :].astype(f32)
         dn[at, :] = dh
         dz = dh.astype(bf16)
         dy[at, :] = dz
         do = nt(dz, mat(1, layer)) * ilbuf[at, :].astype(f32)
         prod = do.astype(bf16).astype(f32) * obuf[at, :].astype(f32)
-        for p in range(pairs):
-            cols = slice(p * lanes, (p + 1) * lanes)
-            for side in range(2):
-                own, marks = lane_marks(head_size, side)
-                delta = -jnp.sum(prod[:, cols] * own, axis=1, keepdims=True)
-                hi = delta.astype(bf16).astype(f32)
-                fill = hi * marks[0] + (delta - hi) * marks[1]
-                doa[side, at, cols] = (do[:, cols] * (1.0 - marks[0] - marks[1]) + fill).astype(bf16)
+        lane = lax.broadcasted_iota(jnp.int32, (1, quad), 1) % head_size
+        side = lax.broadcasted_iota(jnp.int32, (1, quad), 1) // head_size % 2
+        hi_at, lo_at = (lane == 0).astype(f32), (lane == 1).astype(f32)
+        free = 1.0 - hi_at - lo_at
+        head_of = lax.broadcasted_iota(jnp.int32, (quad, quad), 0) // head_size
+        gets = lax.broadcasted_iota(jnp.int32, (quad, quad), 1) // head_size
+        swap_sum = jnp.where(head_of == gets + 1 - 2 * (gets % 2), -1.0, 0.0).astype(bf16)
+        for q in range(quads):
+            cols = slice(q * quad, (q + 1) * quad)
+            upper = prod[:, cols].astype(bf16)
+            delta = mm(upper, swap_sum) + mm((prod[:, cols] - upper.astype(f32)).astype(bf16), swap_sum)
+            hi = delta.astype(bf16).astype(f32)
+            filled = do[:, cols] * free + hi * hi_at + (delta - hi) * lo_at
+            for k in range(2):
+                doa[k, at, cols] = jnp.where(side == k, do[:, cols], filled).astype(bf16)
 
     def backward_attention(layer, q, s):
         at = seg_rows(s)
@@ -1080,9 +1102,8 @@
                 do_h = doa[side, at, cols]
                 va = vp * own.astype(bf16) + (marks[0] + marks[1]).astype(bf16)
                 weights = ebuf[s, h]
-                d_scores = weights.astype(f32) * nt(do_h, va)
-                dbias[pl.ds(h, 1), :] += jnp.sum(d_scores[:, :lanes], axis=0, keepdims=True)
-                d_scores = d_scores.astype(bf16)
+                d_scores = weights * nt(do_h, va).astype(bf16)
+                dbias[pl.ds(h, 1), :] += jnp.sum(d_scores[:, :lanes].astype(f32), axis=0, keepdims=True)
                 half = slice(side * head_size, (side + 1) * head_size)
                 dq.append(mm(d_scores, kp))
                 dk.append(mm(q_turned[half, :], d_scores))
@@ -1124,6 +1145,11 @@
         def _():
             wait_rows(doa.at[1], 3)
 
+        @pl.when(layer == 0)
+        def _():
+            for s in range(segs):
+                spill_copies(s, True, (7,))[0].wait()
+
         @pl.loop(0, segs)
         def _(s):
             backward_middle(layer, s)
@@ -1135,19 +1161,8 @@
         @pl.when(layer == 1)
         def _():
             for s in range(segs):
-                for copy in spill_copies(s, True, (2, 3, 4, 5, 6)):
+                for copy in spill_copies(s, True, (2, 3, 4, 5)):
                     copy.start()
-
-        @pl.loop(0, segs)
-        def _(s):
-            at = seg_rows(s)
-
-            @pl.when(layer == 0)
-            def _():
-                spill_copies(s, True, (7,))[0].wait()
-
-            v = ub[at, :].astype(f32)
-            dy[at, :] = (v * lax.rsqrt(jnp.mean(v * v, axis=1, keepdims=True) + norm_eps) * gains[layer, 0]).astype(bf16)
 
         @pl.loop(0, quads)
         def _(q):
@@ -1160,18 +1175,20 @@
 
                 backward_attention(layer, q, s)
 
-                @pl.when((layer == 1) & (q == quads - 1))
-                def _():
-                    spill_copies(s, True, (1,))[0].start()
-
                 for i in range(quads):
                     for k in range(segs):
                         back_point(layer, "att" + str(i) + str(k), q * segs + s, i * segs + k)
 
             for k in range(3):
-                d_weight = tn(dy[...], qkv[:, pl.ds(pl.multiple_of(k * width + q * quad, quad), quad)])
+                d_weight = tn(hbuf[...], qkv[:, pl.ds(pl.multiple_of(k * width + q * quad, quad), quad)])
                 add_gain(0, d_weight, mat(0, layer, pl.ds(pl.multiple_of(lanes + k * width + q * quad, lanes), quad)))
                 put_mat(0, slot, d_weight.astype(bf16), pl.ds(pl.multiple_of(grad_col(q, k), lanes), quad))
+
+            @pl.when((layer == 1) & (q == quads - 1))
+            def _():
+                for k in (6, 1):
+                    for s in range(segs):
+                        spill_copies(s, True, (k,))[0].start()
 
             @pl.when(q == quads - 1)
             def _():
@@ -1186,10 +1203,11 @@
             for k in range(segs):
                 back_point(layer, "in" + str(k), s, k)
 
+
         @pl.when(layer == 1)
         def _():
             for s in range(segs):
-                for copy in spill_copies(s, True, (0, 7)):
+                for copy in spill_copies(s, True, (7, 0)):
                     copy.start()
 
         if not routed:
@@ -1262,12 +1280,9 @@
         pltpu.VMEM((2, *wide), bf16),
         pltpu.VMEM(wide, f32),
         pltpu.VMEM((2, 2, 1, width), f32),
-        pltpu.VMEM((heads, slots, lanes), f32),
-        pltpu.VMEM((width, lanes), f32),
         pltpu.VMEM((2, width, lanes), f32),
         pltpu.VMEM((heads, lanes), f32),
         pltpu.VMEM((2, 8, lanes), f32),
-        dma((segs, 8)),
         dma((segs, 8)),
         dma((8,)),
         dma((9,)),
@@ -1290,6 +1305,7 @@
         scratch += [
             pltpu.VMEM((4, 2, 8, lanes), f32),
             pltpu.VMEM((7, 2, 8, lanes), f32),
+            pltpu.VMEM((2, width // 32, lanes), bf16),
             dma((5, 5)),
             dma((5, 8)),
             pltpu.SemaphoreType.REGULAR((5, 4)),
@@ -1299,7 +1315,7 @@
     return pl.pallas_call(
         partial(fused_layers, dims, routed),
         out_shape=out_shape,
-        in_specs=[smem] + [hbm] * (len(row_args) + len(weights)),
+        in_specs=[smem] + [hbm] * (len(row_args) + 4) + [vmem] * (len(weights) - 4),
         out_specs=[hbm] * row_outs + [vmem] + [hbm] * (len(out_shape) - row_outs - 1),
         scratch_shapes=scratch,
         compiler_params=pltpu.CompilerParams(**params),
@@ -1375,12 +1391,9 @@
     heads = forget_bias.shape[1] * lax.axis_size("dp") // slots
     per_doc = micro // lengths.shape[0]
     dims = (segs, rows, width, ff, slots, heads, per_doc)
-    small = jnp.stack([gain_attn, gain_ffn, forget_bias], axis=2)
-    small = jnp.pad(small, ((0, 0), (0, 0), (0, lanes - 3)))
-
     if lax.axis_size("dp") == 16 and w_qkv.shape[1] == 32:
-        pieces = (w_qkv, w_out, w_up, w_down, small)
-        weights = [piece.reshape(2, -1, piece.shape[2]) for piece in pieces]
+        weights = [piece.reshape(2, -1, piece.shape[2]) for piece in (w_qkv, w_out, w_up, w_down)]
+        weights += [gain_attn, gain_ffn, forget_bias]
         row_args = (tokens, memory, grad_tokens, grad_memory)
         *outs, small_grads, stats = run_layers(dims, True, lengths, row_args, weights)
         outs = settle(outs, small_grads, stats)
@@ -1388,6 +1401,8 @@
         return (*outs[:4], *mats, *outs[8:])
 
     own_len = lax.dynamic_slice_in_dim(lengths, section * segs // per_doc, segs // per_doc, 0)
+    small = jnp.stack([gain_attn, gain_ffn, forget_bias], axis=2)
+    small = jnp.pad(small, ((0, 0), (0, 0), (0, lanes - 3)))
     pieces = (jnp.concatenate([small, w_qkv], axis=2), w_out, w_up, w_down)
 
     def unpack(grads):
@@ -1429,8 +1444,8 @@
         return lax.psum_scatter(chip, "dp", scatter_dimension=1, tiled=True).astype(f32)
 
     shares = unpack([scatter(grad) for grad in grads])
-    totals = lax.psum(stats[:, :4, 0], ("section", "dp"))
-    rms = jnp.sqrt(totals[:, :3] / (totals[0, 3] * width))
+    totals = lax.psum(stats[:, :4], ("section", "dp"))
+    rms = jnp.sqrt(jnp.sum(totals[:, :3], axis=2) / (totals[0, 3, 0] * width))
     result = jnp.stack([y.reshape(segs, rows, width), du.reshape(segs, rows, width)])
 
     def half_of(which):

time: 180 us -> 175 us (0.972)
  Pallas kernels: 178 us -> 174 us
    pallas_call x1, Pallas kernels: 174 us -> 170 us  [run_layers(): pl.pallas_call(partial(fused_layers, dims, routed), out_shape=out_shape,...]
where the time goes in v6:
time: 175 us
  Pallas kernels  174 us (99%)
    pallas_call x1, Pallas kernels, run_layers(): pl.pallas_call(partial(fused_layers, dims, routed), out_shape=out_shape,...  170 us
    pallas_call x1, Pallas kernels, settle(): pl.pallas_call(settle_kernel, out_shape=[shape(part.shape, part.dtype) fo...  4.31 us

profile of v6, /device:TPU:0, one launch (start us, length us, event | category | flops | bytes accessed | tf_op | source)
XLA Modules:
  0.0 174.8 jit_solution(960286704065219302)
XLA Ops:
  0.6 169.6 %shard_map.211 = (bf16[4,256,512]{2,1,0:T(8,128)(2,1)}, bf16[4,32,512]{2,1,0:T(8,128)(2,1)}, bf16[4,256,512]{2,1,0:T(8,128)(2,1)}, bf16[4,32,512]{2,1,0:T(8,128)...) custom-call(s32[2]{0:T(128)} %refs_0_.1, ...), custom_call_target="tpu_custom_call" | custom-call | tf_op jit(solution)/shard_map/pallas_call | solution.py:1315
  170.3 4.3 %shard_map.212 = (bf16[4,256,512]{2,1,0:T(8,128)(2,1)}, bf16[4,32,512]{2,1,0:T(8,128)(2,1)}, bf16[4,256,512]{2,1,0:T(8,128)(2,1)}, bf16[4,32,512]{2,1,0:T(8,128)...) custom-call(bf16[4,256,512]{2,1,0:T(8,128)(2,1)} %get-tuple-element., ...), custom_call_target="tpu_custom_call" | custom-call | tf_op jit(solution)/shard_map/pallas_call | solution.py:1354

commit v7 on v6

--- a/solution.py
+++ b/solution.py
@@ -244,24 +244,24 @@
                 wait_bytes(view(n, slice(0, 3), y, x, every), sem_send.at[n, few])
 
         def hops(text):
-            kinds = dict(z=start_z, f=first_hop, s=second_hop, l=last_share)
+            kinds = dict(z=start_z, f=first_hop, s=second_hop, l=last_share, u=take_small)
             for word in text:
                 kinds[word[0]](int(word[1:]))
 
-        opening = ("z0", "z1", "z2", "z3", "z4", "z5", "f0", "f1", "s0", "z6", "f2", "s1", "z7", "f3", "s2", "l0", "f4", "s3", "l1", "f5", "s4", "f6", "l2", "z8", "z9", "z11")
+        opening = ("z0", "z1", "z2", "z3", "z4", "z5", "f0", "f1", "s0", "z6", "f2", "s1", "z7", "f3", "s2", "l0", "f4", "s3", "l1", "f5", "u0", "l2", "s4", "f6", "z8", "z9", "z11")
         hops_at = {
             (0, 0, "qkv"): ("s5", "f7", "z10", "z15"),
             (0, 0, "quad0"): ("s6", "z12", "l3"),
             (0, 0, "quad1"): ("f8", "f11", "z13"),
             (0, 1, "qkv"): ("s7", "f9", "l4"),
             (0, 1, "quad0"): ("f10", "s8", "z14", "f15", "l5"),
-            (0, 1, "quad1"): ("l6", "s9", "s11"),
+            (0, 1, "quad1"): ("l6", "s11"),
             (0, 0, "gate"): ("f12",),
-            (0, 0, "ffna"): ("l7", "s10", "f13"),
+            (0, 0, "ffna"): ("l7", "s9", "s10", "f13"),
             (0, 1, "ffna"): ("s15",),
             (0, 0, "ffnb"): ("s12", "l8", "f14"),
             (0, 1, "ffnb"): ("s13", "l9", "l10"),
-            (1, 0, "quad0"): ("s14",),
+            (1, 0, "qkv"): ("s14",),
             (1, 1, "qkv"): ("l12", "l13"),
             (1, 1, "quad0"): ("l11", "l14"),
             (1, 1, "quad1"): ("l15",),
@@ -417,16 +417,11 @@
             copy.start()
         for n in range(8, len(units)):
             share_own(n)
-        hops(opening)
     else:
         for n in range(len(units)):
             weight_copy(n).start()
     stat_ref[...] = jnp.zeros_like(stat_ref)
 
-    wait_bytes(ub, sem_io.at[0])
-    wait_bytes(dy, sem_io.at[1])
-    if routed:
-        wait_bytes(ub, sem_io.at[2])
 
     def wait_rows(buf, first):
         if routed:
@@ -445,32 +440,41 @@
     def forward_attention(layer, s):
         at = seg_rows(s)
         mask = mask_col(s)
-        for p in range(pairs):
-            cols = slice(p * lanes, (p + 1) * lanes)
-            qp = qkv[at, cols]
-            kp = qkv[at, slice(width + p * lanes, width + (p + 1) * lanes)]
-            vp = qkv[at, slice(2 * width + p * lanes, 2 * width + (p + 1) * lanes)]
-            outs = []
-            for side in range(2):
-                h = 2 * p + side
-                own, marks = lane_marks(head_size, side)
-                bias = gain_sums[0, h * slots : (h + 1) * slots]
-                hi = bias.astype(bf16).astype(f32)
-                aux = jnp.concatenate([hi * marks[1] + (bias - hi) * marks[2], jnp.zeros((tok_rows, lanes), f32)], axis=0)
-                aux = aux + mask * marks[0]
-                extra = marks[0] + marks[1] + marks[2]
-                ka = kp * own.astype(bf16) + aux.astype(bf16)
-                qa = qp * (1.0 - extra).astype(bf16) + extra.astype(bf16)
-                scores = nt(qa, ka)
-                top = jnp.max(scores, axis=1, keepdims=True)
-                weights = jnp.exp2(scores - top).astype(bf16)
-                ebuf[s, h] = weights
-                va = vp * own.astype(bf16) + (1.0 - own).astype(bf16)
-                outs.append(mm(weights, va))
+
+        def pair_cols(k, p):
+            return slice(k * width + p * lanes, k * width + (p + 1) * lanes)
+
+        def scores_of(h):
+            p, side = h // 2, h % 2
+            qp, kp = qkv[at, pair_cols(0, p)], qkv[at, pair_cols(1, p)]
+            own, marks = lane_marks(head_size, side)
+            bias = gain_sums[0, h * slots : (h + 1) * slots]
+            hi = bias.astype(bf16).astype(f32)
+            aux = jnp.concatenate([hi * marks[1] + (bias - hi) * marks[2], jnp.zeros((tok_rows, lanes), f32)], axis=0)
+            aux = aux + mask * marks[0]
+            extra = marks[0] + marks[1] + marks[2]
+            ka = kp * own.astype(bf16) + aux.astype(bf16)
+            qa = qp * (1.0 - extra).astype(bf16) + extra.astype(bf16)
+            return nt(qa, ka)
+
+        scores, outs = scores_of(0), []
+        for h in range(heads):
+            p, side = h // 2, h % 2
+            following = scores_of(h + 1) if h + 1 < heads else None
+            top = jnp.max(scores, axis=1, keepdims=True)
+            weights = jnp.exp2(scores - top).astype(bf16)
+            ebuf[s, h] = weights
+            own, _ = lane_marks(head_size, side)
+            va = qkv[at, pair_cols(2, p)] * own.astype(bf16) + (1.0 - own).astype(bf16)
+            outs.append(mm(weights, va))
+            scores = following
+            if side == 0:
+                continue
             own, _ = lane_marks(head_size, 0)
-            raw = jnp.where(own > 0, outs[0], outs[1])
-            sums = pltpu.roll(jnp.where(own > 0, outs[1], outs[0]), head_size, 1)
+            raw = jnp.where(own > 0, outs[-2], outs[-1])
+            sums = pltpu.roll(jnp.where(own > 0, outs[-1], outs[-2]), head_size, 1)
             inv = 1.0 / sums
+            cols = pair_cols(0, p)
             ilbuf[at, cols] = inv.astype(ilbuf.dtype)
             obuf[at, cols] = (raw * inv).astype(bf16)
             if p % 2 == 1:
@@ -485,6 +489,10 @@
         for h in range(heads):
             column = gain_sums[1, pl.ds(h, slots, stride=heads)][:, 2:3]
             gain_sums[0, h * slots : (h + 1) * slots] = jnp.broadcast_to(column * log2_e, (slots, lanes))
+
+    def take_small(layer):
+        complete(8 * layer)
+        unpack_small(layer)
 
     def forward_attn(layer, s):
         at = seg_rows(s)
@@ -540,7 +548,7 @@
                 dn[at, :] += part
             before = following
 
-    def forward_ffn_a(layer, s):
+    def forward_mid(layer, s):
         at = seg_rows(s)
         valid = valid_rows(s)
         z = mm(obuf[at, :], mat(1, layer))
@@ -548,6 +556,8 @@
         h = ub[at, :].astype(f32) + z
         hbuf[at, :] = h.astype(bf16)
         doa[0, at, :] = (h * lax.rsqrt(jnp.mean(h * h, axis=1, keepdims=True) + norm_eps) * gains[layer, 1]).astype(bf16)
+
+    def forward_ffn_a(layer, s):
         ffn_part(s, layer, range(ff // chunk // 2))
         after(layer, s, "ffna")
 
@@ -575,11 +585,22 @@
 
         after(layer, s, "ffnb")
 
+    if routed:
+        hops(opening)
+        wait_bytes(ub, sem_io.at[2])
+    wait_bytes(ub, sem_io.at[0])
+    wait_bytes(dy, sem_io.at[1])
+
     @pl.loop(0, 2)
     def _(layer):
         after(layer, 0, "open")
-        need(layer, first_units)
-        unpack_small(layer)
+        for at_layer in range(2):
+            if at_layer == 1 or not routed:
+                @pl.when(layer == at_layer)
+                def _(at_layer=at_layer):
+                    take_small(at_layer)
+
+        need(layer, [n for n in first_units if n % 8 > 0])
 
         @pl.loop(0, segs)
         def _(s):
@@ -587,6 +608,8 @@
 
         after(layer, 0, "gate")
         need(layer, later_units)
+        for s in range(segs):
+            forward_mid(layer, s)
 
         @pl.loop(0, segs)
         def _(s):
@@ -1049,9 +1072,10 @@
         def _(c):
             cols = pl.ds(pl.multiple_of(c * chunk, chunk), chunk)
             planes = pl.ds(c, 1)
-            d_pre = nt(dy[...], mat(3, layer, planes=planes)).astype(bf16) * slope[:, cols]
+            d_act = nt(dy[...], mat(3, layer, planes=planes)).astype(bf16)
+            put_mat(3, slot, tn(active[:, cols], dy[...]).astype(bf16), planes=planes)
+            d_pre = d_act * slope[:, cols]
             slope[:, cols] = d_pre
-            put_mat(3, slot, tn(active[:, cols], dy[...]).astype(bf16), planes=planes)
             d_up = mm(mat(0, slot, turned_cols), d_pre)
             add_gain(1, d_up, mat(2, layer, cols))
             put_mat(2, slot, d_up.astype(bf16), cols)
@@ -1087,31 +1111,38 @@
 
     def backward_attention(layer, q, s):
         at = seg_rows(s)
-        for p in range(2):
-            cols, kcols, vcols = (
-                pl.ds(pl.multiple_of(k * width + q * quad + p * lanes, lanes), lanes) for k in range(3)
-            )
-            qp = qkv[at, cols]
-            kp = qkv[at, kcols]
-            vp = qkv[at, vcols]
-            q_turned = qp.T
-            dq, dk, dv = [], [], []
-            for side in range(2):
-                h = 4 * q + 2 * p + side
-                own, marks = lane_marks(head_size, side)
-                do_h = doa[side, at, cols]
-                va = vp * own.astype(bf16) + (marks[0] + marks[1]).astype(bf16)
-                weights = ebuf[s, h]
-                d_scores = weights * nt(do_h, va).astype(bf16)
-                dbias[pl.ds(h, 1), :] += jnp.sum(d_scores[:, :lanes].astype(f32), axis=0, keepdims=True)
-                half = slice(side * head_size, (side + 1) * head_size)
-                dq.append(mm(d_scores, kp))
-                dk.append(mm(q_turned[half, :], d_scores))
-                dv.append(mm(do_h.T[half, :], weights))
+
+        def pair_cols(k, p):
+            return pl.ds(pl.multiple_of(k * width + q * quad + p * lanes, lanes), lanes)
+
+        def d_probs_of(h):
+            p, side = h // 2, h % 2
+            own, marks = lane_marks(head_size, side)
+            do_h = doa[side, at, pair_cols(0, p)]
+            va = qkv[at, pair_cols(2, p)] * own.astype(bf16) + (marks[0] + marks[1]).astype(bf16)
+            return do_h, nt(do_h, va)
+
+        do_h, d_probs = d_probs_of(0)
+        dq, dk, dv = [], [], []
+        for h in range(4):
+            p, side = h // 2, h % 2
+            head = 4 * q + h
+            following = d_probs_of(h + 1) if h < 3 else (None, None)
+            qp, kp = qkv[at, pair_cols(0, p)], qkv[at, pair_cols(1, p)]
+            half = slice(side * head_size, (side + 1) * head_size)
+            weights = ebuf[s, head]
+            dv.append(mm(do_h.T[half, :], weights))
+            d_scores = weights * d_probs.astype(bf16)
+            dbias[pl.ds(head, 1), :] += jnp.sum(d_scores[:, :lanes].astype(f32), axis=0, keepdims=True)
+            dq.append(mm(d_scores, kp))
+            dk.append(mm(qp.T[half, :], d_scores))
+            do_h, d_probs = following
+            if side == 0:
+                continue
             own, _ = lane_marks(head_size, 0)
-            qkv[at, cols] = (jnp.where(own > 0, dq[0], dq[1]) * score_scale).astype(bf16)
-            qkv[at, kcols] = (jnp.concatenate(dk, axis=0).T * (1.0 / log2_e)).astype(bf16)
-            qkv[at, vcols] = jnp.concatenate(dv, axis=0).T.astype(bf16)
+            qkv[at, pair_cols(0, p)] = (jnp.where(own > 0, dq[-2], dq[-1]) * score_scale).astype(bf16)
+            qkv[at, pair_cols(1, p)] = (jnp.concatenate(dk[-2:], axis=0).T * (1.0 / log2_e)).astype(bf16)
+            qkv[at, pair_cols(2, p)] = jnp.concatenate(dv[-2:], axis=0).T.astype(bf16)
 
     def backward_input(layer, s):
         at = seg_rows(s)

time: 175 us -> 172 us (0.983)
  Pallas kernels: 174 us -> 171 us
    pallas_call x1, Pallas kernels: 170 us -> 167 us  [run_layers(): pl.pallas_call(partial(fused_layers, dims, routed), out_shape=out_shape,...]
where the time goes in v7:
time: 172 us
  Pallas kernels  171 us (99%)
    pallas_call x1, Pallas kernels, run_layers(): pl.pallas_call(partial(fused_layers, dims, routed), out_shape=out_shape,...  167 us
    pallas_call x1, Pallas kernels, settle(): pl.pallas_call(settle_kernel, out_shape=[shape(part.shape, part.dtype) fo...  4.31 us

profile of v7, /device:TPU:0, one launch (start us, length us, event | category | flops | bytes accessed | tf_op | source)
XLA Modules:
  0.0 171.9 jit_solution(5197655489327100862)
XLA Ops:
  0.6 166.8 %shard_map.211 = (bf16[4,256,512]{2,1,0:T(8,128)(2,1)}, bf16[4,32,512]{2,1,0:T(8,128)(2,1)}, bf16[4,256,512]{2,1,0:T(8,128)(2,1)}, bf16[4,32,512]{2,1,0:T(8,128)...) custom-call(s32[2]{0:T(128)} %refs_0_.1, ...), custom_call_target="tpu_custom_call" | custom-call | tf_op jit(solution)/shard_map/pallas_call | solution.py:1346
  167.4 4.3 %shard_map.212 = (bf16[4,256,512]{2,1,0:T(8,128)(2,1)}, bf16[4,32,512]{2,1,0:T(8,128)(2,1)}, bf16[4,256,512]{2,1,0:T(8,128)(2,1)}, bf16[4,32,512]{2,1,0:T(8,128)...) custom-call(bf16[4,256,512]{2,1,0:T(8,128)(2,1)} %get-tuple-element., ...), custom_call_target="tpu_custom_call" | custom-call | tf_op jit(solution)/shard_map/pallas_call | solution.py:1385

commit v8 on v7

--- a/solution.py
+++ b/solution.py
@@ -65,7 +65,7 @@
         fin = take(5)
         stat_sum, stat_land, small_buf = take(3)
         weight_in = [*weight_in, small_buf]
-        rs_send, rs_recv, rs_free, stat_send, stat_recv = take(5)
+        rs_recv, rs_free, stat_recv = take(3)
     head_size = width // heads
     pairs = width // lanes
     tok_rows = rows - slots
@@ -73,6 +73,9 @@
     quad = 2 * lanes
     first_doc = lax.axis_index("section") * segs // per_doc if routed else 0
     every = slice(None)
+
+    def sent_sem(k):
+        return sem_send.at[k // 2, k % 2]
 
     def wait_bytes(ref, sem):
         pltpu.make_async_copy(ref, ref, sem).wait()
@@ -644,7 +647,7 @@
             return pltpu.make_async_remote_copy(
                 src_ref=src,
                 dst_ref=dst,
-                send_sem=rs_send.at[u, step],
+                send_sem=sent_sem(5 * u + step),
                 recv_sem=rs_recv.at[u, k],
                 device_id=target,
                 device_id_type=pl.DeviceIdType.MESH,
@@ -711,7 +714,7 @@
             return pltpu.make_async_remote_copy(
                 src_ref=spot(layer, u, away, y, x, core),
                 dst_ref=lands[u][3].at[half, k],
-                send_sem=rs_send.at[u, 3],
+                send_sem=sent_sem(5 * u + 3),
                 recv_sem=rs_recv.at[u, 6 + half],
                 device_id=(layer, place(away, y, x)),
                 device_id_type=pl.DeviceIdType.MESH,
@@ -911,23 +914,23 @@
         def rs_sent(layer, u, step):
             three = slice(0, 3)
             if step == 0:
-                wait_bytes(spot(layer, u, every, every, every, other), rs_send.at[u, 0])
+                wait_bytes(spot(layer, u, every, every, every, other), sent_sem(5 * u + 0))
             elif step == 1 and u in fast:
-                wait_bytes(spot(layer, u, three, every, every, core), rs_send.at[u, 1])
+                wait_bytes(spot(layer, u, three, every, every, core), sent_sem(5 * u + 1))
             elif step == 1:
-                wait_bytes(spot(layer, u, every, y, every, core), rs_send.at[u, 1])
+                wait_bytes(spot(layer, u, every, y, every, core), sent_sem(5 * u + 1))
             elif step == 2:
-                wait_bytes(spot(layer, u, every, y, x, core), rs_send.at[u, 2])
+                wait_bytes(spot(layer, u, every, y, x, core), sent_sem(5 * u + 2))
             elif u not in fast:
-                wait_bytes(spot(layer, u, three, y, x, core), rs_send.at[u, 3])
+                wait_bytes(spot(layer, u, three, y, x, core), sent_sem(5 * u + 3))
             else:
                 @pl.when(core == layer)
                 def _():
-                    wait_bytes(spot(layer, u, three, y, x, core), rs_send.at[u, 3])
+                    wait_bytes(spot(layer, u, three, y, x, core), sent_sem(5 * u + 3))
 
                 @pl.when(core != layer)
                 def _():
-                    wait_bytes(spot(layer, u, every, y, x, core), rs_send.at[u, 3])
+                    wait_bytes(spot(layer, u, every, y, x, core), sent_sem(5 * u + 3))
 
         def rs_finish(layer, u):
             for step in (0, 1, 3) if u in fast else range(4):
@@ -939,7 +942,7 @@
             return pltpu.make_async_remote_copy(
                 src_ref=stat_sum.at[step],
                 dst_ref=stat_land.at[place_at],
-                send_sem=stat_send.at[step],
+                send_sem=sent_sem(25 + step),
                 recv_sem=stat_recv.at[step],
                 device_id=target,
                 device_id_type=pl.DeviceIdType.MESH,
@@ -959,7 +962,7 @@
                     stat_copy(3, k).start()
             else:
                 wait_bytes(stat_land.at[pl.ds(3, 3)], stat_recv.at[3])
-                wait_bytes(stat_land.at[pl.ds(3, 3)], stat_send.at[3])
+                wait_bytes(stat_land.at[pl.ds(3, 3)], sent_sem(25 + 3))
                 total = stat_land[3] + stat_land[4] + stat_land[5] + stat_land[6]
                 stat_ref[...] = total
                 stat_done()
@@ -1092,7 +1095,7 @@
         dz = dh.astype(bf16)
         dy[at, :] = dz
         do = nt(dz, mat(1, layer)) * ilbuf[at, :].astype(f32)
-        prod = do.astype(bf16).astype(f32) * obuf[at, :].astype(f32)
+        prod = do.astype(bf16) * obuf[at, :]
         lane = lax.broadcasted_iota(jnp.int32, (1, quad), 1) % head_size
         side = lax.broadcasted_iota(jnp.int32, (1, quad), 1) // head_size % 2
         hi_at, lo_at = (lane == 0).astype(f32), (lane == 1).astype(f32)
@@ -1102,8 +1105,7 @@
         swap_sum = jnp.where(head_of == gets + 1 - 2 * (gets % 2), -1.0, 0.0).astype(bf16)
         for q in range(quads):
             cols = slice(q * quad, (q + 1) * quad)
-            upper = prod[:, cols].astype(bf16)
-            delta = mm(upper, swap_sum) + mm((prod[:, cols] - upper.astype(f32)).astype(bf16), swap_sum)
+            delta = mm(prod[:, cols], swap_sum)
             hi = delta.astype(bf16).astype(f32)
             filled = do[:, cols] * free + hi * hi_at + (delta - hi) * lo_at
             for k in range(2):
@@ -1337,10 +1339,8 @@
             pltpu.VMEM((4, 2, 8, lanes), f32),
             pltpu.VMEM((7, 2, 8, lanes), f32),
             pltpu.VMEM((2, width // 32, lanes), bf16),
-            dma((5, 5)),
             dma((5, 8)),
             pltpu.SemaphoreType.REGULAR((5, 4)),
-            dma((4,)),
             dma((4,)),
         ]
     return pl.pallas_call(

time: 172 us -> 171 us (level)
  no operation moved by 1% of the time
where the time goes in v8:
time: 171 us
  Pallas kernels  170 us (99%)
    pallas_call x1, Pallas kernels, run_layers(): pl.pallas_call(partial(fused_layers, dims, routed), out_shape=out_shape,...  166 us
    pallas_call x1, Pallas kernels, settle(): pl.pallas_call(settle_kernel, out_shape=[shape(part.shape, part.dtype) fo...  4.31 us

profile of v8, /device:TPU:0, one launch (start us, length us, event | category | flops | bytes accessed | tf_op | source)
XLA Modules:
  0.0 170.7 jit_solution(1838040384897244586)
XLA Ops:
  0.6 165.6 %shard_map.211 = (bf16[4,256,512]{2,1,0:T(8,128)(2,1)}, bf16[4,32,512]{2,1,0:T(8,128)(2,1)}, bf16[4,256,512]{2,1,0:T(8,128)(2,1)}, bf16[4,32,512]{2,1,0:T(8,128)...) custom-call(s32[2]{0:T(128)} %refs_0_.1, ...), custom_call_target="tpu_custom_call" | custom-call | tf_op jit(solution)/shard_map/pallas_call | solution.py:1346
  166.3 4.3 %shard_map.212 = (bf16[4,256,512]{2,1,0:T(8,128)(2,1)}, bf16[4,32,512]{2,1,0:T(8,128)(2,1)}, bf16[4,256,512]{2,1,0:T(8,128)(2,1)}, bf16[4,32,512]{2,1,0:T(8,128)...) custom-call(bf16[4,256,512]{2,1,0:T(8,128)(2,1)} %get-tuple-element., ...), custom_call_target="tpu_custom_call" | custom-call | tf_op jit(solution)/shard_map/pallas_call | solution.py:1385
